TPU v7x, 32 devices: a whole 2x2x4 slice. The times are simulated.
32 devices in a mesh: section: 2 (over core), seq: 4 (over y, x), dp: 4 (over z).
Axes of the slice: x: 2, y: 2, z: 4, core: 2. Of those that a mesh axis runs over, the one named last changes fastest.
Arguments:
- tokens: bfloat16 [8, 1024, 1024], P('dp', 'seq'), may hold values from -6 to 6
- out_grad: bfloat16 [8, 1024, 1024], P('dp', 'seq'), may hold values from -6 to 6
- lengths: int32 [8, 4], P('dp'), may hold values from 0 to 1024, as said below
- ln1_gain: bfloat16 [2, 1024], P('section', 'seq'), may hold values from 0.5 to 1.5
- w_in: bfloat16 [2, 1024, 3072], P('section', 'seq'), may hold values from -0.1875 to 0.1875
- short_w: bfloat16 [2, 3, 3072], P('section', None, 'seq'), may hold values from -3 to 3
- filt_in: bfloat16 [2, 33, 64], P('section', None, 'seq'), may hold values from -1 to 1
- filt_shift: bfloat16 [2, 64], P('section', 'seq'), may hold values from -3.140625 to 3.140625
- sine_freq: bfloat16 [2, 64], P('section', 'seq'), may hold values from 2 to 30
- filt_out: bfloat16 [2, 64, 1024], P('section', 'seq'), may hold values from -0.0625 to 0.0625
- decay: bfloat16 [2, 1024], P('section', 'seq'), may hold values from 0.5 to 32
- filter_bias: bfloat16 [2, 1024], P('section', 'seq'), may hold values from -4 to 4
- w_out: bfloat16 [2, 1024, 1024], P('section', 'seq'), may hold values from -0.1875 to 0.1875
- ln2_gain: bfloat16 [2, 1024], P('section', 'seq'), may hold values from 0.5 to 1.5
- mlp_up: bfloat16 [2, 1024, 4096], P('section', 'seq'), may hold values from -0.1875 to 0.1875
- mlp_down: bfloat16 [2, 4096, 1024], P('section', 'seq'), may hold values from -0.09375 to 0.09375
Outputs:
- layer_outputs: bfloat16 [2, 8, 1024, 1024], P('section', 'dp', 'seq')
- input_grads: bfloat16 [2, 8, 1024, 1024], P('section', 'dp', 'seq')
- grad_ln1_gain: float32 [2, 1024], P('section', 'seq')
- grad_w_in: float32 [2, 1024, 3072], P('section', 'seq')
- grad_short_w: float32 [2, 3, 3072], P('section', None, 'seq')
- grad_filt_in: float32 [2, 33, 64], P('section', None, 'seq')
- grad_filt_shift: float32 [2, 64], P('section', 'seq')
- grad_sine_freq: float32 [2, 64], P('section', 'seq')
- grad_filt_out: float32 [2, 64, 1024], P('section', 'seq')
- grad_decay: float32 [2, 1024], P('section', 'seq')
- grad_filter_bias: float32 [2, 1024], P('section', 'seq')
- grad_w_out: float32 [2, 1024, 1024], P('section', 'seq')
- grad_ln2_gain: float32 [2, 1024], P('section', 'seq')
- grad_mlp_up: float32 [2, 1024, 4096], P('section', 'seq')
- grad_mlp_down: float32 [2, 4096, 1024], P('section', 'seq')
Inputs may be any that keep to these rules, and one draw needn't show every extreme that they name: `lengths`: row by row: an entry is the length in tokens of the document that starts at that block's first position, or 0 where no document starts; entry 0 is positive; a document of length n covers ceil(n / 256) blocks from its start and the next document starts in the block after them; the last one ends in the last block; among each replica's 2 rows, one holds a single document of 1024 tokens.
All inputs are finite; a program needn't handle non-finite values.
Results may differ from a plain program's by a relative error of at most 0.04.
Values may be sent and summed in bfloat16 or wider, within the bound.
A program may use at most 448 MiB of HBM per device.

v0:
```python
import math

import jax
import jax.numpy as jnp
from jax import lax
from jax.sharding import PartitionSpec as P

FREQS = 16


PRECISE = lax.Precision.HIGHEST
EPSILON = 1e-05


def shifted(block, axis, distance):
    devices = range(lax.axis_size(axis))
    route = [(i - distance, i) for i in devices if i - distance in devices]
    return lax.ppermute(block, axis, route)


def as_sent(array):
    return jax.tree.map(lambda a: a.astype(jnp.bfloat16) if a.dtype == jnp.float32 else a, array)


def matmul_high(left, right):
    return jnp.dot(left, right, preferred_element_type=jnp.float32, precision=PRECISE)


def matmul_low(left, right):
    return jnp.dot(left, right, preferred_element_type=jnp.float32)


def transpose_left(left, right):
    return lax.dot_general(
        left, right, (((0,), (0,)), ((), ())), preferred_element_type=jnp.float32
    )


def transpose_right(left, right):
    return lax.dot_general(
        left, right, (((1,), (1,)), ((), ())), preferred_element_type=jnp.float32
    )


def layer_norm(values, gains):
    row_mean = jnp.mean(values, axis=-1, keepdims=True)
    centered = values - row_mean
    variance = jnp.mean(centered * centered, axis=-1, keepdims=True)
    return centered * lax.rsqrt(variance + EPSILON) * gains


def gelu_tanh(values):
    return jax.nn.gelu(values, approximate=True)


def positions_embedding(slots, harmonic_count):
    steps_all = jnp.arange(slots, dtype=jnp.int32)
    scaled = steps_all.astype(jnp.float32) / slots
    harmonics = jnp.arange(1, harmonic_count + 1, dtype=jnp.int32)
    phase = (steps_all[:, None] * harmonics[None, :] % slots).astype(jnp.float32) * (
        2.0 * math.pi / slots
    )
    return jnp.concatenate([scaled[:, None], jnp.cos(phase), jnp.sin(phase)], axis=1)


def filter_taps(filt_in, filt_shift, sine_freq, filt_out, decay, embedding):
    slots = embedding.shape[0]
    hidden_sine = jnp.sin(sine_freq * (matmul_high(embedding, filt_in) + filt_shift))
    scaled = jnp.arange(slots, dtype=jnp.int32).astype(jnp.float32) / slots
    return matmul_high(hidden_sine, filt_out) * jnp.exp(-decay[None, :] * scaled[:, None])


def select_entry(table, position):
    return jnp.sum(jnp.where(jnp.arange(table.shape[0], dtype=jnp.int32) == position, table, 0))


def block_geometry(length_row, block_rows, seq_index):
    count = length_row.shape[0]
    index_all = jnp.arange(count, dtype=jnp.int32)
    regions = lax.cummax(jnp.where(length_row > 0, index_all, 0), axis=0)
    doc_length = jnp.sum(
        jnp.where(regions[:, None] == index_all[None, :], length_row[None, :], 0), axis=1
    )
    own_region = select_entry(regions, seq_index)
    offsets = (seq_index - own_region) * block_rows + jnp.arange(block_rows, dtype=jnp.int32)
    valid_rows = (offsets < select_entry(doc_length, seq_index)).astype(jnp.float32)
    carried_on = jnp.logical_and(
        seq_index > 0, select_entry(regions, seq_index - 1) == own_region
    ).astype(jnp.float32)
    return (regions, valid_rows, carried_on)


def short_mix(rim_values, proj_values, weight_values, carried_on):
    total_rows = proj_values.shape[0]
    extended = jnp.concatenate([rim_values * carried_on, proj_values], axis=0)
    return (
        weight_values[0] * extended[2:]
        + weight_values[1] * extended[1 : total_rows + 1]
        + weight_values[2] * extended[:total_rows]
    )


def dft_tables(block_rows):
    size = 2 * block_rows
    freq_index = jnp.arange(size, dtype=jnp.int32)
    sample = jnp.arange(block_rows, dtype=jnp.int32)
    phase = (freq_index[:, None] * sample[None, :] % size).astype(jnp.float32) * (
        2.0 * math.pi / size
    )
    parity = (1 - 2 * (freq_index % 2)).astype(jnp.float32)[:, None]
    return (jnp.cos(phase), -jnp.sin(phase), parity)


def transform(cosine, sine, blocks):
    real_part = jnp.einsum("fs,nsd->nfd", cosine, blocks, precision=PRECISE)
    imag_part = jnp.einsum("fs,nsd->nfd", sine, blocks, precision=PRECISE)
    return (real_part, imag_part)


def transform_back(cosine, sine, real_part, imag_part):
    return jnp.einsum("fs,nfd->nsd", cosine, real_part, precision=PRECISE) + jnp.einsum(
        "fs,nfd->nsd", sine, imag_part, precision=PRECISE
    )


def lag_mask(regions, lag, backward_sense):
    count = regions.shape[0]
    index_all = jnp.arange(count, dtype=jnp.int32)
    other = jnp.where(backward_sense, index_all + lag, index_all - lag)
    inside = jnp.logical_and(other >= 0, other < count)
    other_region = jnp.sum(
        jnp.where(other[:, None] == index_all[None, :], regions[None, :], 0), axis=1
    )
    return jnp.logical_and(inside, other_region == regions).astype(jnp.float32)[:, None, None]


def channel_convolve(spec_real, spec_imag, filt_real_cols, filt_imag_cols, regions):
    count = spec_real.shape[0]
    zeros = jnp.zeros_like(spec_real)
    padded_real = jnp.concatenate([zeros, spec_real], axis=0)
    padded_imag = jnp.concatenate([zeros, spec_imag], axis=0)

    def one_lag(lag, running):
        src_real = lax.dynamic_slice_in_dim(padded_real, count - lag, count, 0)
        src_imag = lax.dynamic_slice_in_dim(padded_imag, count - lag, count, 0)
        tap_real = lax.dynamic_slice_in_dim(filt_real_cols, lag, 1, 0)
        tap_imag = lax.dynamic_slice_in_dim(filt_imag_cols, lag, 1, 0)
        weight = lag_mask(regions, lag, False)
        return (
            running[0] + weight * (tap_real * src_real - tap_imag * src_imag),
            running[1] + weight * (tap_real * src_imag + tap_imag * src_real),
        )

    return lax.fori_loop(0, count, one_lag, (zeros, zeros))


def channel_correlate(
    own_real, own_imag, grad_real, grad_imag, filt_real_cols, filt_imag_cols, regions
):
    count = grad_real.shape[0]
    zeros = jnp.zeros_like(grad_real)
    padded_real = jnp.concatenate([grad_real, zeros], axis=0)
    padded_imag = jnp.concatenate([grad_imag, zeros], axis=0)

    def one_lag(lag, running):
        later_real = lax.dynamic_slice_in_dim(padded_real, lag, count, 0)
        later_imag = lax.dynamic_slice_in_dim(padded_imag, lag, count, 0)
        tap_real = lax.dynamic_slice_in_dim(filt_real_cols, lag, 1, 0)
        tap_imag = lax.dynamic_slice_in_dim(filt_imag_cols, lag, 1, 0)
        weight = lag_mask(regions, lag, True)
        back_real = running[0] + weight * (tap_real * later_real + tap_imag * later_imag)
        back_imag = running[1] + weight * (tap_real * later_imag - tap_imag * later_real)
        add_real = jnp.sum(
            weight * (own_real * later_real + own_imag * later_imag), axis=0, keepdims=True
        )
        add_imag = jnp.sum(
            weight * (own_real * later_imag - own_imag * later_real), axis=0, keepdims=True
        )
        sum_real = lax.dynamic_update_slice_in_dim(
            running[2], lax.dynamic_slice_in_dim(running[2], lag, 1, 0) + add_real, lag, 0
        )
        sum_imag = lax.dynamic_update_slice_in_dim(
            running[3], lax.dynamic_slice_in_dim(running[3], lag, 1, 0) + add_imag, lag, 0
        )
        return (back_real, back_imag, sum_real, sum_imag)

    return lax.fori_loop(0, count, one_lag, (zeros, zeros, zeros, zeros))


def body(
    tokens,
    out_grad,
    lengths,
    ln1_gain,
    w_in,
    short_w,
    filt_in,
    filt_shift,
    sine_freq,
    filt_out,
    decay,
    filter_bias,
    w_out,
    ln2_gain,
    mlp_up,
    mlp_down,
):
    gathered = (
        lax.all_gather(ln1_gain, "seq", axis=1, tiled=True),
        lax.all_gather(w_in, "seq", axis=1, tiled=True),
        lax.all_gather(short_w, "seq", axis=2, tiled=True),
        lax.all_gather(filt_in, "seq", axis=2, tiled=True),
        lax.all_gather(filt_shift, "seq", axis=1, tiled=True),
        lax.all_gather(sine_freq, "seq", axis=1, tiled=True),
        lax.all_gather(filt_out, "seq", axis=1, tiled=True),
        lax.all_gather(decay, "seq", axis=1, tiled=True),
        lax.all_gather(filter_bias, "seq", axis=1, tiled=True),
        lax.all_gather(w_out, "seq", axis=1, tiled=True),
        lax.all_gather(ln2_gain, "seq", axis=1, tiled=True),
        lax.all_gather(mlp_up, "seq", axis=1, tiled=True),
        lax.all_gather(mlp_down, "seq", axis=1, tiled=True),
    )
    gain_one = gathered[0][0].astype(jnp.float32)
    in_matrix = gathered[1][0]
    short_weights = gathered[2][0].astype(jnp.float32)
    in_filter = gathered[3][0].astype(jnp.float32)
    shift_filter = gathered[4][0].astype(jnp.float32)
    freq_filter = gathered[5][0].astype(jnp.float32)
    out_filter = gathered[6][0].astype(jnp.float32)
    decay_filter = gathered[7][0].astype(jnp.float32)
    bias_filter = gathered[8][0].astype(jnp.float32)
    out_matrix = gathered[9][0]
    gain_two = gathered[10][0].astype(jnp.float32)
    up_matrix = gathered[11][0]
    down_matrix = gathered[12][0]
    micro_count, block_rows, model_width = tokens.shape
    seq_count = lax.axis_size("seq")
    seq_index = lax.axis_index("seq")
    section_index = lax.axis_index("section")
    slots = block_rows * seq_count
    col_width = model_width // seq_count
    col_start = seq_index * col_width
    cosine, sine, parity = dft_tables(block_rows)
    scale_back = parity / (2.0 * block_rows)
    embedding = positions_embedding(slots, FREQS)

    def taps_from(in_weights, shift_values, freq_values, out_weights, decay_values):
        return filter_taps(
            in_weights, shift_values, freq_values, out_weights, decay_values, embedding
        )

    taps, taps_pull = jax.vjp(
        taps_from, in_filter, shift_filter, freq_filter, out_filter, decay_filter
    )
    tap_real, tap_imag = transform(cosine, sine, taps.reshape(seq_count, block_rows, model_width))
    zero_spec = jnp.zeros((1, 2 * block_rows, model_width), jnp.float32)
    filt_real = jnp.concatenate([zero_spec, tap_real[:-1]], axis=0) + parity * tap_real
    filt_imag = jnp.concatenate([zero_spec, tap_imag[:-1]], axis=0) + parity * tap_imag
    filt_real_cols = lax.dynamic_slice_in_dim(filt_real, col_start, col_width, 2)
    filt_imag_cols = lax.dynamic_slice_in_dim(filt_imag, col_start, col_width, 2)

    def backward_tick(stored, upstream, spec_grad_real, spec_grad_imag):
        (
            layer_in,
            normed,
            projected,
            rim_rows,
            mixed,
            signal,
            filtered,
            gated_out,
            residual,
            normed_two,
            upward,
            activated,
            own_real,
            own_imag,
            regions,
            valid_rows,
            carried_on,
        ) = stored
        upstream_low = upstream.astype(jnp.bfloat16)
        grad_down = transpose_left(activated, upstream_low)
        grad_act = transpose_right(upstream_low, down_matrix)
        grad_up_in = jax.vjp(gelu_tanh, upward)[1](grad_act)[0].astype(jnp.bfloat16)
        grad_up = transpose_left(normed_two, grad_up_in)
        grad_norm_two = transpose_right(grad_up_in, up_matrix)
        grad_resid_norm, grad_gain_two = jax.vjp(layer_norm, residual, gain_two)[1](grad_norm_two)
        grad_residual = upstream + grad_resid_norm
        grad_branch = grad_residual.astype(jnp.bfloat16)
        grad_out = transpose_left(gated_out, grad_branch)
        grad_gated = transpose_right(grad_branch, out_matrix)
        first_part = mixed[:, :model_width]
        second_part = mixed[:, model_width : 2 * model_width]
        third_part = mixed[:, 2 * model_width :]
        grad_second = grad_gated * filtered
        grad_filtered = grad_gated * second_part
        grad_bias = jnp.sum(grad_filtered * signal, axis=0)
        sent_back = (grad_filtered * valid_rows[:, None])[None]
        columns = lax.all_to_all(
            sent_back[0].astype(jnp.bfloat16), "seq", split_axis=1, concat_axis=0, tiled=True
        ).astype(jnp.float32)
        later_real, later_imag = transform(
            cosine, sine, columns.reshape(seq_count, block_rows, col_width)
        )
        back_real, back_imag, add_real, add_imag = channel_correlate(
            own_real,
            own_imag,
            scale_back * later_real,
            scale_back * later_imag,
            filt_real_cols,
            filt_imag_cols,
            regions,
        )
        back_cols = transform_back(cosine, sine, back_real, back_imag).reshape(slots, col_width)
        grad_masked = lax.all_to_all(
            as_sent(back_cols), "seq", split_axis=0, concat_axis=1, tiled=True
        ).astype(back_cols.dtype)
        new_real = lax.dynamic_update_slice_in_dim(
            spec_grad_real,
            lax.dynamic_slice_in_dim(spec_grad_real, col_start, col_width, 2) + add_real,
            col_start,
            2,
        )
        new_imag = lax.dynamic_update_slice_in_dim(
            spec_grad_imag,
            lax.dynamic_slice_in_dim(spec_grad_imag, col_start, col_width, 2) + add_imag,
            col_start,
            2,
        )
        grad_signal = grad_masked * valid_rows[:, None] + bias_filter * grad_filtered
        grad_mixed = jnp.concatenate(
            [grad_signal * third_part, grad_second, grad_signal * first_part], axis=1
        )

        def short_from(rim_values, proj_values, weight_values):
            return short_mix(rim_values, proj_values, weight_values, carried_on)

        short_pull = jax.vjp(
            short_from, rim_rows.astype(jnp.float32), projected.astype(jnp.float32), short_weights
        )[1]
        grad_rim, grad_proj, grad_short = short_pull(grad_mixed)
        returned = shifted(grad_rim, "seq", -1)
        grad_proj = grad_proj + jnp.concatenate(
            [jnp.zeros((block_rows - 2, 3 * model_width), jnp.float32), returned], axis=0
        )
        grad_proj_low = grad_proj.astype(jnp.bfloat16)
        grad_in = transpose_left(normed, grad_proj_low)
        grad_normed = transpose_right(grad_proj_low, in_matrix)
        grad_norm_in, grad_gain_one = jax.vjp(layer_norm, layer_in, gain_one)[1](grad_normed)
        grad_layer_in = grad_residual + grad_norm_in
        weight_grads = (
            grad_gain_one,
            grad_in,
            grad_short,
            grad_bias,
            grad_out,
            grad_gain_two,
            grad_up,
            grad_down,
        )
        return (grad_layer_in, weight_grads, new_real, new_imag)

    zero_rows = jnp.zeros((block_rows, model_width), jnp.bfloat16)
    received = zero_rows
    stored_all = []
    produced = []
    for tick_index in range(micro_count + 1):
        batch_index = jnp.clip(tick_index - section_index, 0, micro_count - 1)
        if tick_index < micro_count:
            fresh = tokens[tick_index]
        else:
            fresh = zero_rows
        layer_in = jnp.where(section_index == 0, fresh, received).astype(jnp.float32)
        length_row = lax.dynamic_index_in_dim(lengths, batch_index, 0, keepdims=False)
        forward_regions, forward_valid_rows, forward_carried_on = block_geometry(
            length_row, block_rows, seq_index
        )
        forward_normed = layer_norm(layer_in, gain_one).astype(jnp.bfloat16)
        forward_projected = matmul_low(forward_normed, in_matrix).astype(jnp.bfloat16)
        forward_rim_rows = shifted(forward_projected[block_rows - 2 :], "seq", 1)
        forward_mixed = short_mix(
            forward_rim_rows.astype(jnp.float32),
            forward_projected.astype(jnp.float32),
            short_weights,
            forward_carried_on,
        )
        forward_first_part = forward_mixed[:, :model_width]
        forward_second_part = forward_mixed[:, model_width : 2 * model_width]
        forward_third_part = forward_mixed[:, 2 * model_width :]
        forward_signal = forward_first_part * forward_third_part
        masked = (forward_signal * forward_valid_rows[:, None])[None]
        forward_columns = lax.all_to_all(
            masked[0].astype(jnp.bfloat16), "seq", split_axis=1, concat_axis=0, tiled=True
        ).astype(jnp.float32)
        forward_own_real, forward_own_imag = transform(
            cosine, sine, forward_columns.reshape(seq_count, block_rows, col_width)
        )
        out_real, out_imag = channel_convolve(
            forward_own_real, forward_own_imag, filt_real_cols, filt_imag_cols, forward_regions
        )
        conv_cols = transform_back(
            cosine, sine, scale_back * out_real, scale_back * out_imag
        ).reshape(slots, col_width)
        conv_out = lax.all_to_all(
            as_sent(conv_cols), "seq", split_axis=0, concat_axis=1, tiled=True
        ).astype(conv_cols.dtype)
        forward_filtered = conv_out * forward_valid_rows[:, None] + bias_filter * forward_signal
        forward_gated_out = (forward_second_part * forward_filtered).astype(jnp.bfloat16)
        forward_residual = layer_in + matmul_low(forward_gated_out, out_matrix)
        forward_normed_two = layer_norm(forward_residual, gain_two).astype(jnp.bfloat16)
        forward_upward = matmul_low(forward_normed_two, up_matrix)
        forward_activated = gelu_tanh(forward_upward).astype(jnp.bfloat16)
        layer_out = forward_residual + matmul_low(forward_activated, down_matrix)
        forward_stored = (
            layer_in,
            forward_normed,
            forward_projected,
            forward_rim_rows,
            forward_mixed,
            forward_signal,
            forward_filtered,
            forward_gated_out,
            forward_residual,
            forward_normed_two,
            forward_upward,
            forward_activated,
            forward_own_real,
            forward_own_imag,
            forward_regions,
            forward_valid_rows,
            forward_carried_on,
        )
        layer_out, stored = (layer_out, forward_stored)
        layer_low = layer_out.astype(jnp.bfloat16)
        produced.append(layer_low)
        stored_all.append(stored)
        if tick_index < micro_count:
            received = shifted(layer_low, "section", 1)
    coming = jnp.zeros((block_rows, model_width), jnp.float32)
    spec_grad_real = jnp.zeros_like(filt_real)
    spec_grad_imag = jnp.zeros_like(filt_imag)
    totals = None
    returned_all = []
    for tick_index in range(micro_count + 1):
        if tick_index < micro_count:
            given = out_grad[micro_count - 1 - tick_index].astype(jnp.float32)
        else:
            given = jnp.zeros((block_rows, model_width), jnp.float32)
        upstream = jnp.where(section_index == 1, given, coming)
        grad_layer_in, weight_grads, spec_grad_real, spec_grad_imag = backward_tick(
            stored_all[micro_count - tick_index], upstream, spec_grad_real, spec_grad_imag
        )
        grad_low = grad_layer_in.astype(jnp.bfloat16)
        returned_all.append(grad_low)
        if totals is None:
            totals = weight_grads
        else:
            totals = tuple((earlier + latest for earlier, latest in zip(totals, weight_grads)))
        if tick_index < micro_count:
            coming = shifted(grad_low, "section", -1).astype(jnp.float32)
    grad_h_real = parity * spec_grad_real + jnp.concatenate([spec_grad_real[1:], zero_spec], axis=0)
    grad_h_imag = parity * spec_grad_imag + jnp.concatenate([spec_grad_imag[1:], zero_spec], axis=0)
    grad_taps = transform_back(cosine, sine, grad_h_real, grad_h_imag).reshape(slots, model_width)
    filter_grads = taps_pull(grad_taps)
    full_grads = [
        totals[0][None],
        totals[1][None],
        totals[2][None],
        filter_grads[0][None],
        filter_grads[1][None],
        filter_grads[2][None],
        filter_grads[3][None],
        filter_grads[4][None],
        totals[3][None],
        totals[4][None],
        totals[5][None],
        totals[6][None],
        totals[7][None],
    ]
    spread = (
        lax.psum_scatter(
            full_grads[0].astype(jnp.bfloat16), "seq", scatter_dimension=1, tiled=True
        ).astype(jnp.float32),
        lax.psum_scatter(
            full_grads[1].astype(jnp.bfloat16), "seq", scatter_dimension=1, tiled=True
        ).astype(jnp.float32),
        lax.psum_scatter(
            full_grads[2].astype(jnp.bfloat16), "seq", scatter_dimension=2, tiled=True
        ).astype(jnp.float32),
        lax.psum_scatter(
            full_grads[3].astype(jnp.bfloat16), "seq", scatter_dimension=2, tiled=True
        ).astype(jnp.float32),
        lax.psum_scatter(
            full_grads[4].astype(jnp.bfloat16), "seq", scatter_dimension=1, tiled=True
        ).astype(jnp.float32),
        lax.psum_scatter(
            full_grads[5].astype(jnp.bfloat16), "seq", scatter_dimension=1, tiled=True
        ).astype(jnp.float32),
        lax.psum_scatter(
            full_grads[6].astype(jnp.bfloat16), "seq", scatter_dimension=1, tiled=True
        ).astype(jnp.float32),
        lax.psum_scatter(
            full_grads[7].astype(jnp.bfloat16), "seq", scatter_dimension=1, tiled=True
        ).astype(jnp.float32),
        lax.psum_scatter(
            full_grads[8].astype(jnp.bfloat16), "seq", scatter_dimension=1, tiled=True
        ).astype(jnp.float32),
        lax.psum_scatter(
            full_grads[9].astype(jnp.bfloat16), "seq", scatter_dimension=1, tiled=True
        ).astype(jnp.float32),
        lax.psum_scatter(
            full_grads[10].astype(jnp.bfloat16), "seq", scatter_dimension=1, tiled=True
        ).astype(jnp.float32),
        lax.psum_scatter(
            full_grads[11].astype(jnp.bfloat16), "seq", scatter_dimension=1, tiled=True
        ).astype(jnp.float32),
        lax.psum_scatter(
            full_grads[12].astype(jnp.bfloat16), "seq", scatter_dimension=1, tiled=True
        ).astype(jnp.float32),
    )
    summed = (
        lax.psum(spread[0].astype(jnp.bfloat16), "dp").astype(jnp.float32),
        lax.psum(spread[1].astype(jnp.bfloat16), "dp").astype(jnp.float32),
        lax.psum(spread[2].astype(jnp.bfloat16), "dp").astype(jnp.float32),
        lax.psum(spread[3].astype(jnp.bfloat16), "dp").astype(jnp.float32),
        lax.psum(spread[4].astype(jnp.bfloat16), "dp").astype(jnp.float32),
        lax.psum(spread[5].astype(jnp.bfloat16), "dp").astype(jnp.float32),
        lax.psum(spread[6].astype(jnp.bfloat16), "dp").astype(jnp.float32),
        lax.psum(spread[7].astype(jnp.bfloat16), "dp").astype(jnp.float32),
        lax.psum(spread[8].astype(jnp.bfloat16), "dp").astype(jnp.float32),
        lax.psum(spread[9].astype(jnp.bfloat16), "dp").astype(jnp.float32),
        lax.psum(spread[10].astype(jnp.bfloat16), "dp").astype(jnp.float32),
        lax.psum(spread[11].astype(jnp.bfloat16), "dp").astype(jnp.float32),
        lax.psum(spread[12].astype(jnp.bfloat16), "dp").astype(jnp.float32),
    )
    layer_outputs = jnp.stack(
        [
            jnp.where(section_index == 0, produced[batch_slot], produced[batch_slot + 1])
            for batch_slot in range(micro_count)
        ]
    )[None]
    input_grads = jnp.stack(
        [
            jnp.where(
                section_index == 0,
                returned_all[micro_count - batch_slot],
                returned_all[micro_count - 1 - batch_slot],
            )
            for batch_slot in range(micro_count)
        ]
    )[None]
    return (
        layer_outputs,
        input_grads,
        summed[0],
        summed[1],
        summed[2],
        summed[3],
        summed[4],
        summed[5],
        summed[6],
        summed[7],
        summed[8],
        summed[9],
        summed[10],
        summed[11],
        summed[12],
    )


def solution(mesh):
    in_specs = (
        P("dp", "seq", None),
        P("dp", "seq", None),
        P("dp", None),
        P("section", "seq"),
        P("section", "seq", None),
        P("section", None, "seq"),
        P("section", None, "seq"),
        P("section", "seq"),
        P("section", "seq"),
        P("section", "seq", None),
        P("section", "seq"),
        P("section", "seq"),
        P("section", "seq", None),
        P("section", "seq"),
        P("section", "seq", None),
        P("section", "seq", None),
    )
    out_specs = (
        P("section", "dp", "seq", None),
        P("section", "dp", "seq", None),
        P("section", "seq"),
        P("section", "seq", None),
        P("section", None, "seq"),
        P("section", None, "seq"),
        P("section", "seq"),
        P("section", "seq"),
        P("section", "seq", None),
        P("section", "seq"),
        P("section", "seq"),
        P("section", "seq", None),
        P("section", "seq"),
        P("section", "seq", None),
        P("section", "seq", None),
    )
    return jax.shard_map(body, mesh=mesh, in_specs=in_specs, out_specs=out_specs, check_vma=False)
```

profile of v0, /device:TPU:0, one launch (start us, length us, event | category | flops | bytes accessed | tf_op | source)
XLA Modules:
  0.0 1849.0 jit_solution(5489290894225053652)
XLA Ops:
  10.7 9.6 all_gather.39
  22.0 8.0 all_gather.46
  30.1 8.5 all_gather.45
  40.4 8.9 all-reduce.45
  49.7 8.4 all_gather.43
  63.1 13.5 convolution_bitcast_fusion
  76.6 7.5 all_gather.40
  84.7 14.4 convolution_bitcast_fusion.1
  152.7 66.5 %while.114 = (s32[]{:T(128)}, f32[4,512,256]{2,1,0:T(8,128)}, f32[4,512,256]{2,1,0:T(8,128)}, s32[4]{0:T(128)S(1)}, f32[4,512,256]{2,1,0:T(8,128)}, /*index=5*/f...) while((s32[]{:T(128)}, f32[4,512,256]{2,1,0:T(8,128)}, ...), condition=%wide.region_9.10_spmd.clone, body=%wide.region_7.9_spmd.clone.sunk | while | flops 6291539 | bytes 32506180 | solution.py:154
  219.3 7.4 fusion.117
  237.2 13.7 all_gather.47
  250.9 9.1 all_gather.49
  268.3 7.9 fusion.22
  276.1 30.1 %all-gather.11.cloned.1.call-done = bf16[1,4096,1024]{2,1,0:T(8,128)(2,1)} async-done(((bf16[1,1024,1024]{2,1,0:T(8,128)(2,1)}), bf16[1,4096,1024]{2,1,0:T(8,128)(2,1)}) %all-gather.11.cloned.1.call-update) | async-done | bytes 8388624 | tf_op jit(solution)/shard_map/all_gather | solution.py:221
  306.3 7.4 fusion.169
  359.4 65.7 %while.115 = (s32[]{:T(128)}, f32[4,512,256]{2,1,0:T(8,128)}, f32[4,512,256]{2,1,0:T(8,128)}, s32[4]{0:T(128)S(1)}, f32[4,512,256]{2,1,0:T(8,128)}, /*index=5*/f...) while((s32[]{:T(128)}, f32[4,512,256]{2,1,0:T(8,128)}, ...), condition=%wide.region_21.22_spmd.clone, body=%wide.region_19.21_spmd.clone.sunk | while | flops 6291539 | bytes 32506180 | solution.py:154
  437.6 10.1 all_to_all.156
  491.9 8.1 all-to-all-done.4
  512.1 65.6 %while.116 = (s32[]{:T(128)}, f32[4,512,256]{2,1,0:T(8,128)}, f32[4,512,256]{2,1,0:T(8,128)}, s32[4]{0:T(128)S(1)}, f32[4,512,256]{2,1,0:T(8,128)}, /*index=5*/f...) while((s32[]{:T(128)}, f32[4,512,256]{2,1,0:T(8,128)}, ...), condition=%wide.region_33.34_spmd.clone, body=%wide.region_31.33_spmd.clone.sunk | while | flops 6291539 | bytes 32506180 | solution.py:154
  594.6 7.2 all-to-all-done.5
  614.7 9.5 fusion.67
  665.3 89.4 %while.117 = (s32[]{:T(128)}, f32[4,512,256]{2,1,0:T(8,128)}, f32[4,512,256]{2,1,0:T(8,128)}, f32[4,512,256]{1,2,0:T(8,128)}, f32[4,512,256]{1,2,0:T(8,128)}, /*...) while((s32[]{:T(128)}, f32[4,512,256]{2,1,0:T(8,128)}, ...), condition=%wide.region_42.43_spmd.clone, body=%wide.region_38.42_spmd.clone.sunk | while | flops 11534415 | bytes 49283376 | solution.py:187
  767.0 10.2 all_to_all.157
  805.8 7.3 multiply_reduce_fusion.16
  849.2 89.2 %while.118 = (s32[]{:T(128)}, f32[4,512,256]{2,1,0:T(8,128)}, f32[4,512,256]{2,1,0:T(8,128)}, f32[4,512,256]{1,2,0:T(8,128)}, f32[4,512,256]{1,2,0:T(8,128)}, /*...) while((s32[]{:T(128)}, f32[4,512,256]{2,1,0:T(8,128)}, ...), condition=%wide.region_51.52_spmd.clone, body=%wide.region_47.51_spmd.clone.sunk | while | flops 11534415 | bytes 49283376 | solution.py:187
  1002.1 7.3 multiply_reduce_fusion.15
  1046.2 89.7 %while.119 = (s32[]{:T(128)}, f32[4,512,256]{2,1,0:T(8,128)}, f32[4,512,256]{2,1,0:T(8,128)}, f32[4,512,256]{1,2,0:T(8,128)}, f32[4,512,256]{1,2,0:T(8,128)}, /*...) while((s32[]{:T(128)}, f32[4,512,256]{2,1,0:T(8,128)}, ...), condition=%wide.region_60.61_spmd.clone, body=%wide.region_56.60_spmd.clone.sunk | while | flops 11534415 | bytes 49283376 | solution.py:187
  1153.3 8.5 fusion.333
  1177.8 12.2 fusion.34
  1191.3 10.8 fusion.507
  1202.2 8.9 fusion.506
  1211.1 16.9 fusion.32
  1229.2 11.0 fusion.243
  1240.2 8.7 fusion.338
  1248.9 18.5 fusion.33
  1297.1 14.0 fusion.24
  1318.5 16.1 bitcast_multiply_fusion.2
  1349.8 7.4 bitcast_reduce_fusion
  1364.1 77.1 %reduce-scatter.31.cloned.1.call-done = bf16[1,1024,1024]{2,1,0:T(8,128)(2,1)} async-done(((bf16[1,4096,1024]{2,1,0:T(8,128)(2,1)}), bf16[1,1024,1024]{2,1,0:T(8,128)(2,1)}) %reduce-scatter.31.cloned.1.call-update) | async-done | bytes 2097168 | tf_op jit(solution)/shard_map/reduce_scatter | solution.py:518
  1442.7 7.4 fusion.205
  1451.2 17.0 reduce-scatter.39.cloned.1.call-done
  1469.2 25.8 %reduce-scatter.41.cloned.1.call-done = bf16[256,1]{1,0:T(8,128)(2,1)} async-done(((bf16[1024,1]{1,0:T(8,128)(2,1)}), bf16[256,1]{1,0:T(8,128)(2,1)}) %reduce-scatter.41.cloned.1.call-update) | async-done | bytes 528
  1501.7 15.8 all-reduce.44
  1526.0 22.8 %reduce-scatter.33.cloned.1.call-done = bf16[256,1]{1,0:T(8,128)(2,1)} async-done(((bf16[1024,1]{1,0:T(8,128)(2,1)}), bf16[256,1]{1,0:T(8,128)(2,1)}) %reduce-scatter.33.cloned.1.call-update) | async-done | bytes 528
  1549.8 28.4 %reduce-scatter.35.cloned.1.call-done = bf16[768,3]{1,0:T(8,128)(2,1)} async-done(((bf16[3072,3]{1,0:T(8,128)(2,1)}), bf16[768,3]{1,0:T(8,128)(2,1)}) %reduce-scatter.35.cloned.1.call-update) | async-done | bytes 4624
  1580.5 24.9 %reduce-scatter.25.cloned.1.call-done = bf16[1,16,1024]{2,1,0:T(8,128)(2,1)} async-done(((bf16[1,64,1024]{2,1,0:T(8,128)(2,1)}), bf16[1,16,1024]{2,1,0:T(8,128)(2,1)}) %reduce-scatter.25.cloned.1.call-update) | async-done | bytes 32784 | tf_op jit(solution)/shard_map/reduce_scatter | solution.py:500
  1605.4 24.3 %all-reduce.42 = (bf16[1,256]{1,0:T(2,128)(2,1)S(1)}, bf16[1,3,768]{2,0,1:T(2,128)(2,1)S(1)}, bf16[1,33,16]{1,0,2:T(2,128)(2,1)S(1)}, bf16[1,16]{1,0:T(2,128)(2,...) all-reduce(bf16[1,256]{1,0:T(2,128)(2,1)S(1)} %copy.387, ...), channel_id=1, replica_groups=mesh['section'=2,'seq'=4,'dp'=4] {'dp'}, use_global_device_ids=true, to_apply=%region_67.68 | all-reduce | flops 20272 | bytes 81088 | tf_op jit(solution)/shard_map/psum | solution.py:523
  1634.9 197.7 %all-reduce.48.cloned.1.call-done = (bf16[1,256,3072]{2,1,0:T(8,128)(2,1)}, bf16[1,256,1024]{2,1,0:T(8,128)(2,1)}, bf16[1,256,4096]{2,1,0:T(8,128)(2,1)}, bf16[1,1024,1024]{2,1,0:T(8,128)(2,1)}) async-done(((bf16[1,256,3072]{2,1,0:T(8,128)(2,1)}, bf16[1,256,1024]{2,1,0:T(8,128)(2,1)}, bf16[1,256,4096]{2,1,0:T(8,128)(2,1)}, bf16[1,1024,1024]{2,1,0:T(8,128)(2,1)}), (bf16[1,256,3072]{2,1,0:T(8,128)(2,1)}, ...) | async-done | bytes 6291472 | tf_op jit(solution)/shard_map/psum | solution.py:524
  (1131 shorter events, 1033.6 us)
Async XLA Ops:
  7.2 92.0 %all-gather.5.cloned.1.call-start = ((), (), s32[]{:S(2)}) async-start(), calls=%async_computation.22 | async-start | bytes 7864320 | tf_op jit(solution)/shard_map/all_gather | solution.py:210
  8.0 257.4 %all-gather.7.cloned.1.call-start = ((), (), s32[]{:S(2)}) async-start(), calls=%async_computation.23 | async-start | bytes 2621440 | tf_op jit(solution)/shard_map/all_gather | solution.py:218
  8.8 259.5 %all-gather.9.cloned.1.call-start = ((), (), s32[]{:S(2)}) async-start(), calls=%async_computation.24 | async-start | bytes 10485760 | tf_op jit(solution)/shard_map/all_gather | solution.py:220
  9.5 296.8 %all-gather.11.cloned.1.call-start = ((), (), s32[]{:S(2)}) async-start(), calls=%async_computation.25 | async-start | bytes 10485760 | tf_op jit(solution)/shard_map/all_gather | solution.py:221
  10.4 88.8 %copy-start.191 = (f32[256]{0:T(256)}, f32[256]{0:T(256)S(1)}, u32[]{:S(2)}) copy-start(f32[256]{0:T(256)S(1)} %broadcast_multiply_fusion.15) | copy-start | bytes 3076
  10.7 88.5 %copy-start.200 = (f32[256]{0:T(256)}, f32[256]{0:T(256)S(1)}, u32[]{:S(2)}) copy-start(f32[256]{0:T(256)S(1)} %fusion.392) | copy-start | bytes 3076
  20.4 458.9 %copy-start.129 = (f32[1,1,3072]{2,1,0:T(1,128)}, f32[1,1,3072]{2,1,0:T(1,128)S(1)}, u32[]{:S(2)}) copy-start(f32[1,1,3072]{2,1,0:T(1,128)S(1)} %get-tuple-element.1919) | copy-start | bytes 36868
  20.4 458.9 %copy-start.131 = (f32[1,1,3072]{2,1,0:T(1,128)}, f32[1,1,3072]{2,1,0:T(1,128)S(1)}, u32[]{:S(2)}) copy-start(f32[1,1,3072]{2,1,0:T(1,128)S(1)} %get-tuple-element.1920) | copy-start | bytes 36868
  20.4 458.9 %copy-start.133 = (f32[1,1,3072]{2,1,0:T(1,128)}, f32[1,1,3072]{2,1,0:T(1,128)S(1)}, u32[]{:S(2)}) copy-start(f32[1,1,3072]{2,1,0:T(1,128)S(1)} %get-tuple-element.1921) | copy-start | bytes 36868
  84.1 383.8 %copy-start.119 = (f32[1,1024]{1,0:T(1,128)}, f32[1,1024]{1,0:T(1,128)S(1)}, u32[]{:S(2)}) copy-start(f32[1,1024]{1,0:T(1,128)S(1)} %mul.2498) | copy-start | bytes 12292
  105.2 15.2 collective-permute-start
  109.3 153.4 %copy-start.177 = (f32[256]{0:T(256)}, f32[256]{0:T(256)S(1)}, u32[]{:S(2)}) copy-start(f32[256]{0:T(256)S(1)} %compare_convert_fusion.2) | copy-start | bytes 3076
  125.2 15.3 all-to-all-start
  232.9 27.1 %all-to-all-start.1 = ((bf16[4,256,256]{1,2,0:T(8,128)(2,1)}), bf16[4,256,256]{1,2,0:T(8,128)(2,1)S(1)}, u32[]{:S(2)}, u32[]{:S(2)}) async-start(bf16[4,256,256]{1,2,0:T(8,128)(2,1)} %fusion.184), calls=%async_computation.1 | async-start | bytes 1048576 | tf_op jit(solution)/shard_map/all_to_all | solution.py:405
  313.7 4.3 collective-permute-start.1
  325.1 5.3 collective-permute-start.2
  329.1 122.3 %copy-start.179 = (f32[256]{0:T(256)}, f32[256]{0:T(256)S(1)}, u32[]{:S(2)}) copy-start(f32[256]{0:T(256)S(1)} %compare_convert_fusion.1) | copy-start | bytes 3076
  336.4 11.0 all-to-all-start.2
  464.6 2.8 collective-permute-start.3
  474.4 4.8 collective-permute-start.4
  488.0 12.0 all-to-all-start.4
  590.9 10.9 all-to-all-start.5
  640.1 10.4 all-to-all-start.6
  786.8 6.0 collective-permute-start.5
  796.6 3.9 collective-permute-start.6
  821.5 12.6 all-to-all-start.8
  951.4 12.3 all-to-all-start.9
  974.7 6.1 collective-permute-start.7
  985.5 10.9 collective-permute-start.8
  1017.8 13.1 all-to-all-start.10
  1021.6 342.4 %reduce-scatter.27.cloned.1.call-start = ((), (), s32[]{:S(2)}) async-start(), calls=%async_computation.28 | async-start | bytes 2621440 | tf_op jit(solution)/shard_map/reduce_scatter | solution.py:509
  1148.9 12.9 all-to-all-start.11
  1153.0 211.0 %reduce-scatter.23.cloned.1.call-start = ((), (), s32[]{:S(2)}) async-start(), calls=%async_computation.26 | async-start | bytes 7864320 | tf_op jit(solution)/shard_map/reduce_scatter | solution.py:485
  1172.0 5.9 collective-permute-start.9
  1190.1 173.9 %reduce-scatter.29.cloned.1.call-start = ((), (), s32[]{:S(2)}) async-start(), calls=%async_computation.29 | async-start | bytes 10485760 | tf_op jit(solution)/shard_map/reduce_scatter | solution.py:515
  1228.0 213.1 %reduce-scatter.31.cloned.1.call-start = ((), (), s32[]{:S(2)}) async-start(), calls=%async_computation.30 | async-start | bytes 10485760 | tf_op jit(solution)/shard_map/reduce_scatter | solution.py:518
  1267.4 200.9 %reduce-scatter.39.cloned.1.call-start = ((), (), s32[]{:S(2)}) async-start(), calls=%async_computation.34 | async-start | bytes 327680
  1288.7 206.3 %reduce-scatter.41.cloned.1.call-start = ((), (), s32[]{:S(2)}) async-start(), calls=%async_computation.35 | async-start | bytes 327680
  1289.7 232.4 %reduce-scatter.37.cloned.1.call-start = ((), (), s32[]{:S(2)}) async-start(), calls=%async_computation.33 | async-start | bytes 327680
  1339.1 209.8 %reduce-scatter.33.cloned.1.call-start = ((), (), s32[]{:S(2)}) async-start(), calls=%async_computation.31 | async-start | bytes 327680
  1349.8 228.4 %reduce-scatter.35.cloned.1.call-start = ((), (), s32[]{:S(2)}) async-start(), calls=%async_computation.32 | async-start | bytes 983040
  1357.3 248.1 %reduce-scatter.25.cloned.1.call-start = ((), (), s32[]{:S(2)}) async-start(), calls=%async_computation.27 | async-start | bytes 163840 | tf_op jit(solution)/shard_map/reduce_scatter | solution.py:500
  1363.8 468.8 %all-reduce.48.cloned.1.call-start = ((), (), s32[]{:S(2)}) async-start(), calls=%async_computation.36 | async-start | bytes 12582912 | tf_op jit(solution)/shard_map/psum | solution.py:524
  1442.7 53.2 %copy-start.128 = (bf16[1,64,1024]{2,1,0:T(8,128)(2,1)S(1)}, bf16[1,64,1024]{2,1,0:T(8,128)(2,1)}, u32[]{:S(2)}) copy-start(bf16[1,64,1024]{2,1,0:T(8,128)(2,1)} %copy-done.127) | copy-start | bytes 393220
  1451.2 71.8 %copy-start.55 = (bf16[2,256,1024]{2,1,0:T(8,128)(2,1)S(1)}, bf16[2,256,1024]{2,1,0:T(8,128)(2,1)}, u32[]{:S(2)}) copy-start(bf16[2,256,1024]{2,1,0:T(8,128)(2,1)} %param.28) | copy-start | bytes 3145732
  1451.2 71.8 %copy-start.73 = (f32[256,1024]{1,0:T(8,128)S(1)}, f32[256,1024]{1,0:T(8,128)}, u32[]{:S(2)}) copy-start(f32[256,1024]{1,0:T(8,128)} %copy-done.72) | copy-start | bytes 3145732
  1451.2 71.8 %copy-start.95 = (bf16[256,1024]{1,0:T(8,128)(2,1)S(1)}, bf16[256,1024]{1,0:T(8,128)(2,1)}, u32[]{:S(2)}) copy-start(bf16[256,1024]{1,0:T(8,128)(2,1)} %copy-done.93) | copy-start | bytes 1572868
  1451.2 71.9 %copy-start.216 = (f32[256]{0:T(256)S(1)}, f32[256]{0:T(256)}, u32[]{:S(2)}) copy-start(f32[256]{0:T(256)} %copy-done.215) | copy-start | bytes 3076
  (228 other events, 1920.7 us)
Sparse Core Ops, SparseCore 0:
  9.9 74.0 all-gather.4
  85.9 35.4 all-gather.6
  123.2 88.0 all-gather.8
  213.0 93.2 all-gather.10
  1027.3 36.9 reduce-scatter.26
  1190.2 71.6 reduce-scatter.22
  1265.2 86.3 reduce-scatter.28
  1354.7 86.3 reduce-scatter.30
  1444.1 24.0 reduce-scatter.38
  1470.9 24.0 reduce-scatter.40
  1498.0 24.1 reduce-scatter.36
  1524.8 24.0 reduce-scatter.32
  1552.0 26.1 reduce-scatter.34
  1581.5 23.8 reduce-scatter.24
  1607.9 224.6 all-reduce.47
where the time goes:
time: 1860 us; the launch traced here: 1850 us
  local copies, waits for them, and re-layouts  476 us (26%)
  waiting for transfers between devices  476 us (26%)
  matrix products  425 us (23%)
  other arithmetic  250 us (13%)
  blocking collectives  134 us (7%)
  starting transfers between devices  61.2 us (3%)
  between operations  24.9 us (1%)
    psum x1, waiting for transfers between devices, body(): lax.psum(spread[1].astype(jnp.bfloat16), 'dp').astype(jnp.float32)  198 us
    dot_general x12, matrix products, transpose_left(): lax.dot_general(left, right, (((0,), (0,)), ((), ())), preferred_element_...  113 us
    unnamed x20, waiting for transfers between devices  101 us
    dynamic_slice x24, local copies, waits for them, and re-layouts, one_lag(): later_imag = lax.dynamic_slice_in_dim(padded_imag, lag, count, 0)  91.4 us
    dynamic_slice x24, local copies, waits for them, and re-layouts, one_lag(): src_imag = lax.dynamic_slice_in_dim(padded_imag, count - lag, count, 0)  91.1 us
    reduce_scatter x1, waiting for transfers between devices, body(): lax.psum_scatter(full_grads[12].astype(jnp.bfloat16), 'seq', scatter_dime...  77.1 us
    reduce_sum x12, other arithmetic, one_lag(): jnp.sum(weight * (own_real * later_imag - own_imag * later_real), axis=0,...  76.3 us
    unnamed x510, local copies, waits for them, and re-layouts  68 us
  transfers between devices with their start and end apart: 35, of which 21 were waited for; matrix products, arithmetic and copies ran while one was open for 30% of the time, Pallas kernels for 0%

commit v1 on v0

v1 whole, which is shorter than its diff:
```python
import functools
import math

import jax
import jax.numpy as jnp
import numpy as np
from jax import lax
from jax.experimental import pallas as pl
from jax.experimental.pallas import tpu as pltpu
from jax.sharding import PartitionSpec as P

FREQS = 16
PRECISE = lax.Precision.HIGHEST
EPSILON = 1e-05
BF = jnp.bfloat16
F32 = jnp.float32


def dot(left, right):
    return jnp.dot(left, right, preferred_element_type=F32)


def dot_left(left, right):
    return lax.dot_general(left, right, (((0,), (0,)), ((), ())), preferred_element_type=F32)


def dot_right(left, right):
    return lax.dot_general(left, right, (((1,), (1,)), ((), ())), preferred_element_type=F32)


def layer_norm(values, gains):
    row_mean = jnp.mean(values, axis=-1, keepdims=True)
    centered = values - row_mean
    variance = jnp.mean(centered * centered, axis=-1, keepdims=True)
    return centered * lax.rsqrt(variance + EPSILON) * gains


def gelu_tanh(values):
    return jax.nn.gelu(values, approximate=True)


def positions_embedding(slots, harmonic_count):
    steps_all = np.arange(slots)
    scaled = steps_all / slots
    harmonics = np.arange(1, harmonic_count + 1)
    phase = (steps_all[:, None] * harmonics[None, :] % slots) * (2.0 * math.pi / slots)
    both = np.concatenate([scaled[:, None], np.cos(phase), np.sin(phase)], axis=1)
    return both.astype(np.float32)


def filter_taps(filt_in, filt_shift, sine_freq, filt_out, decay, embedding):
    slots = embedding.shape[0]
    inner = jnp.dot(embedding, filt_in, preferred_element_type=F32, precision=PRECISE)
    hidden_sine = jnp.sin(sine_freq * (inner + filt_shift))
    scaled = jnp.arange(slots, dtype=jnp.int32).astype(F32) / slots
    summed = jnp.dot(hidden_sine, filt_out, preferred_element_type=F32, precision=PRECISE)
    return summed * jnp.exp(-decay[None, :] * scaled[:, None])


def short_mix(rim_values, proj_values, weight_values, carried_on):
    total_rows = proj_values.shape[0]
    extended = jnp.concatenate([rim_values * carried_on, proj_values], axis=0)
    return (
        weight_values[0] * extended[2:]
        + weight_values[1] * extended[1 : total_rows + 1]
        + weight_values[2] * extended[:total_rows]
    )


def packed_dft(rows):
    size = 2 * rows
    phase = (np.arange(rows)[:, None] * np.arange(rows)[None, :] % size) * (2.0 * math.pi / size)
    lower = -np.sin(phase)
    lower[0] = 1 - 2 * (np.arange(rows) % 2)
    table = np.concatenate([np.cos(phase), lower], axis=0)
    weight = np.full((size, 1), 2.0 / size)
    weight[0] = weight[rows] = 1.0 / size
    parity = 1.0 - 2.0 * (np.arange(rows) % 2)
    parity = np.concatenate([parity, parity])[:, None]
    parity[rows] = 1 - 2 * (rows % 2)
    return table.astype(np.float32), weight.astype(np.float32), parity.astype(np.float32)


def spectra_rows(table_ref, source_ref, target_ref, blocks, rows):
    for block in range(blocks):
        target_ref[block] = jnp.dot(
            table_ref[...], source_ref[pl.ds(block * rows, rows), :], preferred_element_type=F32
        )


def convolve_kernel(blocks, rows, step, same_ref, table_ref, back_ref, filt_ref, x_ref, y_ref, spec_ref, out_ref):
    spectra_rows(table_ref, x_ref, spec_ref, blocks, rows)

    def chunk(index, carry):
        real = pl.ds(pl.multiple_of(index * step, step), step)
        imag = pl.ds(pl.multiple_of(rows + index * step, step), step)
        width = x_ref.shape[1]
        first = (lax.broadcasted_iota(jnp.int32, (step, width), 0) + index * step) == 0
        for i in range(blocks):
            total_real = jnp.zeros((step, width), F32)
            total_imag = jnp.zeros((step, width), F32)
            for lag in range(i + 1):
                weight = same_ref[i, i - lag]
                fr = filt_ref[lag, real, :]
                fi = filt_ref[lag, imag, :]
                cross = jnp.where(first, 0.0, fi)
                own = jnp.where(first, fi, fr)
                xr = spec_ref[i - lag, real, :] * weight
                xi = spec_ref[i - lag, imag, :] * weight
                total_real = total_real + (fr * xr - cross * xi)
                total_imag = total_imag + (cross * xr + own * xi)
            out_ref[i, real, :] = total_real.astype(BF)
            out_ref[i, imag, :] = total_imag.astype(BF)
        return carry

    lax.fori_loop(0, rows // step, chunk, 0)
    for block in range(blocks):
        y_ref[pl.ds(block * rows, rows), :] = jnp.dot(
            back_ref[...], out_ref[block], preferred_element_type=F32
        ).astype(BF)


def correlate_kernel(
    blocks, rows, step, same_ref, table_ref, back_ref, scale_ref, filt_ref, x_ref, g_ref,
    dx_ref, dt_ref, spec_ref, grad_ref, out_ref, tap_ref,
):
    spectra_rows(table_ref, x_ref, spec_ref, blocks, rows)
    spectra_rows(table_ref, g_ref, grad_ref, blocks, rows)

    def chunk(index, carry):
        real = pl.ds(pl.multiple_of(index * step, step), step)
        imag = pl.ds(pl.multiple_of(rows + index * step, step), step)
        width = x_ref.shape[1]
        first = (lax.broadcasted_iota(jnp.int32, (step, width), 0) + index * step) == 0
        for j in range(blocks):
            total_real = jnp.zeros((step, width), F32)
            total_imag = jnp.zeros((step, width), F32)
            for lag in range(blocks - j):
                weight = same_ref[j + lag, j]
                fr = filt_ref[lag, real, :]
                fi = filt_ref[lag, imag, :]
                cross = jnp.where(first, 0.0, fi)
                own = jnp.where(first, fi, fr)
                gr = grad_ref[j + lag, real, :] * weight
                gi = grad_ref[j + lag, imag, :] * weight
                total_real = total_real + (fr * gr + cross * gi)
                total_imag = total_imag + (own * gi - cross * gr)
            out_ref[j, real, :] = total_real.astype(BF)
            out_ref[j, imag, :] = total_imag.astype(BF)
        for lag in range(blocks):
            one = jnp.zeros((step, width), F32)
            two = jnp.zeros((step, width), F32)
            three = jnp.zeros((step, width), F32)
            for i in range(lag, blocks):
                weight = same_ref[i, i - lag]
                gr = grad_ref[i, real, :] * weight
                gi = grad_ref[i, imag, :] * weight
                xr = spec_ref[i - lag, real, :]
                xi = spec_ref[i - lag, imag, :]
                one = one + xr * gr
                two = two + xi * gi
                three = three + (xr * gi - xi * gr)
            tap_ref[lag, real, :] = (one + jnp.where(first, 0.0, two)) * scale_ref[real, 0:1]
            tap_ref[lag, imag, :] = jnp.where(first, two, three) * scale_ref[imag, 0:1]
        return carry

    lax.fori_loop(0, rows // step, chunk, 0)
    for block in range(blocks):
        where = pl.ds(block * rows, rows)
        dx_ref[where, :] = jnp.dot(back_ref[...], out_ref[block], preferred_element_type=F32).astype(BF)
        total = tap_ref[block]
        if block + 1 < blocks:
            total = total + scale_ref[:, 1:2] * tap_ref[block + 1]
        dt_ref[where, :] = jnp.dot(back_ref[...], total.astype(BF), preferred_element_type=F32)


VMEM_SPEC = pl.BlockSpec(memory_space=pltpu.VMEM)
SMEM_SPEC = pl.BlockSpec(memory_space=pltpu.SMEM)
KERNEL_BYTES = 48 * 1024 * 1024


def convolve(same, table, back, filt, x_cols, blocks, rows):
    width = x_cols.shape[1]
    return pl.pallas_call(
        functools.partial(convolve_kernel, blocks, rows, min(32, rows)),
        out_shape=jax.ShapeDtypeStruct(x_cols.shape, BF),
        in_specs=[SMEM_SPEC] + [VMEM_SPEC] * 4,
        out_specs=VMEM_SPEC,
        scratch_shapes=[
            pltpu.VMEM((blocks, 2 * rows, width), F32),
            pltpu.VMEM((blocks, 2 * rows, width), BF),
        ],
        compiler_params=pltpu.CompilerParams(vmem_limit_bytes=KERNEL_BYTES),
        name="convolve",
    )(same, table, back, filt, x_cols)


def correlate(same, table, back, scale, filt, x_cols, g_cols, blocks, rows):
    width = x_cols.shape[1]
    return pl.pallas_call(
        functools.partial(correlate_kernel, blocks, rows, min(32, rows)),
        out_shape=(
            jax.ShapeDtypeStruct(x_cols.shape, BF),
            jax.ShapeDtypeStruct(x_cols.shape, F32),
        ),
        in_specs=[SMEM_SPEC] + [VMEM_SPEC] * 6,
        out_specs=(VMEM_SPEC, VMEM_SPEC),
        scratch_shapes=[
            pltpu.VMEM((blocks, 2 * rows, width), F32),
            pltpu.VMEM((blocks, 2 * rows, width), F32),
            pltpu.VMEM((blocks, 2 * rows, width), BF),
            pltpu.VMEM((blocks, 2 * rows, width), F32),
        ],
        compiler_params=pltpu.CompilerParams(vmem_limit_bytes=KERNEL_BYTES),
        name="correlate",
    )(same, table, back, scale, filt, x_cols, g_cols)


def shifted(block, axis, distance):
    devices = range(lax.axis_size(axis))
    route = [(i - distance, i) for i in devices if i - distance in devices]
    return lax.ppermute(block, axis, route)


def swap(block, bit):
    return lax.ppermute(block, "seq", [(i, i ^ bit) for i in range(lax.axis_size("seq"))])


def core_swap(block):
    return lax.ppermute(block, "section", [(0, 1), (1, 0)])


MESH = pl.DeviceIdType.MESH


def shared_rows(rows):
    return rows // 48 * 16 if rows >= 96 else 0


def gather_kernel(sizes, count, *refs):
    total = len(sizes)
    own_refs, out_refs = refs[:total], refs[total : 2 * total]
    send, recv, local = refs[2 * total :]
    core, here, plane = lax.axis_index("section"), lax.axis_index("seq"), lax.axis_index("dp")
    by_x, by_y, far = here + 1 - 2 * (here % 2), (here + 2) % 4, 3 - here
    odd = plane % 2
    to_x, to_y = (core, by_x, plane), (core, by_y, plane)
    to_z, to_core = (core, here, plane + 1 - 2 * odd), (1 - core, here, plane)
    barrier = pltpu.get_barrier_semaphore()
    for target in (to_x, to_y, to_z, to_core):
        pl.semaphore_signal(barrier, inc=1, device_id=target, device_id_type=MESH)
    pl.semaphore_wait(barrier, 4)

    def window(m, block, start, length):
        first = (core * count + block) * sizes[m] + start
        return out_refs[m].at[pl.ds(pl.multiple_of(first, 16), length)]

    def copy(kind, m, source, target_ref, target):
        return pltpu.make_async_remote_copy(
            src_ref=source, dst_ref=target_ref, send_sem=send.at[kind, m], recv_sem=recv.at[kind, m],
            device_id=target, device_id_type=MESH,
        )

    def forward(kind, m, block, start, length, target):
        where = window(m, block, start, length)
        return copy(kind, m, where, where, target)

    started = []

    def go(item):
        item.start()
        started.append(item)
        return item

    def from_own(kind, m, start, length, target):
        source = own_refs[m].at[pl.ds(pl.multiple_of(start, 16), length)]
        return go(copy(kind, m, source, window(m, here, start, length), target))

    kept, thirds, lows, begins = [], [], [], []
    for m in range(total):
        third = shared_rows(sizes[m])
        thirds.append(third)
        begins.append(odd * third)
        lows.append(-(-(sizes[m] - third) // 32) * 16)
    direct, cross, side = {}, {}, {}

    def first_hop(m):
        length = sizes[m] - thirds[m]
        direct[m] = (
            from_own(0, m, begins[m], length, to_x), from_own(1, m, begins[m], length, to_y)
        )

    def given(m):
        return odd * (sizes[m] - thirds[m])

    def second_hop(m):
        length, low = sizes[m] - thirds[m], lows[m]
        direct[m][0].wait_recv()
        low_copy = go(forward(2, m, by_x, begins[m], low, to_y))
        if thirds[m]:
            side[m] = [go(forward(4, m, by_x, given(m), thirds[m], to_z))]
        kept.append(go(forward(7, m, by_x, begins[m], length, to_core)))
        direct[m][1].wait_recv()
        high_copy = go(forward(3, m, by_y, begins[m] + low, length - low, to_x))
        if thirds[m]:
            side[m].append(go(forward(5, m, by_y, given(m), thirds[m], to_z)))
        kept.append(go(forward(8, m, by_y, begins[m], length, to_core)))
        cross[m] = (low_copy, high_copy)

    def third_hop(m):
        length = sizes[m] - thirds[m]
        cross[m][0].wait_recv()
        cross[m][1].wait_recv()
        if thirds[m]:
            side[m].append(go(forward(6, m, far, given(m), thirds[m], to_z)))
        kept.append(go(forward(9, m, far, begins[m], length, to_core)))

    def last_hop(m):
        if thirds[m]:
            missing = (1 - odd) * (sizes[m] - thirds[m])
            for k, block in enumerate((by_x, by_y, far)):
                side[m][k].wait_recv()
                kept.append(go(forward(10 + k, m, block, missing, thirds[m], to_core)))

    first_hop(0)
    first_hop(1)
    locals_ = []
    for m in range(total):
        mine = pltpu.make_async_copy(own_refs[m], window(m, here, 0, sizes[m]), local.at[m])
        mine.start()
        locals_.append(mine)
    for m in range(total):
        second_hop(m)
        if m + 2 < total:
            first_hop(m + 2)
        kept.append(from_own(13, m, 0, sizes[m], to_core))
        if m >= 1:
            third_hop(m - 1)
        if m >= 2:
            last_hop(m - 2)
    third_hop(total - 1)
    for m in range(max(total - 2, 0), total):
        last_hop(m)
    for mine in locals_:
        mine.wait()
    for item in kept:
        item.wait_recv()
    for item in started:
        item.wait_send()


def gather_shards(shards):
    count = lax.axis_size("seq")
    core = lax.axis_index("section")
    if count != 4 or lax.axis_size("dp") % 2:
        result = []
        for shard in shards:
            whole = lax.all_gather(shard, "seq", axis=0, tiled=True)
            other = core_swap(whole)
            low = jnp.where(core == 0, whole, other)
            result.append(jnp.concatenate([low, jnp.where(core == 0, other, whole)], axis=0))
        return result
    sizes = [shard.shape[0] for shard in shards]
    return pl.pallas_call(
        functools.partial(gather_kernel, sizes, count),
        out_shape=[jax.ShapeDtypeStruct((2 * count * a.shape[0], a.shape[1]), a.dtype) for a in shards],
        in_specs=[pl.BlockSpec(memory_space=pl.ANY)] * len(shards),
        out_specs=[pl.BlockSpec(memory_space=pl.ANY)] * len(shards),
        scratch_shapes=[
            pltpu.SemaphoreType.DMA((14, len(shards))),
            pltpu.SemaphoreType.DMA((14, len(shards))),
            pltpu.SemaphoreType.DMA((len(shards),)),
        ],
        compiler_params=pltpu.CompilerParams(collective_id=0, has_side_effects=True),
        name="gather_shards",
    )(*shards)


def core_halves(core, values):
    width = values.shape[1] // 2
    return (
        lax.dynamic_slice_in_dim(values, core * width, width, 1),
        lax.dynamic_slice_in_dim(values, (1 - core) * width, width, 1),
    )


def blocks_by(values, order, axis=1):
    here = lax.axis_index("seq")
    width = values.shape[axis] // 4
    return jnp.concatenate(
        [lax.dynamic_slice_in_dim(values, (here ^ k) * width, width, axis) for k in order], axis=axis
    )


def tied(value, *before):
    for array in before:
        first = array[(0,) * array.ndim].astype(F32)
        value = value + jnp.where(jnp.isnan(first), first, 0.0)
    return value


X_FIRST = (0, 2, 1, 3)
Y_FIRST = (0, 1, 2, 3)


def chip_and_seq_sum(keep, sent, order):
    got = core_swap(sent)
    middle = sent.shape[0] // 2
    near_bit, far_bit = (2, 1) if order == X_FIRST else (1, 2)
    far = (keep(True) + got[middle:].astype(F32)).astype(BF)
    arrived = swap(far, far_bit)
    near = keep(False) + got[:middle].astype(F32) + arrived.astype(F32)
    last = swap(near[middle // 2 :].astype(BF), near_bit)
    return near[: middle // 2] + last.astype(F32), arrived, last


def product_reduce(left, keep, send, order):
    if lax.axis_size("seq") != 4:
        chip = dot_left(left, keep) + core_swap(dot_left(left, send).astype(BF)).astype(F32)
        summed = lax.psum_scatter(chip.astype(BF), "seq", scatter_dimension=0, tiled=True).astype(F32)
        return summed, summed, summed
    left = blocks_by(left, order)
    middle = left.shape[1] // 2

    def kept(far):
        return dot_left(left[:, middle:] if far else left[:, :middle], keep)

    return chip_and_seq_sum(kept, dot_left(left, send).astype(BF), order)


def array_reduce(values, core, order):
    count, rows, width = values.shape
    keep, send = core_halves(core, values.reshape(count * rows, width))
    if count != 4:
        chip = keep + core_swap(send.astype(BF)).astype(F32)
        summed = lax.psum_scatter(chip.astype(BF), "seq", scatter_dimension=0, tiled=True).astype(F32)
        return summed, summed, summed
    keep = blocks_by(keep, order, 0)
    middle = keep.shape[0] // 2
    sent = blocks_by(send, order, 0).astype(BF)
    return chip_and_seq_sum(lambda far: keep[middle:] if far else keep[:middle], sent, order)


def sum_planes(values):
    values = lax.optimization_barrier(values.astype(BF))
    if True:
        return lax.psum(values, "dp")
    place = lax.axis_index("dp")
    inward = lax.ppermute(values, "dp", [(0, 1), (3, 2)])
    pair = lax.optimization_barrier((values.astype(F32) + inward.astype(F32)).astype(BF))
    crossed = lax.ppermute(pair, "dp", [(1, 2), (2, 1)])
    total = lax.optimization_barrier((pair.astype(F32) + crossed.astype(F32)).astype(BF))
    outward = lax.ppermute(total, "dp", [(1, 0), (2, 3)])
    return jnp.where(jnp.logical_or(place == 0, place == 3), outward, total)


def body(
    tokens, out_grad, lengths, ln1_gain, w_in, short_w, filt_in, filt_shift, sine_freq, filt_out,
    decay, filter_bias, w_out, ln2_gain, mlp_up, mlp_down,
):
    micro, rows, width = tokens.shape
    count = lax.axis_size("seq")
    here = lax.axis_index("seq")
    core = lax.axis_index("section")
    slots = rows * count
    col_width = width // count
    hidden = mlp_up.shape[2]
    hidden_block = hidden // count
    half_block = hidden_block // 2
    table_np, weight_np, parity_np = packed_dft(rows)
    table = jnp.asarray(table_np).astype(BF)
    back = jnp.asarray(np.ascontiguousarray(table_np.T)).astype(BF)
    scale = jnp.asarray(np.concatenate([weight_np, parity_np], axis=1))
    embedding = jnp.asarray(positions_embedding(slots, FREQS))

    small = (ln1_gain, short_w, filt_in, filt_shift, sine_freq, filt_out, decay, filter_bias, ln2_gain)
    small_shapes = [a.shape[1:] for a in small]
    small_sizes = [math.prod(s) for s in small_shapes]
    lane = 1024
    packed_rows = -(-sum(small_sizes) // (lane * 16)) * 16
    flat = jnp.concatenate([a.reshape(-1) for a in small])
    flat = jnp.pad(flat, (0, packed_rows * lane - flat.shape[0])).reshape(packed_rows, lane)
    flat_all, out_all, in_all, up_all, down_all = gather_shards([flat, w_out[0], w_in[0], mlp_up[0], mlp_down[0]])
    everywhere = flat_all.reshape(2, count, packed_rows * lane)
    gathered = [
        (
            in_all[layer * width : (layer + 1) * width], out_all[layer * width : (layer + 1) * width],
            up_all[layer * width : (layer + 1) * width], down_all[layer * hidden : (layer + 1) * hidden],
        )
        for layer in range(2)
    ]
    small_axis = (0, 1, 1, 0, 0, 0, 0, 0, 0)

    def small_of(layer):
        found = []
        offset = 0
        for shape, size, axis in zip(small_shapes, small_sizes, small_axis):
            part = everywhere[layer, :, offset : offset + size].reshape((count,) + shape)
            part = jnp.moveaxis(part, 0, axis)
            full = list(shape)
            full[axis] = shape[axis] * count
            found.append(part.reshape(full).astype(F32))
            offset += size
        return found

    length_row = lax.dynamic_index_in_dim(lengths, core, 0, keepdims=False)
    index_all = jnp.arange(count, dtype=jnp.int32)
    started = jnp.logical_and(length_row[None, :] > 0, index_all[None, :] <= index_all[:, None])
    regions = jnp.max(jnp.where(started, index_all[None, :], 0), axis=1)
    doc_length = jnp.sum(jnp.where(regions[:, None] == index_all[None, :], length_row[None, :], 0), axis=1)
    own_region = jnp.sum(jnp.where(index_all == here, regions, 0))
    own_length = jnp.sum(jnp.where(index_all == here, doc_length, 0))
    last_region = jnp.sum(jnp.where(index_all == here - 1, regions, 0))
    offsets = (here - own_region) * rows + jnp.arange(rows, dtype=jnp.int32)
    valid = (offsets < own_length).astype(F32)[:, None]
    carried_on = jnp.logical_and(here > 0, last_region == own_region).astype(F32)
    same = (regions[:, None] == regions[None, :]).astype(F32)

    def to_columns(values):
        return lax.all_to_all(values.astype(BF), "seq", split_axis=1, concat_axis=0, tiled=True)

    def to_rows(values):
        return lax.all_to_all(values, "seq", split_axis=0, concat_axis=1, tiled=True).astype(F32)

    def filter_stage(layer):
        _, _, in_w, shift_w, freq_w, out_w, decay_w, _, _ = small_of(layer)
        out_cols = lax.dynamic_slice_in_dim(out_w, here * col_width, col_width, 1)
        decay_cols = lax.dynamic_slice_in_dim(decay_w, here * col_width, col_width, 0)
        taps, pull = jax.vjp(
            lambda *p: filter_taps(*p, embedding), in_w, shift_w, freq_w, out_cols, decay_cols
        )
        spectra = jnp.einsum(
            "fs,msc->mfc", table, taps.astype(BF).reshape(count, rows, col_width), preferred_element_type=F32
        )
        before = jnp.concatenate([jnp.zeros_like(spectra[:1]), spectra[:-1]], axis=0)
        return (spectra + scale[:, 1:2] * before) * scale[:, 0:1], pull

    def forward(layer_in, layer):
        gain_one, short_weights, _, _, _, _, _, bias, gain_two = small_of(layer)
        in_matrix, out_matrix, up_matrix, down_matrix = gathered[layer]
        filt, pull = filter_stage(layer)
        normed = layer_norm(layer_in, gain_one).astype(BF)
        projected = dot(normed, in_matrix).astype(BF)
        rim = shifted(projected[rows - 2 :], "seq", 1)
        mixed = short_mix(rim.astype(F32), projected.astype(F32), short_weights, carried_on)
        first, second, third = mixed[:, :width], mixed[:, width : 2 * width], mixed[:, 2 * width :]
        signal = first * third
        x_cols = to_columns(signal * valid)
        y_cols = convolve(same, table, back, filt, x_cols, count, rows)
        filtered = to_rows(y_cols) * valid + bias * signal
        gated = (second * filtered).astype(BF)
        residual = layer_in + dot(gated, out_matrix)
        normed_two = layer_norm(residual, gain_two).astype(BF)
        upward = dot(normed_two, up_matrix)
        active = gelu_tanh(upward).astype(BF)
        layer_out = residual + dot(active, down_matrix)
        stored = (
            layer_in, normed, projected, rim, mixed, signal, filtered, gated, residual, normed_two,
            upward, active, x_cols, filt, pull,
        )
        return layer_out.astype(BF), stored

    def backward(upstream, stored, layer, before):
        (
            layer_in, normed, projected, rim, mixed, signal, filtered, gated, residual, normed_two,
            upward, active, x_cols, filt, pull,
        ) = stored
        gain_one, short_weights, in_w, shift_w, freq_w, out_w, decay_w, bias, gain_two = small_of(layer)
        in_matrix, out_matrix, up_matrix, down_matrix = gathered[layer]
        upstream_keep, upstream_send = core_halves(core, upstream)
        grad_hidden = jax.vjp(gelu_tanh, upward)[1](dot_right(upstream, down_matrix))[0].astype(BF)
        hidden_keep, hidden_send = core_halves(core, grad_hidden)
        grad_down = product_reduce(active, upstream_keep, upstream_send, Y_FIRST)
        grad_up = product_reduce(normed_two, hidden_keep, hidden_send, X_FIRST)
        grad_norm_two = dot_right(grad_hidden, up_matrix)
        grad_resid_norm, grad_gain_two = jax.vjp(layer_norm, residual, gain_two)[1](grad_norm_two)
        grad_residual = upstream.astype(F32) + grad_resid_norm
        grad_branch = tied(grad_residual, *before[0]).astype(BF)
        branch_keep, branch_send = core_halves(core, grad_branch)
        grad_out = product_reduce(gated, branch_keep, branch_send, X_FIRST)
        grad_gated = dot_right(grad_branch, out_matrix)
        first, second, third = mixed[:, :width], mixed[:, width : 2 * width], mixed[:, 2 * width :]
        grad_second = grad_gated * filtered
        grad_filtered = grad_gated * second
        grad_bias = jnp.sum(grad_filtered * signal, axis=0)
        g_cols = to_columns(grad_filtered * valid)
        dx_cols, grad_taps = correlate(same, table, back, scale, filt, x_cols, g_cols, count, rows)
        grad_signal = to_rows(dx_cols) * valid + bias * grad_filtered
        grad_mixed = jnp.concatenate([grad_signal * third, grad_second, grad_signal * first], axis=1)
        short_pull = jax.vjp(
            lambda a, b, c: short_mix(a, b, c, carried_on), rim.astype(F32), projected.astype(F32), short_weights
        )[1]
        grad_rim, grad_proj, grad_short = short_pull(grad_mixed)
        returned = shifted(grad_rim, "seq", -1)
        tail = grad_proj[rows - 2 :] + returned
        grad_proj = jnp.concatenate([grad_proj[: rows - 2], tail], axis=0)
        grad_proj = tied(grad_proj, *before[1]).astype(BF)
        proj_keep, proj_send = core_halves(core, grad_proj)
        half = proj_keep.shape[1] // 2
        grad_in_low = product_reduce(normed, proj_keep[:, :half], proj_send[:, :half], X_FIRST)
        grad_in_high = product_reduce(normed, proj_keep[:, half:], proj_send[:, half:], Y_FIRST)
        grad_normed = dot_right(grad_proj, in_matrix)
        grad_norm_in, grad_gain_one = jax.vjp(layer_norm, layer_in, gain_one)[1](grad_normed)
        grad_layer_in = grad_residual + grad_norm_in
        d_in, d_shift, d_freq, d_out_cols, d_decay_cols = pull(grad_taps)
        d_out = lax.dynamic_update_slice_in_dim(jnp.zeros_like(out_w), d_out_cols, here * col_width, 1)
        d_decay = lax.dynamic_update_slice_in_dim(jnp.zeros_like(decay_w), d_decay_cols, here * col_width, 0)
        small_grads = (
            grad_gain_one, grad_short, d_in, d_shift, d_freq, d_out, d_decay, grad_bias, grad_gain_two
        )
        parts = []
        for grad, shape, axis in zip(small_grads, small_shapes, small_axis):
            split = list(grad.shape)
            split[axis : axis + 1] = [count, shape[axis]]
            parts.append(jnp.moveaxis(grad.reshape(split), axis, 0).reshape(count, -1))
        packed = jnp.concatenate(parts, axis=1)
        packed = jnp.pad(packed, ((0, 0), (0, packed_rows * lane - packed.shape[1])))
        grad_small = array_reduce(packed.reshape(count, packed_rows, lane), core, Y_FIRST)
        return grad_layer_in, (grad_small, grad_in_low, grad_in_high, grad_out, grad_up, grad_down)

    def row_of(values):
        return lax.dynamic_index_in_dim(values, core, 0, keepdims=False)

    out_first, stored_first = forward(row_of(tokens).astype(F32), 0)
    out_second, stored_second = forward(out_first.astype(F32), 1)
    grad_second, sums_second = backward(row_of(out_grad), stored_second, 1, ((), ()))
    small_two, in_low_two, in_high_two, out_two, up_two, down_two = sums_second
    grad_second = tied(grad_second, up_two[1], down_two[1]).astype(BF)
    mlp_two = [lax.psum(part[0].astype(BF), "dp") for part in (up_two, down_two)]
    before = ((up_two[2], down_two[2], in_low_two[1], in_high_two[1]), tuple(mlp_two))
    grad_first, sums_first = backward(grad_second, stored_first, 0, before)
    grad_first = grad_first.astype(BF)
    summed = [[sum_planes(part[0]) for part in sums] for sums in (sums_first, sums_second)]
    summed[1][4:] = mlp_two

    def both_rows(of_first, of_second):
        kept = jnp.where(core == 0, of_first, of_second)
        received = core_swap(jnp.where(core == 0, of_second, of_first))
        return jnp.stack([jnp.where(core == 0, kept, received), jnp.where(core == 0, received, kept)])[None]

    layer_outputs = both_rows(out_first, out_second)
    input_grads = both_rows(grad_first, grad_second)

    def finish(index, join):
        whole = []
        for layer, sums in enumerate(summed):
            own = sums[index]
            received = lax.ppermute(own, "section", [(1 - layer, layer)])
            whole.append(join(own, received) if layer == 0 else join(received, own))
        return jnp.where(core == 0, whole[0], whole[1]).astype(F32)

    def side_by_side(low, high):
        return jnp.concatenate([low, high], axis=1)

    def finish_in():
        whole = []
        for layer, sums in enumerate(summed):
            own = jnp.concatenate(sums[1:3], axis=1)
            received = lax.ppermute(own, "section", [(1 - layer, layer)])
            whole.append(side_by_side(own, received) if layer == 0 else side_by_side(received, own))
        return jnp.where(core == 0, whole[0], whole[1]).astype(F32)

    small_total = finish(0, side_by_side).reshape(-1)
    grad_in = finish_in()
    grad_out = finish(3, side_by_side)
    grad_up = finish(4, side_by_side)
    grad_down = finish(5, side_by_side)
    small_out = []
    offset = 0
    for shape, size in zip(small_shapes, small_sizes):
        small_out.append(small_total[offset : offset + size].reshape((1,) + shape))
        offset += size
    g_ln1, g_short, g_fin, g_shift, g_freq, g_fout, g_decay, g_bias, g_ln2 = small_out
    return (
        layer_outputs, input_grads, g_ln1, grad_in[None], g_short, g_fin, g_shift, g_freq, g_fout, g_decay, g_bias,
        grad_out[None], g_ln2, grad_up[None], grad_down[None],
    )


def solution(mesh):
    vector = P("section", "seq")
    matrix = P("section", "seq", None)
    last = P("section", None, "seq")
    tokens = P("dp", "seq", None)
    outputs = P("section", "dp", "seq", None)
    in_specs = (
        tokens, tokens, P("dp", None), vector, matrix, last, last, vector, vector, matrix, vector, vector, matrix,
        vector, matrix, matrix,
    )
    out_specs = (
        outputs, outputs, vector, matrix, last, last, vector, vector, matrix, vector, vector, matrix, vector, matrix,
        matrix,
    )
    return jax.shard_map(body, mesh=mesh, in_specs=in_specs, out_specs=out_specs, check_vma=False)
```

time: 1860 us -> 1100 us (0.59)
  local copies, waits for them, and re-layouts: 476 us -> 113 us
  matrix products: 425 us -> 193 us
  Pallas kernels: 0 us -> 213 us
  waiting for transfers between devices: 476 us -> 310 us
  blocking collectives: 134 us -> 0 us
  other arithmetic: 250 us -> 124 us
  starting transfers between devices: 61.2 us -> 102 us
    dynamic_slice x108 -> x12, local copies, waits for them, and re-layouts: 248 us -> 12.7 us  [blocks_by(): lax.dynamic_slice_in_dim(values, (here ^ k) * width, width, axis)]
    dot_general x69 -> x58, matrix products: 425 us -> 193 us  [the longest x30 78.2 us: dot_left(): lax.dot_general(left, right, (((0,), (0,)), ((), ())), preferred_element_...]
    pallas_call x0 -> x5, Pallas kernels: none -> 213 us  [the longest x1 198 us: gather_shards(): pl.pallas_call(functools.partial(gather_kernel, sizes, count), out_shape=...]
    ppermute x0 -> x48, waiting for transfers between devices: none -> 153 us  [the longest x24 151 us: swap(): lax.ppermute(block, 'seq', [(i, i ^ bit) for i in range(lax.axis_size('se...]
    reduce_scatter x5 -> x0, waiting for transfers between devices: 102 us -> none  [the longest x1 77.1 us: body(): lax.psum_scatter(full_grads[12].astype(jnp.bfloat16), 'seq', scatter_dime...]
    unnamed x20 -> x3, waiting for transfers between devices: 101 us -> 0.05 us
    reduce_sum x44 -> x4, other arithmetic: 87.9 us -> 2.62 us  [the longest x1 1.17 us: filter_taps(): return summed * jnp.exp(-decay[None, :] * scaled[:, None])]
    all_gather x7 -> x0, blocking collectives: 64.9 us -> none  [the longest x1 13.7 us: body(): lax.all_gather(filter_bias, 'seq', axis=1, tiled=True)]
  transfers between devices with their start and end apart: 35 -> 63, of which waited for: 21 -> 20; matrix products, arithmetic and copies ran while one was open for 30% -> 27% of each run, Pallas kernels for 0% -> 1%
where the time goes in v1:
time: 1100 us; the launch traced here: 1090 us
  waiting for transfers between devices  310 us (28%)
  Pallas kernels  213 us (19%)
  matrix products  193 us (18%)
  other arithmetic  124 us (11%)
  local copies, waits for them, and re-layouts  113 us (10%)
  starting transfers between devices  102 us (9%)
  between operations  35.2 us (3%)
    pallas_call x1, Pallas kernels, gather_shards(): pl.pallas_call(functools.partial(gather_kernel, sizes, count), out_shape=...  198 us
    ppermute x24, waiting for transfers between devices, swap(): lax.ppermute(block, 'seq', [(i, i ^ bit) for i in range(lax.axis_size('se...  151 us
    psum x2, waiting for transfers between devices, sum_planes(): return lax.psum(values, 'dp')  133 us
    dot_general x30, matrix products, dot_left(): lax.dot_general(left, right, (((0,), (0,)), ((), ())), preferred_element_...  78.2 us
    dot_general x8, matrix products, dot_right(): lax.dot_general(left, right, (((1,), (1,)), ((), ())), preferred_element_...  50.9 us
    unnamed x500, local copies, waits for them, and re-layouts  40 us
    dot_general x8, matrix products, dot(): return jnp.dot(left, right, preferred_element_type=F32)  38.8 us
    ppermute x24, starting transfers between devices, swap(): lax.ppermute(block, 'seq', [(i, i ^ bit) for i in range(lax.axis_size('se...  32.1 us
  transfers between devices with their start and end apart: 63, of which 20 were waited for; matrix products, arithmetic and copies ran while one was open for 27% of the time, Pallas kernels for 1%

profile of v1, /device:TPU:0, one launch (start us, length us, event | category | flops | bytes accessed | tf_op | source)
XLA Modules:
  0.0 1089.8 jit_solution(7455610178951432950)
XLA Ops:
  17.0 198.1 %gather_shards.1 = (bf16[256,1024]{1,0:T(8,128)(2,1)}, bf16[2048,1024]{1,0:T(8,128)(2,1)}, bf16[2048,3072]{1,0:T(8,128)(2,1)}, bf16[2048,4096]{1,0:T(8,128)(2,1)}, bf16[8192,1024]{1,0:T(8,128)(2,1)}) custom-call(bf16[32,1024]{1,0:T(8,128)(2,1)} %reshape.768.refs_0_, bf16[256,1024]{1,0:T(8,128)(2,1)} %bitcast.286, bf16[256,3072]{1,0:T(8,128)(2,1)} %bitcast.281, ...), custom_call_target="tpu_custom_call" | custom-call | tf_op jit(solution)/shard_map/gather_shards/pallas_call | solution.py:364
  217.3 6.5 fusion.421
  250.7 3.7 all-to-all-start
  254.4 5.0 add_multiply_fusion
  265.3 4.1 all-to-all-start.1
  269.5 6.9 all-to-all-done.1
  282.5 8.9 multiply_convert_fusion.1
  294.6 6.5 fusion.423
  307.1 5.2 multiply_add_fusion
  315.9 5.0 all-to-all-start.2
  332.7 4.1 all-to-all-start.3
  349.8 5.7 multiply_convert_fusion
  358.2 7.0 fusion.37
  365.3 8.2 multiply_reduce_fusion.6
  380.3 4.3 multiply_reduce_fusion.7
  394.4 4.8 convolution_convert_fusion.3
  399.8 4.4 convolution_convert_fusion.1
  411.9 4.2 correlate.2
  422.8 4.2 all-to-all-start.5
  427.0 4.0 multiply_reduce_fusion.16
  462.0 4.9 fusion.121
  476.5 3.8 add_convert_fusion.3
  486.4 3.9 add_convert_fusion.2
  493.8 10.4 collective-permute-done.11
  513.9 41.6 %collective-permute-done.40 = bf16[256,512]{1,0:T(8,128)(2,1)S(1)} collective-permute-done((bf16[256,512]{1,0:T(8,128)(2,1)S(1)}, bf16[256,512]{1,0:T(8,128)(2,1)S(1)}, u32[]{:S(2)}, u32[]{:S(2)}) %collective-permute-start.40) | collective-permute-done | bytes 262176 | tf_op jit(solution)/shard_map/ppermute | solution.py:226
  584.5 8.1 fusion.30
  592.7 8.1 multiply_reduce_fusion.9
  601.4 3.7 convert_add_fusion.2
  625.7 5.9 collective-permute-done.9
  637.1 5.5 multiply_reduce_fusion.10
  646.2 4.1 all-to-all-start.6
  664.4 5.7 correlate.3
  670.2 4.2 multiply_reduce_fusion.17
  679.0 4.1 all-to-all-start.7
  688.6 4.6 collective-permute-done.21
  717.6 4.2 slice.654
  721.8 7.2 collective-permute-done.35
  731.1 5.8 collective-permute-done.36
  737.7 10.2 all-reduce.28.cloned.1.call-done
  758.5 4.7 fusion.119
  779.0 3.7 add_convert_fusion
  792.3 50.6 %collective-permute-done.18 = bf16[32,512]{1,0:T(8,128)(2,1)S(1)} collective-permute-done((bf16[32,512]{1,0:T(8,128)(2,1)S(1)}, bf16[32,512]{1,0:T(8,128)(2,1)S(1)}, u32[]{:S(2)}, u32[]{:S(2)}) %collective-permute-start.18) | collective-permute-done | bytes 32800 | tf_op jit(solution)/shard_map/ppermute | solution.py:226
  865.2 19.5 %collective-permute-done.44 = bf16[256,2048]{1,0:T(8,128)(2,1)S(1)} collective-permute-done((bf16[256,2048]{1,0:T(8,128)(2,1)S(1)}, bf16[256,2048]{1,0:T(8,128)(2,1)S(1)}, u32[]{:S(2)}, u32[]{:S(2)}) %collective-permute-start.44) | collective-permute-done | bytes 1048608 | tf_op jit(solution)/shard_map/ppermute | solution.py:226
  888.7 7.2 broadcast_select_fusion.2
  909.9 132.7 %all-reduce.26.cloned.1.call-done = (bf16[256,768]{1,0:T(8,128)(2,1)}, bf16[256,768]{1,0:T(8,128)(2,1)}, bf16[256,768]{1,0:T(8,128)(2,1)}, bf16[256,768]{1,0:T(8...) async-done(((bf16[256,768]{1,0:T(8,128)(2,1)}, bf16[256,768]{1,0:T(8,128)(2,1)}, ...) | async-done | bytes 4194320 | tf_op jit(solution)/shard_map/psum | solution.py:447
  1046.0 4.6 collective-permute-start.33
  1059.6 5.0 collective-permute-start.41
  1075.3 4.9 fusion.63
  (876 shorter events, 374.8 us)
Async XLA Ops:
  225.0 21.0 %collective-permute-start = (bf16[2,3072]{1,0:T(2,128)(2,1)S(1)}, bf16[2,3072]{1,0:T(2,128)(2,1)S(1)}, u32[]{:S(2)}, u32[]{:S(2)}) collective-permute-start(bf16[2,3072]{1,0:T(2,128)(2,1)S(1)} %slice.601), channel_id=1, source_target_pairs={{0,4},{4,8},{8,12},{1,5},{5,9},{9,13},{2,6},{6,10},{10,14},{3,7},{... | collective-permute-start | bytes 36872 | tf_op jit(solution)/shard_map/ppermute | solution.py:222
  388.2 17.4 %all-to-all-start.4 = ((bf16[256,4,256]{2,0,1:T(8,128)(2,1)}), bf16[256,4,256]{2,0,1:T(8,128)(2,1)S(1)}, u32[]{:S(2)}, u32[]{:S(2)}) async-start(bf16[256,4,256]{2,0,1:T(8,128)(2,1)} %bitcast.270), calls=%async_computation.4 | async-start | bytes 1048576 | tf_op jit(solution)/shard_map/all_to_all | solution.py:520
  394.4 76.4 %collective-permute-start.38 = (bf16[1024,512]{1,0:T(8,128)(2,1)}, bf16[1024,512]{1,0:T(8,128)(2,1)}, u32[]{:S(2)}, u32[]{:S(2)}) collective-permute-start(bf16[1024,512]{1,0:T(8,128)(2,1)} %convolution_convert_fusion.8), channel_id=1, source_target_pairs={{0,16},{16,0},{1,17},{17,1},{2,18},{18,2},{3,19},{19,3},{4,20},{20... | collective-permute-start | bytes 3145736 | tf_op jit(solution)/shard_map/ppermute | solution.py:230
  399.3 77.2 %collective-permute-start.4 = (bf16[1024,2048]{1,0:T(8,128)(2,1)}, bf16[1024,2048]{1,0:T(8,128)(2,1)}, u32[]{:S(2)}, u32[]{:S(2)}) collective-permute-start(bf16[1024,2048]{1,0:T(8,128)(2,1)} %convolution_convert_fusion.3), channel_id=1, source_target_pairs={{0,16},{16,0},{1,17},{17,1},{2,18},{18,2},{3,19},{19,3},{4,20},{20... | collective-permute-start | bytes 12582920 | tf_op jit(solution)/shard_map/ppermute | solution.py:230
  404.2 82.2 %collective-permute-start.6 = (bf16[4096,512]{1,0:T(8,128)(2,1)}, bf16[4096,512]{1,0:T(8,128)(2,1)}, u32[]{:S(2)}, u32[]{:S(2)}) collective-permute-start(bf16[4096,512]{1,0:T(8,128)(2,1)} %convolution_convert_fusion.1), channel_id=1, source_target_pairs={{0,16},{16,0},{1,17},{17,1},{2,18},{18,2},{3,19},{19,3},{4,20},{20... | collective-permute-start | bytes 12582920 | tf_op jit(solution)/shard_map/ppermute | solution.py:230
  422.8 16.1 %all-to-all-start.5 = ((bf16[4,256,256]{2,1,0:T(8,128)(2,1)}), bf16[4,256,256]{2,1,0:T(8,128)(2,1)}, u32[]{:S(2)}, u32[]{:S(2)}) async-start(bf16[4,256,256]{2,1,0:T(8,128)(2,1)} %bitcast.259), calls=%async_computation.5 | async-start | bytes 1048576 | tf_op jit(solution)/shard_map/all_to_all | solution.py:523
  459.8 14.8 %collective-permute-start.10 = (bf16[1024,768]{1,0:T(8,128)(2,1)}, bf16[1024,768]{1,0:T(8,128)(2,1)}, u32[]{:S(2)}, u32[]{:S(2)}) collective-permute-start(bf16[1024,768]{1,0:T(8,128)(2,1)} %convolution_convert_fusion.7), channel_id=1, source_target_pairs={{0,16},{16,0},{1,17},{17,1},{2,18},{18,2},{3,19},{19,3},{4,20},{20... | collective-permute-start | bytes 4718600 | tf_op jit(solution)/shard_map/ppermute | solution.py:230
  462.0 20.2 %collective-permute-start.12 = (bf16[1024,768]{1,0:T(8,128)(2,1)}, bf16[1024,768]{1,0:T(8,128)(2,1)}, u32[]{:S(2)}, u32[]{:S(2)}) collective-permute-start(bf16[1024,768]{1,0:T(8,128)(2,1)} %convolution_convert_fusion.6), channel_id=1, source_target_pairs={{0,16},{16,0},{1,17},{17,1},{2,18},{18,2},{3,19},{19,3},{4,20},{20... | collective-permute-start | bytes 4718600 | tf_op jit(solution)/shard_map/ppermute | solution.py:230
  472.4 18.1 %collective-permute-start.39 = (bf16[512,512]{1,0:T(8,128)(2,1)S(1)}, bf16[512,512]{1,0:T(8,128)(2,1)S(1)}, u32[]{:S(2)}, u32[]{:S(2)}) collective-permute-start(bf16[512,512]{1,0:T(8,128)(2,1)S(1)} %add_convert_fusion.8), channel_id=1, source_target_pairs={{0,4},{4,0},{8,12},{12,8},{1,5},{5,1},{9,13},{13,9},{2,6},{6,2},{1... | collective-permute-start | bytes 1572872 | tf_op jit(solution)/shard_map/ppermute | solution.py:226
  476.4 27.8 %collective-permute-start.11 = (bf16[512,768]{1,0:T(8,128)(2,1)S(1)}, bf16[512,768]{1,0:T(8,128)(2,1)S(1)}, u32[]{:S(2)}, u32[]{:S(2)}) collective-permute-start(bf16[512,768]{1,0:T(8,128)(2,1)S(1)} %add_convert_fusion.7), channel_id=1, source_target_pairs={{0,4},{4,0},{8,12},{12,8},{1,5},{5,1},{9,13},{13,9},{2,6},{6,2},{1... | collective-permute-start | bytes 2359304 | tf_op jit(solution)/shard_map/ppermute | solution.py:226
  480.3 86.3 %collective-permute-start.5 = (bf16[512,2048]{1,0:T(8,128)(2,1)}, bf16[512,2048]{1,0:T(8,128)(2,1)}, u32[]{:S(2)}, u32[]{:S(2)}) collective-permute-start(bf16[512,2048]{1,0:T(8,128)(2,1)} %add_convert_fusion.3), channel_id=1, source_target_pairs={{0,4},{4,0},{8,12},{12,8},{1,5},{5,1},{9,13},{13,9},{2,6},{6,2},{1... | collective-permute-start | bytes 6291464 | tf_op jit(solution)/shard_map/ppermute | solution.py:226
  483.8 26.3 %collective-permute-start.13 = (bf16[512,768]{1,0:T(8,128)(2,1)S(1)}, bf16[512,768]{1,0:T(8,128)(2,1)S(1)}, u32[]{:S(2)}, u32[]{:S(2)}) collective-permute-start(bf16[512,768]{1,0:T(8,128)(2,1)S(1)} %add_convert_fusion.6), channel_id=1, source_target_pairs={{0,8},{4,12},{8,0},{12,4},{1,9},{5,13},{9,1},{13,5},{2,10},{6,14},... | collective-permute-start | bytes 2359304 | tf_op jit(solution)/shard_map/ppermute | solution.py:226
  490.4 87.1 %collective-permute-start.7 = (bf16[2048,512]{1,0:T(8,128)(2,1)}, bf16[2048,512]{1,0:T(8,128)(2,1)}, u32[]{:S(2)}, u32[]{:S(2)}) collective-permute-start(bf16[2048,512]{1,0:T(8,128)(2,1)} %add_convert_fusion.2), channel_id=1, source_target_pairs={{0,8},{4,12},{8,0},{12,4},{1,9},{5,13},{9,1},{13,5},{2,10},{6,14},... | collective-permute-start | bytes 6291464 | tf_op jit(solution)/shard_map/ppermute | solution.py:226
  491.8 63.7 %collective-permute-start.40 = (bf16[256,512]{1,0:T(8,128)(2,1)S(1)}, bf16[256,512]{1,0:T(8,128)(2,1)S(1)}, u32[]{:S(2)}, u32[]{:S(2)}) collective-permute-start(bf16[256,512]{1,0:T(8,128)(2,1)S(1)} %slice.914), channel_id=1, source_target_pairs={{0,8},{4,12},{8,0},{12,4},{1,9},{5,13},{9,1},{13,5},{2,10},{6,14},... | collective-permute-start | bytes 786440 | tf_op jit(solution)/shard_map/ppermute | solution.py:226
  506.6 55.9 %collective-permute-start.31 = (bf16[256,768]{1,0:T(8,128)(2,1)}, bf16[256,768]{1,0:T(8,128)(2,1)}, u32[]{:S(2)}, u32[]{:S(2)}) collective-permute-start(bf16[256,768]{1,0:T(8,128)(2,1)} %slice.911), channel_id=1, source_target_pairs={{0,8},{4,12},{8,0},{12,4},{1,9},{5,13},{9,1},{13,5},{2,10},{6,14},... | collective-permute-start | bytes 1179656 | tf_op jit(solution)/shard_map/ppermute | solution.py:226
  512.7 51.9 %collective-permute-start.32 = (bf16[256,768]{1,0:T(8,128)(2,1)}, bf16[256,768]{1,0:T(8,128)(2,1)}, u32[]{:S(2)}, u32[]{:S(2)}) collective-permute-start(bf16[256,768]{1,0:T(8,128)(2,1)} %slice.910), channel_id=1, source_target_pairs={{0,4},{4,0},{8,12},{12,8},{1,5},{5,1},{9,13},{13,9},{2,6},{6,2},{1... | collective-permute-start | bytes 1179656 | tf_op jit(solution)/shard_map/ppermute | solution.py:226
  575.7 47.6 %collective-permute-start.8 = (bf16[256,2048]{1,0:T(8,128)(2,1)}, bf16[256,2048]{1,0:T(8,128)(2,1)}, u32[]{:S(2)}, u32[]{:S(2)}) collective-permute-start(bf16[256,2048]{1,0:T(8,128)(2,1)} %slice.909), channel_id=1, source_target_pairs={{0,8},{4,12},{8,0},{12,4},{1,9},{5,13},{9,1},{13,5},{2,10},{6,14},... | collective-permute-start | bytes 3145736 | tf_op jit(solution)/shard_map/ppermute | solution.py:226
  608.3 23.4 %collective-permute-start.9 = (bf16[1024,512]{1,0:T(8,128)(2,1)}, bf16[1024,512]{1,0:T(8,128)(2,1)}, u32[]{:S(2)}, u32[]{:S(2)}) collective-permute-start(bf16[1024,512]{1,0:T(8,128)(2,1)} %slice.908), channel_id=1, source_target_pairs={{0,4},{4,0},{8,12},{12,8},{1,5},{5,1},{9,13},{13,9},{2,6},{6,2},{1... | collective-permute-start | bytes 3145736 | tf_op jit(solution)/shard_map/ppermute | solution.py:226
  612.5 161.3 %collective-permute-start.42 = (bf16[1024,2048]{1,0:T(8,128)(2,1)}, bf16[1024,2048]{1,0:T(8,128)(2,1)}, u32[]{:S(2)}, u32[]{:S(2)}) collective-permute-start(bf16[1024,2048]{1,0:T(8,128)(2,1)} %convolution_convert_fusion.2), channel_id=1, source_target_pairs={{0,16},{16,0},{1,17},{17,1},{2,18},{18,2},{3,19},{19,3},{4,20},{20... | collective-permute-start | bytes 12582920 | tf_op jit(solution)/shard_map/ppermute | solution.py:230
  618.5 160.5 %collective-permute-start.47 = (bf16[4096,512]{1,0:T(8,128)(2,1)}, bf16[4096,512]{1,0:T(8,128)(2,1)}, u32[]{:S(2)}, u32[]{:S(2)}) collective-permute-start(bf16[4096,512]{1,0:T(8,128)(2,1)} %convolution_convert_fusion), channel_id=1, source_target_pairs={{0,16},{16,0},{1,17},{17,1},{2,18},{18,2},{3,19},{19,3},{4,20},{20... | collective-permute-start | bytes 12582920 | tf_op jit(solution)/shard_map/ppermute | solution.py:230
  646.2 15.2 %all-to-all-start.6 = ((bf16[256,4,256]{2,0,1:T(8,128)(2,1)}), bf16[256,4,256]{2,0,1:T(8,128)(2,1)}, u32[]{:S(2)}, u32[]{:S(2)}) async-start(bf16[256,4,256]{2,0,1:T(8,128)(2,1)} %bitcast.269), calls=%async_computation.6 | async-start | bytes 1048576 | tf_op jit(solution)/shard_map/all_to_all | solution.py:520
  650.3 97.6 %all-reduce.28.cloned.1.call-start = ((), (), s32[]{:S(2)}) async-start(), calls=%async_computation.10 | async-start | bytes 4194304 | tf_op jit(solution)/shard_map/psum | solution.py:629
  653.3 59.3 %collective-permute-start.34 = (bf16[1024,512]{1,0:T(8,128)(2,1)}, bf16[1024,512]{1,0:T(8,128)(2,1)}, u32[]{:S(2)}, u32[]{:S(2)}) collective-permute-start(bf16[1024,512]{1,0:T(8,128)(2,1)} %convolution_convert_fusion.9), channel_id=1, source_target_pairs={{0,16},{16,0},{1,17},{17,1},{2,18},{18,2},{3,19},{19,3},{4,20},{20... | collective-permute-start | bytes 3145736 | tf_op jit(solution)/shard_map/ppermute | solution.py:230
  679.0 23.8 %all-to-all-start.7 = ((bf16[4,256,256]{2,1,0:T(8,128)(2,1)}), bf16[4,256,256]{2,1,0:T(8,128)(2,1)}, u32[]{:S(2)}, u32[]{:S(2)}) async-start(bf16[4,256,256]{2,1,0:T(8,128)(2,1)} %bitcast.54), calls=%async_computation.7 | async-start | bytes 1048576 | tf_op jit(solution)/shard_map/all_to_all | solution.py:523
  683.1 218.9 %all-reduce.24.cloned.1.call-start = ((), (), s32[]{:S(2)}) async-start(), calls=%async_computation.8 | async-start | bytes 131072 | tf_op jit(solution)/shard_map/psum | solution.py:447
  715.2 13.7 %collective-permute-start.35 = (bf16[512,512]{1,0:T(8,128)(2,1)}, bf16[512,512]{1,0:T(8,128)(2,1)}, u32[]{:S(2)}, u32[]{:S(2)}) collective-permute-start(bf16[512,512]{1,0:T(8,128)(2,1)} %add_convert_fusion.9), channel_id=1, source_target_pairs={{0,4},{4,0},{8,12},{12,8},{1,5},{5,1},{9,13},{13,9},{2,6},{6,2},{1... | collective-permute-start | bytes 1572872 | tf_op jit(solution)/shard_map/ppermute | solution.py:226
  716.0 15.1 %collective-permute-start.14 = (f32[2,3072]{1,0:T(2,128)S(1)}, f32[2,3072]{1,0:T(2,128)S(1)}, u32[]{:S(2)}, u32[]{:S(2)}) collective-permute-start(f32[2,3072]{1,0:T(2,128)S(1)} %add_multiply_fusion.2), channel_id=1, source_target_pairs={{4,0},{8,4},{12,8},{5,1},{9,5},{13,9},{6,2},{10,6},{14,10},{7,3},{... | collective-permute-start | bytes 73736 | tf_op jit(solution)/shard_map/ppermute | solution.py:222
  758.4 24.8 %collective-permute-start.27 = (bf16[1024,768]{1,0:T(8,128)(2,1)}, bf16[1024,768]{1,0:T(8,128)(2,1)}, u32[]{:S(2)}, u32[]{:S(2)}) collective-permute-start(bf16[1024,768]{1,0:T(8,128)(2,1)} %convolution_convert_fusion.4), channel_id=1, source_target_pairs={{0,16},{16,0},{1,17},{17,1},{2,18},{18,2},{3,19},{19,3},{4,20},{20... | collective-permute-start | bytes 4718600 | tf_op jit(solution)/shard_map/ppermute | solution.py:230
  768.3 18.9 %collective-permute-start.24 = (bf16[1024,768]{1,0:T(8,128)(2,1)S(1)}, bf16[1024,768]{1,0:T(8,128)(2,1)S(1)}, u32[]{:S(2)}, u32[]{:S(2)}) collective-permute-start(bf16[1024,768]{1,0:T(8,128)(2,1)S(1)} %convolution_convert_fusion.5), channel_id=1, source_target_pairs={{0,16},{16,0},{1,17},{17,1},{2,18},{18,2},{3,19},{19,3},{4,20},{20... | collective-permute-start | bytes 4718600 | tf_op jit(solution)/shard_map/ppermute | solution.py:230
  772.1 17.1 %collective-permute-start.17 = (bf16[64,512]{1,0:T(8,128)(2,1)S(1)}, bf16[64,512]{1,0:T(8,128)(2,1)S(1)}, u32[]{:S(2)}, u32[]{:S(2)}) collective-permute-start(bf16[64,512]{1,0:T(8,128)(2,1)S(1)} %fusion.320), channel_id=1, source_target_pairs={{0,8},{4,12},{8,0},{12,4},{1,9},{5,13},{9,1},{13,5},{2,10},{6,14},... | collective-permute-start | bytes 196616 | tf_op jit(solution)/shard_map/ppermute | solution.py:226
  777.5 75.1 %collective-permute-start.43 = (bf16[512,2048]{1,0:T(8,128)(2,1)}, bf16[512,2048]{1,0:T(8,128)(2,1)}, u32[]{:S(2)}, u32[]{:S(2)}) collective-permute-start(bf16[512,2048]{1,0:T(8,128)(2,1)} %add_convert_fusion.1), channel_id=1, source_target_pairs={{0,4},{4,0},{8,12},{12,8},{1,5},{5,1},{9,13},{13,9},{2,6},{6,2},{1... | collective-permute-start | bytes 6291464 | tf_op jit(solution)/shard_map/ppermute | solution.py:226
  782.7 75.5 %collective-permute-start.48 = (bf16[2048,512]{1,0:T(8,128)(2,1)}, bf16[2048,512]{1,0:T(8,128)(2,1)}, u32[]{:S(2)}, u32[]{:S(2)}) collective-permute-start(bf16[2048,512]{1,0:T(8,128)(2,1)} %add_convert_fusion), channel_id=1, source_target_pairs={{0,8},{4,12},{8,0},{12,4},{1,9},{5,13},{9,1},{13,5},{2,10},{6,14},... | collective-permute-start | bytes 6291464 | tf_op jit(solution)/shard_map/ppermute | solution.py:226
  785.7 61.5 %collective-permute-start.28 = (bf16[512,768]{1,0:T(8,128)(2,1)}, bf16[512,768]{1,0:T(8,128)(2,1)}, u32[]{:S(2)}, u32[]{:S(2)}) collective-permute-start(bf16[512,768]{1,0:T(8,128)(2,1)} %add_convert_fusion.4), channel_id=1, source_target_pairs={{0,8},{4,12},{8,0},{12,4},{1,9},{5,13},{9,1},{13,5},{2,10},{6,14},... | collective-permute-start | bytes 2359304 | tf_op jit(solution)/shard_map/ppermute | solution.py:226
  788.6 61.6 %collective-permute-start.25 = (bf16[512,768]{1,0:T(8,128)(2,1)}, bf16[512,768]{1,0:T(8,128)(2,1)S(1)}, u32[]{:S(2)}, u32[]{:S(2)}) collective-permute-start(bf16[512,768]{1,0:T(8,128)(2,1)} %add_convert_fusion.5), channel_id=1, source_target_pairs={{0,4},{4,0},{8,12},{12,8},{1,5},{5,1},{9,13},{13,9},{2,6},{6,2},{1... | collective-permute-start | bytes 2359304 | tf_op jit(solution)/shard_map/ppermute | solution.py:226
  789.2 53.7 %collective-permute-start.18 = (bf16[32,512]{1,0:T(8,128)(2,1)S(1)}, bf16[32,512]{1,0:T(8,128)(2,1)S(1)}, u32[]{:S(2)}, u32[]{:S(2)}) collective-permute-start(bf16[32,512]{1,0:T(8,128)(2,1)S(1)} %slice.917), channel_id=1, source_target_pairs={{0,4},{4,0},{8,12},{12,8},{1,5},{5,1},{9,13},{13,9},{2,6},{6,2},{1... | collective-permute-start | bytes 98312 | tf_op jit(solution)/shard_map/ppermute | solution.py:226
  843.6 199.1 %all-reduce.26.cloned.1.call-start = ((), (), s32[]{:S(2)}) async-start(), calls=%async_computation.9 | async-start | bytes 8388608 | tf_op jit(solution)/shard_map/psum | solution.py:447
  849.3 13.1 %collective-permute-start.29 = (bf16[256,768]{1,0:T(8,128)(2,1)S(1)}, bf16[256,768]{1,0:T(8,128)(2,1)S(1)}, u32[]{:S(2)}, u32[]{:S(2)}) collective-permute-start(bf16[256,768]{1,0:T(8,128)(2,1)S(1)} %slice.912), channel_id=1, source_target_pairs={{0,4},{4,0},{8,12},{12,8},{1,5},{5,1},{9,13},{13,9},{2,6},{6,2},{1... | collective-permute-start | bytes 1179656 | tf_op jit(solution)/shard_map/ppermute | solution.py:226
  852.3 12.1 %collective-permute-start.26 = (bf16[256,768]{1,0:T(8,128)(2,1)S(1)}, bf16[256,768]{1,0:T(8,128)(2,1)S(1)}, u32[]{:S(2)}, u32[]{:S(2)}) collective-permute-start(bf16[256,768]{1,0:T(8,128)(2,1)S(1)} %slice.913), channel_id=1, source_target_pairs={{0,8},{4,12},{8,0},{12,4},{1,9},{5,13},{9,1},{13,5},{2,10},{6,14},... | collective-permute-start | bytes 1179656 | tf_op jit(solution)/shard_map/ppermute | solution.py:226
  856.4 28.3 %collective-permute-start.44 = (bf16[256,2048]{1,0:T(8,128)(2,1)S(1)}, bf16[256,2048]{1,0:T(8,128)(2,1)S(1)}, u32[]{:S(2)}, u32[]{:S(2)}) collective-permute-start(bf16[256,2048]{1,0:T(8,128)(2,1)S(1)} %slice.907), channel_id=1, source_target_pairs={{0,8},{4,12},{8,0},{12,4},{1,9},{5,13},{9,1},{13,5},{2,10},{6,14},... | collective-permute-start | bytes 3145736 | tf_op jit(solution)/shard_map/ppermute | solution.py:226
  861.5 24.5 %collective-permute-start.49 = (bf16[1024,512]{1,0:T(8,128)(2,1)S(1)}, bf16[1024,512]{1,0:T(8,128)(2,1)S(1)}, u32[]{:S(2)}, u32[]{:S(2)}) collective-permute-start(bf16[1024,512]{1,0:T(8,128)(2,1)S(1)} %slice.906), channel_id=1, source_target_pairs={{0,4},{4,0},{8,12},{12,8},{1,5},{5,1},{9,13},{13,9},{2,6},{6,2},{1... | collective-permute-start | bytes 3145736 | tf_op jit(solution)/shard_map/ppermute | solution.py:226
  899.0 176.3 %collective-permute-start.46 = (bf16[256,2048]{1,0:T(8,128)(2,1)}, bf16[256,2048]{1,0:T(8,128)(2,1)}, u32[]{:S(2)}, u32[]{:S(2)}) collective-permute-start(bf16[256,2048]{1,0:T(8,128)(2,1)} %get-tuple-element.81), channel_id=1, source_target_pairs={{0,16},{1,17},{2,18},{3,19},{4,20},{5,21},{6,22},{7,23},{8,24},{9,... | collective-permute-start | bytes 3145736 | tf_op jit(solution)/shard_map/ppermute | solution.py:648
  909.2 144.9 %collective-permute-start.15 = (bf16[256,1024]{1,0:T(8,128)(2,1)}, bf16[256,1024]{1,0:T(8,128)(2,1)}, u32[]{:S(2)}, u32[]{:S(2)}) collective-permute-start(bf16[256,1024]{1,0:T(8,128)(2,1)} %get-tuple-element.86), channel_id=1, source_target_pairs={{0,16},{16,0},{1,17},{17,1},{2,18},{18,2},{3,19},{19,3},{4,20},{20... | collective-permute-start | bytes 1572872 | tf_op jit(solution)/shard_map/ppermute | solution.py:230
  1042.6 16.9 %collective-permute-start.37 = (bf16[256,512]{1,0:T(8,128)(2,1)}, bf16[256,512]{1,0:T(8,128)(2,1)}, u32[]{:S(2)}, u32[]{:S(2)}) collective-permute-start(bf16[256,512]{1,0:T(8,128)(2,1)} %get-tuple-element.76), channel_id=1, source_target_pairs={{16,0},{17,1},{18,2},{19,3},{20,4},{21,5},{22,6},{23,7},{24,8},{25... | collective-permute-start | bytes 786440 | tf_op jit(solution)/shard_map/ppermute | solution.py:648
  1046.0 22.4 %collective-permute-start.33 = (bf16[256,1536]{1,0:T(8,128)(2,1)}, bf16[256,1536]{1,0:T(8,128)(2,1)}, u32[]{:S(2)}, u32[]{:S(2)}) collective-permute-start(bf16[256,1536]{1,0:T(8,128)(2,1)} %pad_maximum_fusion.7), channel_id=1, source_target_pairs={{0,16},{1,17},{2,18},{3,19},{4,20},{5,21},{6,22},{7,23},{8,24},{9,... | collective-permute-start | bytes 2359304 | tf_op jit(solution)/shard_map/ppermute | solution.py:659
  1052.8 18.9 %collective-permute-start.30 = (bf16[256,1536]{1,0:T(8,128)(2,1)}, bf16[256,1536]{1,0:T(8,128)(2,1)}, u32[]{:S(2)}, u32[]{:S(2)}) collective-permute-start(bf16[256,1536]{1,0:T(8,128)(2,1)} %pad_maximum_fusion.6), channel_id=1, source_target_pairs={{16,0},{17,1},{18,2},{19,3},{20,4},{21,5},{22,6},{23,7},{24,8},{25... | collective-permute-start | bytes 2359304 | tf_op jit(solution)/shard_map/ppermute | solution.py:659
  1054.1 21.2 %collective-permute-start.45 = (bf16[256,2048]{1,0:T(8,128)(2,1)}, bf16[256,2048]{1,0:T(8,128)(2,1)}, u32[]{:S(2)}, u32[]{:S(2)}) collective-permute-start(bf16[256,2048]{1,0:T(8,128)(2,1)} %get-tuple-element.78), channel_id=1, source_target_pairs={{16,0},{17,1},{18,2},{19,3},{20,4},{21,5},{22,6},{23,7},{24,8},{25... | collective-permute-start | bytes 3145736 | tf_op jit(solution)/shard_map/ppermute | solution.py:648
  1067.0 13.2 %collective-permute-start.51 = (bf16[1024,512]{1,0:T(8,128)(2,1)S(1)}, bf16[1024,512]{1,0:T(8,128)(2,1)S(1)}, u32[]{:S(2)}, u32[]{:S(2)}) collective-permute-start(bf16[1024,512]{1,0:T(8,128)(2,1)S(1)} %copy-done.110), channel_id=1, source_target_pairs={{0,16},{1,17},{2,18},{3,19},{4,20},{5,21},{6,22},{7,23},{8,24},{9,... | collective-permute-start | bytes 3145736 | tf_op jit(solution)/shard_map/ppermute | solution.py:648
  1068.3 11.8 %collective-permute-start.50 = (bf16[1024,512]{1,0:T(8,128)(2,1)S(1)}, bf16[1024,512]{1,0:T(8,128)(2,1)S(1)}, u32[]{:S(2)}, u32[]{:S(2)}) collective-permute-start(bf16[1024,512]{1,0:T(8,128)(2,1)S(1)} %copy-done.111), channel_id=1, source_target_pairs={{16,0},{17,1},{18,2},{19,3},{20,4},{21,5},{22,6},{23,7},{24,8},{25... | collective-permute-start | bytes 3145736 | tf_op jit(solution)/shard_map/ppermute | solution.py:648
  (259 other events, 2569.3 us)
Sparse Core Ops, SparseCore 0:
  659.2 88.6 all-reduce.27
  843.7 32.0 all-reduce.23
  887.4 155.1 all-reduce.25

commit v2 on v1

--- a/solution.py
+++ b/solution.py
@@ -222,10 +222,6 @@
     return lax.ppermute(block, axis, route)
 
 
-def swap(block, bit):
-    return lax.ppermute(block, "seq", [(i, i ^ bit) for i in range(lax.axis_size("seq"))])
-
-
 def core_swap(block):
     return lax.ppermute(block, "section", [(0, 1), (1, 0)])
 
@@ -384,74 +380,247 @@
     )
 
 
-def blocks_by(values, order, axis=1):
-    here = lax.axis_index("seq")
-    width = values.shape[axis] // 4
-    return jnp.concatenate(
-        [lax.dynamic_slice_in_dim(values, (here ^ k) * width, width, axis) for k in order], axis=axis
-    )
-
-
-def tied(value, *before):
-    for array in before:
-        first = array[(0,) * array.ndim].astype(F32)
-        value = value + jnp.where(jnp.isnan(first), first, 0.0)
-    return value
-
-
 X_FIRST = (0, 2, 1, 3)
 Y_FIRST = (0, 1, 2, 3)
 
 
-def chip_and_seq_sum(keep, sent, order):
-    got = core_swap(sent)
-    middle = sent.shape[0] // 2
-    near_bit, far_bit = (2, 1) if order == X_FIRST else (1, 2)
-    far = (keep(True) + got[middle:].astype(F32)).astype(BF)
-    arrived = swap(far, far_bit)
-    near = keep(False) + got[:middle].astype(F32) + arrived.astype(F32)
-    last = swap(near[middle // 2 :].astype(BF), near_bit)
-    return near[: middle // 2] + last.astype(F32), arrived, last
-
-
-def product_reduce(left, keep, send, order):
-    if lax.axis_size("seq") != 4:
-        chip = dot_left(left, keep) + core_swap(dot_left(left, send).astype(BF)).astype(F32)
-        summed = lax.psum_scatter(chip.astype(BF), "seq", scatter_dimension=0, tiled=True).astype(F32)
-        return summed, summed, summed
-    left = blocks_by(left, order)
-    middle = left.shape[1] // 2
-
-    def kept(far):
-        return dot_left(left[:, middle:] if far else left[:, :middle], keep)
-
-    return chip_and_seq_sum(kept, dot_left(left, send).astype(BF), order)
-
-
-def array_reduce(values, core, order):
-    count, rows, width = values.shape
-    keep, send = core_halves(core, values.reshape(count * rows, width))
-    if count != 4:
-        chip = keep + core_swap(send.astype(BF)).astype(F32)
-        summed = lax.psum_scatter(chip.astype(BF), "seq", scatter_dimension=0, tiled=True).astype(F32)
-        return summed, summed, summed
-    keep = blocks_by(keep, order, 0)
-    middle = keep.shape[0] // 2
-    sent = blocks_by(send, order, 0).astype(BF)
-    return chip_and_seq_sum(lambda far: keep[middle:] if far else keep[:middle], sent, order)
-
-
-def sum_planes(values):
-    values = lax.optimization_barrier(values.astype(BF))
-    if True:
-        return lax.psum(values, "dp")
-    place = lax.axis_index("dp")
-    inward = lax.ppermute(values, "dp", [(0, 1), (3, 2)])
-    pair = lax.optimization_barrier((values.astype(F32) + inward.astype(F32)).astype(BF))
-    crossed = lax.ppermute(pair, "dp", [(1, 2), (2, 1)])
-    total = lax.optimization_barrier((pair.astype(F32) + crossed.astype(F32)).astype(BF))
-    outward = lax.ppermute(total, "dp", [(1, 0), (2, 3)])
-    return jnp.where(jnp.logical_or(place == 0, place == 3), outward, total)
+def reduce_kernel(items, halves, planes, *refs):
+    total = len(items)
+    sides = len(halves) * 2 + 1
+    inputs, refs = refs[:sides], refs[sides:]
+    own_out, refs = refs[:total], refs[total:]
+    other_out, refs = (refs[:total], refs[total:]) if planes else (own_out, refs)
+    hold, inbox, far_in, near_in, plane_in, cross_in, refs = (
+        refs[:total], refs[total : 2 * total], refs[2 * total : 3 * total], refs[3 * total : 4 * total],
+        refs[4 * total : 5 * total], refs[5 * total : 6 * total], refs[6 * total :],
+    )
+    send, recv, local = refs
+    core, here, plane = lax.axis_index("section"), lax.axis_index("seq"), lax.axis_index("dp")
+    by_x, by_y, far = here + 1 - 2 * (here % 2), (here + 2) % 4, 3 - here
+    to_x, to_y, to_core = (core, by_x, plane), (core, by_y, plane), (1 - core, here, plane)
+    to_inner = (core, here, (plane + 3) // 3)
+    to_outer = (core, here, 3 * (plane // 2))
+    to_cross = (core, here, 3 - plane)
+    outer = jnp.logical_or(plane == 0, plane == 3)
+    inner = jnp.logical_and(plane > 0, plane < 3)
+
+    barrier = pltpu.get_barrier_semaphore()
+
+    def greet(target):
+        pl.semaphore_signal(barrier, inc=1, device_id=target, device_id_type=MESH)
+
+    for target in (to_x, to_y, to_core):
+        greet(target)
+    if planes:
+
+        @pl.when(outer)
+        def _():
+            greet(to_inner)
+            pl.semaphore_wait(barrier, 4)
+
+        @pl.when(inner)
+        def _():
+            greet(to_outer)
+            greet(to_cross)
+            pl.semaphore_wait(barrier, 5)
+    else:
+        pl.semaphore_wait(barrier, 3)
+
+    def copy(kind, m, source, target_ref, target):
+        return pltpu.make_async_remote_copy(
+            src_ref=source, dst_ref=target_ref, send_sem=send.at[kind, m], recv_sem=recv.at[kind, m],
+            device_id=target, device_id_type=MESH,
+        )
+
+    def rows_of(ref, m, slot, slots=1):
+        rows = items[m][0]
+        return ref[m].at[pl.ds(slot * rows, slots * rows)]
+
+    def copies(m):
+        along_x = items[m][5] == X_FIRST
+        return dict(
+            core=lambda: copy(0, m, hold[m], inbox[m], to_core),
+            far=lambda: copy(1, m, rows_of(hold, m, 2, 2), far_in[m], to_x if along_x else to_y),
+            near=lambda: copy(2, m, rows_of(hold, m, 1), near_in[m], to_y if along_x else to_x),
+            inward=lambda: copy(3, m, rows_of(hold, m, 0), plane_in[m], to_inner),
+            cross=lambda: copy(4, m, rows_of(hold, m, 0), cross_in[m], to_cross),
+            outward=lambda: copy(3, m, rows_of(hold, m, 0), plane_in[m], to_outer),
+            last_held=lambda: copy(5, m, rows_of(hold, m, 0), other_out[m], to_core),
+            last_got=lambda: copy(5, m, plane_in[m], other_out[m], to_core),
+            held=lambda: pltpu.make_async_copy(rows_of(hold, m, 0), own_out[m], local.at[m]),
+            got=lambda: pltpu.make_async_copy(plane_in[m], own_out[m], local.at[m]),
+        )
+
+    moves = [copies(m) for m in range(total)]
+
+    def fill(m, slot, side, adds):
+        rows, columns, left, right, first, order = items[m]
+        block = {0: here, 1: by_x, 2: by_y, 3: far}[order[slot]]
+        high, wide = min(rows, 256), columns if columns <= 768 else 512
+        across = columns // wide
+        start = side * halves[right] + first if right >= 0 else side * columns
+
+        def step(index, carry):
+            down, along = index // across, index % across
+            picked = pl.ds(pl.multiple_of(block * rows + down * high, 16), high)
+            which = pl.ds(pl.multiple_of(start + along * wide, 128), wide)
+            if right >= 0:
+                value = jnp.dot(
+                    inputs[left][picked, :], inputs[len(halves) + right][:, which], preferred_element_type=F32
+                )
+            else:
+                value = inputs[-1][picked, which]
+            where = pl.ds(pl.multiple_of(along * wide, 128), wide)
+            for ref, base in adds:
+                value = value + ref[m][pl.ds(pl.multiple_of(base * rows + down * high, 16), high), where].astype(F32)
+            hold[m][pl.ds(pl.multiple_of(slot * rows + down * high, 16), high), where] = value.astype(BF)
+            return carry
+
+        lax.fori_loop(0, rows // high * across, step, 0)
+
+    def add_plane(m, ref):
+        rows = items[m][0]
+        high = min(rows, 64)
+
+        def step(index, carry):
+            where = pl.ds(pl.multiple_of(index * high, 16), high)
+            value = hold[m][where, :].astype(F32) + ref[m][where, :].astype(F32)
+            hold[m][where, :] = value.astype(BF)
+            return carry
+
+        lax.fori_loop(0, rows // high, step, 0)
+
+    def to_other_core(m):
+        for slot in (2, 3, 1, 0):
+            fill(m, slot, 1 - core, [])
+        moves[m]["core"]().start()
+
+    def first_hop(m):
+        moves[m]["core"]().wait()
+        for slot in (2, 3):
+            fill(m, slot, core, [(inbox, slot)])
+        moves[m]["far"]().start()
+
+    def second_hop(m):
+        moves[m]["far"]().wait_recv()
+        fill(m, 1, core, [(inbox, 1), (far_in, 1)])
+        moves[m]["near"]().start()
+
+    def arrive(m):
+        moves[m]["near"]().wait_recv()
+        fill(m, 0, core, [(inbox, 0), (far_in, 0), (near_in, 0)])
+        if planes:
+
+            @pl.when(outer)
+            def _():
+                moves[m]["inward"]().start()
+        else:
+            moves[m]["held"]().start()
+
+    def meet(m):
+        @pl.when(inner)
+        def _():
+            moves[m]["inward"]().wait_recv()
+            add_plane(m, plane_in)
+            moves[m]["cross"]().start()
+
+    def settle(m):
+        @pl.when(inner)
+        def _():
+            moves[m]["cross"]().wait()
+            add_plane(m, cross_in)
+            moves[m]["outward"]().start()
+            moves[m]["last_held"]().start()
+            moves[m]["held"]().start()
+
+    def finish(m):
+        @pl.when(outer)
+        def _():
+            moves[m]["inward"]().wait()
+            moves[m]["last_got"]().start()
+            moves[m]["got"]().start()
+
+    stages = [to_other_core, first_hop, second_hop, arrive]
+    if planes:
+        stages = stages + [meet, settle, finish]
+    for when in range(total // 2 + len(stages) - 1):
+        for number in reversed(range(len(stages))):
+            pair = when - number
+            if 0 <= pair < total // 2:
+                stages[number](2 * pair)
+                stages[number](2 * pair + 1)
+
+    for m in range(total):
+        moves[m]["far"]().wait_send()
+        moves[m]["near"]().wait_send()
+        if planes:
+
+            @pl.when(inner)
+            def _():
+                moves[m]["outward"]().wait_send()
+                moves[m]["last_held"]().wait()
+                moves[m]["held"]().wait()
+
+            @pl.when(outer)
+            def _():
+                moves[m]["last_got"]().wait()
+                moves[m]["got"]().wait()
+        else:
+            moves[m]["held"]().wait()
+
+
+def reduce_layer(lefts, rights, packed, planes, number):
+    count = lax.axis_size("seq")
+    halves = [right.shape[1] // 2 for right in rights]
+    small_rows, small_width = packed.shape[0] // count, packed.shape[1] // 2
+    up, down, enter, leave = (left.shape[0] // count for left in lefts)
+    items = [
+        (leave, halves[3], 3, 3, 0, X_FIRST),
+        (small_rows, small_width, -1, -1, 0, Y_FIRST),
+        (enter, halves[2] // 2, 2, 2, 0, X_FIRST),
+        (enter, halves[2] // 2, 2, 2, halves[2] // 2, Y_FIRST),
+        (up, halves[0] // 2, 0, 0, 0, X_FIRST),
+        (down, halves[1] // 2, 1, 1, 0, Y_FIRST),
+        (up, halves[0] // 2, 0, 0, halves[0] // 2, X_FIRST),
+        (down, halves[1] // 2, 1, 1, halves[1] // 2, Y_FIRST),
+    ]
+    shapes = [jax.ShapeDtypeStruct((item[0], item[1]), BF) for item in items]
+
+    def buffers(slots):
+        return [pltpu.VMEM((slots * item[0], item[1]), BF) for item in items]
+
+    hbm = pl.BlockSpec(memory_space=pl.ANY)
+    total = len(items)
+    outs = 2 if planes else 1
+    result = pl.pallas_call(
+        functools.partial(reduce_kernel, items, halves, planes),
+        out_shape=shapes * outs,
+        in_specs=[VMEM_SPEC] * (2 * len(lefts) + 1),
+        out_specs=[hbm] * (outs * total),
+        scratch_shapes=buffers(4) + buffers(4) + buffers(2) + buffers(1) + buffers(1) + buffers(1)
+        + [pltpu.SemaphoreType.DMA((6, total)), pltpu.SemaphoreType.DMA((6, total)), pltpu.SemaphoreType.DMA((total,))],
+        compiler_params=pltpu.CompilerParams(
+            collective_id=number, has_side_effects=True, vmem_limit_bytes=58 * 1024 * 1024
+        ),
+        name="reduce_layer",
+    )(*lefts, *rights, packed)
+    joined = []
+    for part in range(outs):
+        out, small, in_low, in_high, up_low, down_low, up_high, down_high = result[part * total : (part + 1) * total]
+        pairs = ((up_low, up_high), (down_low, down_high), (in_low, in_high))
+        joined.append([jnp.concatenate(pair, axis=1) for pair in pairs] + [out, small])
+    return joined
+
+
+def reduce_plain(lefts, rights, packed, core):
+    own = []
+    for left, right in [*zip(lefts, rights), (None, packed)]:
+        full = right if left is None else dot(left, right)
+        keep, send = core_halves(core, full.astype(BF))
+        chip = (keep.astype(F32) + core_swap(send).astype(F32)).astype(BF)
+        summed = lax.psum_scatter(chip, "seq", scatter_dimension=0, tiled=True)
+        own.append(lax.psum(summed, "dp"))
+    return own
 
 
 def body(
@@ -560,24 +729,18 @@
         )
         return layer_out.astype(BF), stored
 
-    def backward(upstream, stored, layer, before):
+    def backward(upstream, stored, layer):
         (
             layer_in, normed, projected, rim, mixed, signal, filtered, gated, residual, normed_two,
             upward, active, x_cols, filt, pull,
         ) = stored
         gain_one, short_weights, in_w, shift_w, freq_w, out_w, decay_w, bias, gain_two = small_of(layer)
         in_matrix, out_matrix, up_matrix, down_matrix = gathered[layer]
-        upstream_keep, upstream_send = core_halves(core, upstream)
         grad_hidden = jax.vjp(gelu_tanh, upward)[1](dot_right(upstream, down_matrix))[0].astype(BF)
-        hidden_keep, hidden_send = core_halves(core, grad_hidden)
-        grad_down = product_reduce(active, upstream_keep, upstream_send, Y_FIRST)
-        grad_up = product_reduce(normed_two, hidden_keep, hidden_send, X_FIRST)
         grad_norm_two = dot_right(grad_hidden, up_matrix)
         grad_resid_norm, grad_gain_two = jax.vjp(layer_norm, residual, gain_two)[1](grad_norm_two)
         grad_residual = upstream.astype(F32) + grad_resid_norm
-        grad_branch = tied(grad_residual, *before[0]).astype(BF)
-        branch_keep, branch_send = core_halves(core, grad_branch)
-        grad_out = product_reduce(gated, branch_keep, branch_send, X_FIRST)
+        grad_branch = grad_residual.astype(BF)
         grad_gated = dot_right(grad_branch, out_matrix)
         first, second, third = mixed[:, :width], mixed[:, width : 2 * width], mixed[:, 2 * width :]
         grad_second = grad_gated * filtered
@@ -594,14 +757,10 @@
         returned = shifted(grad_rim, "seq", -1)
         tail = grad_proj[rows - 2 :] + returned
         grad_proj = jnp.concatenate([grad_proj[: rows - 2], tail], axis=0)
-        grad_proj = tied(grad_proj, *before[1]).astype(BF)
-        proj_keep, proj_send = core_halves(core, grad_proj)
-        half = proj_keep.shape[1] // 2
-        grad_in_low = product_reduce(normed, proj_keep[:, :half], proj_send[:, :half], X_FIRST)
-        grad_in_high = product_reduce(normed, proj_keep[:, half:], proj_send[:, half:], Y_FIRST)
+        grad_proj = grad_proj.astype(BF)
         grad_normed = dot_right(grad_proj, in_matrix)
         grad_norm_in, grad_gain_one = jax.vjp(layer_norm, layer_in, gain_one)[1](grad_normed)
-        grad_layer_in = grad_residual + grad_norm_in
+        grad_layer_in = (grad_residual + grad_norm_in).astype(BF)
         d_in, d_shift, d_freq, d_out_cols, d_decay_cols = pull(grad_taps)
         d_out = lax.dynamic_update_slice_in_dim(jnp.zeros_like(out_w), d_out_cols, here * col_width, 1)
         d_decay = lax.dynamic_update_slice_in_dim(jnp.zeros_like(decay_w), d_decay_cols, here * col_width, 0)
@@ -615,23 +774,28 @@
             parts.append(jnp.moveaxis(grad.reshape(split), axis, 0).reshape(count, -1))
         packed = jnp.concatenate(parts, axis=1)
         packed = jnp.pad(packed, ((0, 0), (0, packed_rows * lane - packed.shape[1])))
-        grad_small = array_reduce(packed.reshape(count, packed_rows, lane), core, Y_FIRST)
-        return grad_layer_in, (grad_small, grad_in_low, grad_in_high, grad_out, grad_up, grad_down)
+        lefts = [normed_two.T, active.T, normed.T, gated.T]
+        rights = [grad_hidden, upstream, grad_proj, grad_branch]
+        return grad_layer_in, (lefts, rights, packed.reshape(count * packed_rows, lane))
 
     def row_of(values):
         return lax.dynamic_index_in_dim(values, core, 0, keepdims=False)
 
     out_first, stored_first = forward(row_of(tokens).astype(F32), 0)
     out_second, stored_second = forward(out_first.astype(F32), 1)
-    grad_second, sums_second = backward(row_of(out_grad), stored_second, 1, ((), ()))
-    small_two, in_low_two, in_high_two, out_two, up_two, down_two = sums_second
-    grad_second = tied(grad_second, up_two[1], down_two[1]).astype(BF)
-    mlp_two = [lax.psum(part[0].astype(BF), "dp") for part in (up_two, down_two)]
-    before = ((up_two[2], down_two[2], in_low_two[1], in_high_two[1]), tuple(mlp_two))
-    grad_first, sums_first = backward(grad_second, stored_first, 0, before)
-    grad_first = grad_first.astype(BF)
-    summed = [[sum_planes(part[0]) for part in sums] for sums in (sums_first, sums_second)]
-    summed[1][4:] = mlp_two
+    grad_second, factors_second = backward(row_of(out_grad), stored_second, 1)
+    routed = count == 4 and lax.axis_size("dp") == 4
+    if routed:
+        own_second = [lax.psum(part, "dp") for part in reduce_layer(*factors_second, False, 1)[0]]
+    else:
+        own_second = reduce_plain(*factors_second, core)
+    grad_first, factors_first = backward(grad_second, stored_first, 0)
+    if routed:
+        own_first, other_first = reduce_layer(*factors_first, True, 2)
+    else:
+        own_first = reduce_plain(*factors_first, core)
+        other_first = [lax.ppermute(part, "section", [(1, 0)]) for part in own_first]
+    other_second = [lax.ppermute(part, "section", [(0, 1)]) for part in own_second]
 
     def both_rows(of_first, of_second):
         kept = jnp.where(core == 0, of_first, of_second)
@@ -641,30 +805,13 @@
     layer_outputs = both_rows(out_first, out_second)
     input_grads = both_rows(grad_first, grad_second)
 
-    def finish(index, join):
-        whole = []
-        for layer, sums in enumerate(summed):
-            own = sums[index]
-            received = lax.ppermute(own, "section", [(1 - layer, layer)])
-            whole.append(join(own, received) if layer == 0 else join(received, own))
-        return jnp.where(core == 0, whole[0], whole[1]).astype(F32)
-
-    def side_by_side(low, high):
-        return jnp.concatenate([low, high], axis=1)
-
-    def finish_in():
-        whole = []
-        for layer, sums in enumerate(summed):
-            own = jnp.concatenate(sums[1:3], axis=1)
-            received = lax.ppermute(own, "section", [(1 - layer, layer)])
-            whole.append(side_by_side(own, received) if layer == 0 else side_by_side(received, own))
-        return jnp.where(core == 0, whole[0], whole[1]).astype(F32)
-
-    small_total = finish(0, side_by_side).reshape(-1)
-    grad_in = finish_in()
-    grad_out = finish(3, side_by_side)
-    grad_up = finish(4, side_by_side)
-    grad_down = finish(5, side_by_side)
+    def finish(index):
+        low = jnp.where(core == 0, own_first[index], other_second[index])
+        high = jnp.where(core == 0, other_first[index], own_second[index])
+        return jnp.concatenate([low, high], axis=1).astype(F32)
+
+    grad_up, grad_down, grad_in, grad_out = (finish(index) for index in range(4))
+    small_total = finish(4).reshape(-1)
     small_out = []
     offset = 0
     for shape, size in zip(small_shapes, small_sizes):

time: 1100 us -> 927 us (0.84)
  Pallas kernels: 213 us -> 521 us
  waiting for transfers between devices: 310 us -> 18 us
  matrix products: 193 us -> 105 us
  starting transfers between devices: 102 us -> 54.2 us
  other arithmetic: 124 us -> 81 us
  blocking collectives: 0 us -> 20 us
  between operations: 35.2 us -> 19.2 us
  local copies, waits for them, and re-layouts: 113 us -> 97.9 us
    pallas_call x0 -> x2, Pallas kernels: none -> 308 us  [reduce_layer(): pl.pallas_call(functools.partial(reduce_kernel, items, halves, planes), o...]
    ppermute x34 -> x5, waiting for transfers between devices: 151 us -> 0.01 us  [body(): lax.ppermute(part, 'section', [(0, 1)])]
    psum x3 -> x1, waiting for transfers between devices: 143 us -> 0.01 us  [body(): lax.psum(part, 'dp')]
    dot_general x30 -> x0, matrix products: 78.2 us -> none  [dot_left(): lax.dot_general(left, right, (((0,), (0,)), ((), ())), preferred_element_...]
    ppermute x34 -> x5, starting transfers between devices: 55.7 us -> 8.98 us  [body(): lax.ppermute(part, 'section', [(0, 1)])]
    convert_element_type x26 -> x8, other arithmetic: 40.5 us -> 16.1 us  [the longest x4 8.23 us: finish(): return jnp.concatenate([low, high], axis=1).astype(F32)]
    psum x0 -> x1, blocking collectives: none -> 20 us  [body(): lax.psum(part, 'dp')]
    add x9 -> x0, other arithmetic: 14.5 us -> none  [the longest x8 14.4 us: chip_and_seq_sum(): near = keep(False) + got[:middle].astype(F32) + arrived.astype(F32)]
  transfers between devices with their start and end apart: 63 -> 20, of which waited for: 20 -> 6; matrix products, arithmetic and copies ran while one was open for 27% -> 12% of each run, Pallas kernels for 1% -> 34%
where the time goes in v2:
time: 927 us; the launch traced here: 916 us
  Pallas kernels  521 us (56%)
  matrix products  105 us (11%)
  local copies, waits for them, and re-layouts  97.9 us (11%)
  other arithmetic  81 us (9%)
  starting transfers between devices  54.2 us (6%)
  blocking collectives  20 us (2%)
  between operations  19.2 us (2%)
  waiting for transfers between devices  18 us (2%)
    pallas_call x2, Pallas kernels, reduce_layer(): pl.pallas_call(functools.partial(reduce_kernel, items, halves, planes), o...  308 us
    pallas_call x1, Pallas kernels, gather_shards(): pl.pallas_call(functools.partial(gather_kernel, sizes, count), out_shape=...  198 us
    dot_general x8, matrix products, dot_right(): lax.dot_general(left, right, (((1,), (1,)), ((), ())), preferred_element_...  44.1 us
    unnamed x398, local copies, waits for them, and re-layouts  42.9 us
    dot_general x8, matrix products, dot(): return jnp.dot(left, right, preferred_element_type=F32)  40.1 us
    psum x1, blocking collectives, body(): lax.psum(part, 'dp')  20 us
  transfers between devices with their start and end apart: 20, of which 6 were waited for; matrix products, arithmetic and copies ran while one was open for 12% of the time, Pallas kernels for 34%

profile of v2, /device:TPU:0, one launch (start us, length us, event | category | flops | bytes accessed | tf_op | source)
XLA Modules:
  0.0 916.4 jit_solution(1208226650303579424)
XLA Ops:
  14.5 198.1 %gather_shards.1 = (bf16[256,1024]{1,0:T(8,128)(2,1)}, bf16[2048,1024]{1,0:T(8,128)(2,1)}, bf16[2048,3072]{1,0:T(8,128)(2,1)}, bf16[2048,4096]{1,0:T(8,128)(2,1)}, bf16[8192,1024]{1,0:T(8,128)(2,1)}) custom-call(bf16[32,1024]{1,0:T(8,128)(2,1)} %reshape.611.refs_0_, bf16[256,1024]{1,0:T(8,128)(2,1)} %bitcast.270, bf16[256,3072]{1,0:T(8,128)(2,1)} %bitcast.269, ...), custom_call_target="tpu_custom_call" | custom-call | tf_op jit(solution)/shard_map/gather_shards/pallas_call | solution.py:360
  214.7 6.4 fusion.201
  222.3 3.4 collective-permute-start
  229.7 2.7 multiply_convert_fusion.17
  242.7 4.9 multiply_add_fusion.1
  251.3 3.7 all-to-all-start
  255.0 5.1 add_multiply_fusion
  265.9 4.1 all-to-all-start.1
  270.1 6.9 all-to-all-done.1
  282.8 6.4 fusion.14
  289.9 2.7 slice-done.3
  292.6 2.9 convert_reduce_fusion
  295.8 6.3 fusion.203
  303.4 3.3 collective-permute-start.1
  308.7 4.8 multiply_add_fusion
  317.1 4.5 all-to-all-start.2
  324.7 5.6 copy.100
  335.4 4.6 all-to-all-start.3
  340.0 4.8 fusion.45.refs_1_
  353.1 7.8 fusion.6
  361.0 5.6 copy.106
  366.6 7.6 fusion.37.refs_4_
  374.3 7.4 multiply_reduce_fusion.6
  384.0 4.0 multiply_reduce_fusion.7
  390.0 4.4 all-to-all-start.4
  394.4 8.7 broadcast_select_fusion.2
  403.1 2.6 fusion.53.refs_1_
  417.8 4.1 correlate.2
  422.7 4.2 all-to-all-start.5
  427.7 3.3 convolution_dynamic-update-slice_fusion
  431.0 3.2 multiply_reduce_fusion.16
  451.8 2.7 collective-permute-done.3
  460.3 6.9 fusion.30.refs_4_
  467.3 7.4 multiply_reduce_fusion.9
  477.1 3.3 multiply_reduce_fusion.10
  482.5 5.2 all-to-all-start.6
  500.4 5.5 correlate.3
  506.0 2.8 multiply_reduce_fusion.17
  511.8 2.9 convolution_dynamic-update-slice_fusion.1
  517.6 4.2 all-to-all-start.7
  522.0 127.6 %reduce_layer.3 = (bf16[256,512]{1,0:T(8,128)(2,1)}, bf16[32,512]{1,0:T(8,128)(2,1)}, bf16[256,768]{1,0:T(8,128)(2,1)}, bf16[256,768]{1,0:T(8,128)(2,1)}, bf16[2...) custom-call(bf16[1024,256]{1,0:T(8,128)(2,1)} %copy.109.refs_0_, ...), custom_call_target="tpu_custom_call" | custom-call | tf_op jit(solution)/shard_map/reduce_layer/pallas_call | solution.py:595
  649.6 20.0 %psum.35 = bf16[32,512]{1,0:T(8,128)(2,1)S(1)} all-reduce(bf16[32,512]{1,0:T(8,128)(2,1)} %get-tuple-element.58), channel_id=1, replica_groups=mesh['section'=2,'seq'=4,'dp'=4] {'dp'}, use_global_device_ids=true, to_apply=%region_39.40 | all-reduce | flops 16384 | bytes 65536 | tf_op jit(solution)/shard_map/psum | solution.py:789
  684.5 2.8 pad_add_fusion
  695.2 5.4 fusion.119
  703.9 180.5 %reduce_layer.2 = (bf16[256,512]{1,0:T(8,128)(2,1)}, bf16[32,512]{1,0:T(8,128)(2,1)}, bf16[256,768]{1,0:T(8,128)(2,1)}, bf16[256,768]{1,0:T(8,128)(2,1)}, bf16[2...) custom-call(bf16[1024,256]{1,0:T(8,128)(2,1)} %copy.103.refs_0_, ...), custom_call_target="tpu_custom_call" | custom-call | tf_op jit(solution)/shard_map/reduce_layer/pallas_call | solution.py:595
  890.9 3.1 collective-permute-start.10
  903.6 2.6 maximum_convert_fusion.1
  906.6 2.5 maximum_convert_fusion
  (622 shorter events, 167.6 us)
Async XLA Ops:
  14.5 199.7 %copy-start.71 = (bf16[2,256,1024]{2,1,0:T(8,128)(2,1)S(1)}, bf16[2,256,1024]{2,1,0:T(8,128)(2,1)}, u32[]{:S(2)}) copy-start(bf16[2,256,1024]{2,1,0:T(8,128)(2,1)} %param.20) | copy-start | bytes 3145732
  214.6 11.4 %copy-start.185 = (s32[2,4]{1,0:T(2,128)S(1)}, s32[2,4]{1,0:T(2,128)}, u32[]{:S(2)}) copy-start(s32[2,4]{1,0:T(2,128)} %param.22) | copy-start | bytes 100
  214.7 12.4 %copy-start.54 = (f32[1024,33]{1,0:T(8,128)S(1)}, f32[1024,33]{1,0:T(8,128)}, u32[]{:S(2)}) copy-start(f32[1024,33]{1,0:T(8,128)} %constant.90.clone) | copy-start | bytes 405508
  222.3 20.4 %collective-permute-start = (bf16[2,3072]{1,0:T(2,128)(2,1)S(1)}, bf16[2,3072]{1,0:T(2,128)(2,1)S(1)}, u32[]{:S(2)}, u32[]{:S(2)}) collective-permute-start(bf16[2,3072]{1,0:T(2,128)(2,1)S(1)} %slice.286), channel_id=1, source_target_pairs={{0,4},{4,8},{8,12},{1,5},{5,9},{9,13},{2,6},{6,10},{10,14},{3,7},{... | collective-permute-start | bytes 36872 | tf_op jit(solution)/shard_map/ppermute | solution.py:222
  251.3 11.4 %all-to-all-start = ((bf16[256,4,256]{2,0,1:T(8,128)(2,1)}), bf16[256,4,256]{2,0,1:T(8,128)(2,1)S(1)}, u32[]{:S(2)}, u32[]{:S(2)}) async-start(bf16[256,4,256]{2,0,1:T(8,128)(2,1)} %bitcast.241), calls=%async_computation | async-start | bytes 1048576 | tf_op jit(solution)/shard_map/all_to_all | solution.py:689
  262.7 15.6 %copy-start.3 = (bf16[256,4,256]{2,0,1:T(8,128)(2,1)}, bf16[256,4,256]{2,0,1:T(8,128)(2,1)S(1)}, u32[]{:S(2)}) copy-start(bf16[256,4,256]{2,0,1:T(8,128)(2,1)S(1)} %all-to-all-done) | copy-start | bytes 1572868
  265.9 11.1 %all-to-all-start.1 = ((bf16[4,256,256]{2,1,0:T(8,128)(2,1)}), bf16[4,256,256]{2,1,0:T(8,128)(2,1)}, u32[]{:S(2)}, u32[]{:S(2)}) async-start(bf16[4,256,256]{2,1,0:T(8,128)(2,1)} %bitcast.247), calls=%async_computation.1 | async-start | bytes 1048576 | tf_op jit(solution)/shard_map/all_to_all | solution.py:692
  270.1 12.7 %copy-start.145 = (f32[1,2,4,128]{3,1,2,0:T(2,128)}, f32[1,2,4,128]{3,1,2,0:T(2,128)S(1)}, u32[]{:S(2)}) copy-start(f32[1,2,4,128]{3,1,2,0:T(2,128)S(1)} %copy.131) | copy-start | bytes 12292
  270.1 25.7 %copy-start.133 = (f32[1,2,4,128]{3,1,2,0:T(2,128)}, f32[1,2,4,128]{3,1,2,0:T(2,128)S(1)}, u32[]{:S(2)}) copy-start(f32[1,2,4,128]{3,1,2,0:T(2,128)S(1)} %copy.132) | copy-start | bytes 12292
  280.3 8.9 copy-start.84
  282.8 9.8 %slice-start.3 = ((s8[16777216]{0:T(1024)(128)(4,1)}), s8[4194304]{0:T(1024)(128)(4,1)S(1)}, s32[]{:S(2)}) async-start(s8[16777216]{0:T(1024)(128)(4,1)} %bitcast.322), calls=%async_computation.12 | async-start | bytes 8388608
  303.4 4.7 collective-permute-start.1
  317.1 13.2 %all-to-all-start.2 = ((bf16[256,4,256]{2,0,1:T(8,128)(2,1)}), bf16[256,4,256]{2,0,1:T(8,128)(2,1)S(1)}, u32[]{:S(2)}, u32[]{:S(2)}) async-start(bf16[256,4,256]{2,0,1:T(8,128)(2,1)} %bitcast.262), calls=%async_computation.2 | async-start | bytes 1048576 | tf_op jit(solution)/shard_map/all_to_all | solution.py:689
  330.3 14.4 %copy-start.5 = (bf16[256,4,256]{2,0,1:T(8,128)(2,1)}, bf16[256,4,256]{2,0,1:T(8,128)(2,1)S(1)}, u32[]{:S(2)}) copy-start(bf16[256,4,256]{2,0,1:T(8,128)(2,1)S(1)} %all-to-all-done.2) | copy-start | bytes 1572868
  335.4 11.5 %all-to-all-start.3 = ((bf16[4,256,256]{2,1,0:T(8,128)(2,1)}), bf16[4,256,256]{2,1,0:T(8,128)(2,1)}, u32[]{:S(2)}, u32[]{:S(2)}) async-start(bf16[4,256,256]{2,1,0:T(8,128)(2,1)} %bitcast.248), calls=%async_computation.3 | async-start | bytes 1048576 | tf_op jit(solution)/shard_map/all_to_all | solution.py:692
  352.2 22.0 %copy-start.169 = (f32[256]{0:T(256)}, f32[256]{0:T(256)S(1)}, u32[]{:S(2)}) copy-start(f32[256]{0:T(256)S(1)} %broadcast_multiply_fusion.6) | copy-start | bytes 3076
  352.5 21.8 %copy-start.181 = (f32[256]{0:T(256)}, f32[256]{0:T(256)S(1)}, u32[]{:S(2)}) copy-start(f32[256]{0:T(256)S(1)} %fusion.172) | copy-start | bytes 3076
  374.3 9.7 %copy-start.63 = (bf16[2048,1024]{1,0:T(8,128)(2,1)S(1)}, bf16[2048,1024]{1,0:T(8,128)(2,1)}, u32[]{:S(2)}) copy-start(bf16[2048,1024]{1,0:T(8,128)(2,1)} %get-tuple-element.50) | copy-start | bytes 12582916
  390.0 21.4 %all-to-all-start.4 = ((bf16[256,4,256]{2,0,1:T(8,128)(2,1)}), bf16[256,4,256]{2,0,1:T(8,128)(2,1)S(1)}, u32[]{:S(2)}, u32[]{:S(2)}) async-start(bf16[256,4,256]{2,0,1:T(8,128)(2,1)} %bitcast.261), calls=%async_computation.4 | async-start | bytes 1048576 | tf_op jit(solution)/shard_map/all_to_all | solution.py:689
  394.4 8.7 copy-start.25
  411.4 27.9 %collective-permute-start.2 = (bf16[256,1024]{1,0:T(8,128)(2,1)}, bf16[256,1024]{1,0:T(8,128)(2,1)}, u32[]{:S(2)}, u32[]{:S(2)}) collective-permute-start(bf16[256,1024]{1,0:T(8,128)(2,1)} %get-tuple-element.215), channel_id=1, source_target_pairs={{0,16},{16,0},{1,17},{17,1},{2,18},{18,2},{3,19},{19,3},{4,20},{20... | collective-permute-start | bytes 1572872 | tf_op jit(solution)/shard_map/ppermute | solution.py:226
  422.7 18.9 %all-to-all-start.5 = ((bf16[4,256,256]{2,1,0:T(8,128)(2,1)}), bf16[4,256,256]{2,1,0:T(8,128)(2,1)}, u32[]{:S(2)}, u32[]{:S(2)}) async-start(bf16[4,256,256]{2,1,0:T(8,128)(2,1)} %bitcast.249), calls=%async_computation.5 | async-start | bytes 1048576 | tf_op jit(solution)/shard_map/all_to_all | solution.py:692
  448.7 5.8 collective-permute-start.3
  459.9 16.0 %copy-start.28 = (bf16[256,1024]{1,0:T(8,128)(2,1)}, bf16[256,1024]{1,0:T(8,128)(2,1)S(1)}, u32[]{:S(2)}) copy-start(bf16[256,1024]{1,0:T(8,128)(2,1)S(1)} %get-tuple-element.169.refs_5_) | copy-start | bytes 1572868
  467.3 9.8 %copy-start.64 = (bf16[2048,1024]{1,0:T(8,128)(2,1)S(1)}, bf16[2048,1024]{1,0:T(8,128)(2,1)}, u32[]{:S(2)}) copy-start(bf16[2048,1024]{1,0:T(8,128)(2,1)} %get-tuple-element.50) | copy-start | bytes 12582916
  481.5 11.2 %copy-start.182 = (f32[1024]{0:T(1024)S(1)}, f32[1024]{0:T(1024)}, u32[]{:S(2)}) copy-start(f32[1024]{0:T(1024)} %get-tuple-element.121) | copy-start | bytes 12292
  482.5 15.0 %all-to-all-start.6 = ((bf16[256,4,256]{2,0,1:T(8,128)(2,1)}), bf16[256,4,256]{2,0,1:T(8,128)(2,1)}, u32[]{:S(2)}, u32[]{:S(2)}) async-start(bf16[256,4,256]{2,0,1:T(8,128)(2,1)} %bitcast.260), calls=%async_computation.6 | async-start | bytes 1048576 | tf_op jit(solution)/shard_map/all_to_all | solution.py:689
  489.9 16.0 %copy-start.140 = (f32[256]{0:T(256)S(1)}, f32[256]{0:T(256)}, u32[]{:S(2)}) copy-start(f32[256]{0:T(256)} %copy-done.139) | copy-start | bytes 3076
  489.9 16.0 %copy-start.157 = (f32[64]{0:T(128)S(1)}, f32[64]{0:T(128)}, u32[]{:S(2)}) copy-start(f32[64]{0:T(128)} %copy-done.156) | copy-start | bytes 772
  493.3 15.4 %copy-start.142 = (f32[256]{0:T(256)S(1)}, f32[256]{0:T(256)}, u32[]{:S(2)}) copy-start(f32[256]{0:T(256)} %copy-done.141) | copy-start | bytes 3076
  517.6 159.5 %all-to-all-start.7 = ((bf16[4,256,256]{2,1,0:T(8,128)(2,1)}), bf16[4,256,256]{2,1,0:T(8,128)(2,1)}, u32[]{:S(2)}, u32[]{:S(2)}) async-start(bf16[4,256,256]{2,1,0:T(8,128)(2,1)} %bitcast.46), calls=%async_computation.7 | async-start | bytes 1048576 | tf_op jit(solution)/shard_map/all_to_all | solution.py:692
  521.7 369.2 %all-reduce.20.cloned.1.call-start = ((), (), s32[]{:S(2)}) async-start(), calls=%async_computation.8 | async-start | bytes 6291456 | tf_op jit(solution)/shard_map/psum | solution.py:789
  649.6 26.5 %copy-start.108 = (bf16[256,768]{1,0:T(8,128)(2,1)S(1)}, bf16[256,768]{1,0:T(8,128)(2,1)}, u32[]{:S(2)}) copy-start(bf16[256,768]{1,0:T(8,128)(2,1)} %get-tuple-element.62) | copy-start | bytes 1179652
  649.6 26.5 %copy-start.109 = (bf16[256,768]{1,0:T(8,128)(2,1)S(1)}, bf16[256,768]{1,0:T(8,128)(2,1)}, u32[]{:S(2)}) copy-start(bf16[256,768]{1,0:T(8,128)(2,1)} %get-tuple-element.63) | copy-start | bytes 1179652
  669.6 216.7 %collective-permute-start.6 = (bf16[32,512]{1,0:T(8,128)(2,1)S(1)}, bf16[32,512]{1,0:T(8,128)(2,1)}, u32[]{:S(2)}, u32[]{:S(2)}) collective-permute-start(bf16[32,512]{1,0:T(8,128)(2,1)S(1)} %psum.35), channel_id=1, source_target_pairs={{0,16},{1,17},{2,18},{3,19},{4,20},{5,21},{6,22},{7,23},{8,24},{9,... | collective-permute-start | bytes 98312 | tf_op jit(solution)/shard_map/ppermute | solution.py:798
  687.9 5.9 collective-permute-start.4
  703.9 180.5 %copy-start.29 = (bf16[256,1024]{1,0:T(8,128)(2,1)S(1)}, bf16[256,1024]{1,0:T(8,128)(2,1)}, u32[]{:S(2)}) copy-start(bf16[256,1024]{1,0:T(8,128)(2,1)} %copy-done.28) | copy-start | bytes 1572868
  703.9 180.5 %copy-start.47 = (f32[256,1024]{1,0:T(8,128)S(1)}, f32[256,1024]{1,0:T(8,128)}, u32[]{:S(2)}) copy-start(f32[256,1024]{1,0:T(8,128)} %copy-done.46) | copy-start | bytes 3145732
  703.9 180.6 %copy-start.74 = (bf16[2,256,1024]{2,1,0:T(8,128)(2,1)S(1)}, bf16[2,256,1024]{2,1,0:T(8,128)(2,1)}, u32[]{:S(2)}) copy-start(bf16[2,256,1024]{2,1,0:T(8,128)(2,1)} %param.20) | copy-start | bytes 3145732
  703.9 180.6 %copy-start.175 = (f32[256]{0:T(256)S(1)}, f32[256]{0:T(256)}, u32[]{:S(2)}) copy-start(f32[256]{0:T(256)} %copy-done.174) | copy-start | bytes 3076
  885.9 12.2 %copy-start.102 = (bf16[256,1024]{1,0:T(8,128)(2,1)S(1)}, bf16[256,1024]{1,0:T(8,128)(2,1)}, u32[]{:S(2)}) copy-start(bf16[256,1024]{1,0:T(8,128)(2,1)} %get-tuple-element.73) | copy-start | bytes 1572868
  885.9 12.2 %copy-start.103 = (bf16[256,1024]{1,0:T(8,128)(2,1)S(1)}, bf16[256,1024]{1,0:T(8,128)(2,1)}, u32[]{:S(2)}) copy-start(bf16[256,1024]{1,0:T(8,128)(2,1)} %get-tuple-element.74) | copy-start | bytes 1572868
  885.9 3.9 collective-permute-start.5
  889.8 8.7 copy-start.106
  890.9 12.3 %collective-permute-start.10 = (bf16[1024,512]{1,0:T(8,128)(2,1)}, bf16[1024,512]{1,0:T(8,128)(2,1)S(1)}, u32[]{:S(2)}, u32[]{:S(2)}) collective-permute-start(bf16[1024,512]{1,0:T(8,128)(2,1)} %get-tuple-element.136), channel_id=1, source_target_pairs={{0,16},{1,17},{2,18},{3,19},{4,20},{5,21},{6,22},{7,23},{8,24},{9,... | collective-permute-start | bytes 3145736 | tf_op jit(solution)/shard_map/ppermute | solution.py:798
  894.0 12.2 %collective-permute-start.9 = (bf16[256,2048]{1,0:T(8,128)(2,1)}, bf16[256,2048]{1,0:T(8,128)(2,1)S(1)}, u32[]{:S(2)}, u32[]{:S(2)}) collective-permute-start(bf16[256,2048]{1,0:T(8,128)(2,1)} %get-tuple-element.135), channel_id=1, source_target_pairs={{0,16},{1,17},{2,18},{3,19},{4,20},{5,21},{6,22},{7,23},{8,24},{9,... | collective-permute-start | bytes 3145736 | tf_op jit(solution)/shard_map/ppermute | solution.py:798
  895.4 4.5 collective-permute-start.8
  896.7 4.3 collective-permute-start.7
  (165 other events, 631.0 us)
Sparse Core Ops, SparseCore 0:
  677.2 149.4 all-reduce.19

commit v3 on v2

--- a/solution.py
+++ b/solution.py
@@ -90,11 +90,43 @@
 
 def convolve_kernel(blocks, rows, step, same_ref, table_ref, back_ref, filt_ref, x_ref, y_ref, spec_ref, out_ref):
     spectra_rows(table_ref, x_ref, spec_ref, blocks, rows)
+    convolve_spectra(blocks, rows, step, same_ref, filt_ref, spec_ref, out_ref)
+    for block in range(blocks):
+        y_ref[pl.ds(block * rows, rows), :] = jnp.dot(
+            back_ref[...], out_ref[block], preferred_element_type=F32
+        ).astype(BF)
+
+
+def correlate_kernel(
+    blocks, rows, step, same_ref, table_ref, back_ref, scale_ref, filt_ref, x_ref, g_ref,
+    dx_ref, dt_ref, spec_ref, grad_ref, out_ref, tap_ref,
+):
+    spectra_rows(table_ref, x_ref, spec_ref, blocks, rows)
+    spectra_rows(table_ref, g_ref, grad_ref, blocks, rows)
+    correlate_spectra(blocks, rows, step, same_ref, scale_ref, filt_ref, spec_ref, grad_ref, out_ref, tap_ref)
+    for block in range(blocks):
+        dx_ref[pl.ds(block * rows, rows), :] = jnp.dot(
+            back_ref[...], out_ref[block], preferred_element_type=F32
+        ).astype(BF)
+    taps_back(blocks, rows, back_ref, scale_ref, tap_ref, dt_ref)
+
+
+MESH = pl.DeviceIdType.MESH
+VMEM_SPEC = pl.BlockSpec(memory_space=pltpu.VMEM)
+SMEM_SPEC = pl.BlockSpec(memory_space=pltpu.SMEM)
+KERNEL_BYTES = 48 * 1024 * 1024
+
+
+def lasting(microseconds):
+    return pl.CostEstimate(flops=0, bytes_accessed=int(microseconds * 3.69e6), transcendentals=0)
+
+
+def convolve_spectra(blocks, rows, step, same_ref, filt_ref, spec_ref, out_ref):
+    width = spec_ref.shape[2]
 
     def chunk(index, carry):
         real = pl.ds(pl.multiple_of(index * step, step), step)
         imag = pl.ds(pl.multiple_of(rows + index * step, step), step)
-        width = x_ref.shape[1]
         first = (lax.broadcasted_iota(jnp.int32, (step, width), 0) + index * step) == 0
         for i in range(blocks):
             total_real = jnp.zeros((step, width), F32)
@@ -114,23 +146,14 @@
         return carry
 
     lax.fori_loop(0, rows // step, chunk, 0)
-    for block in range(blocks):
-        y_ref[pl.ds(block * rows, rows), :] = jnp.dot(
-            back_ref[...], out_ref[block], preferred_element_type=F32
-        ).astype(BF)
-
-
-def correlate_kernel(
-    blocks, rows, step, same_ref, table_ref, back_ref, scale_ref, filt_ref, x_ref, g_ref,
-    dx_ref, dt_ref, spec_ref, grad_ref, out_ref, tap_ref,
-):
-    spectra_rows(table_ref, x_ref, spec_ref, blocks, rows)
-    spectra_rows(table_ref, g_ref, grad_ref, blocks, rows)
+
+
+def correlate_spectra(blocks, rows, step, same_ref, scale_ref, filt_ref, spec_ref, grad_ref, out_ref, tap_ref):
+    width = spec_ref.shape[2]
 
     def chunk(index, carry):
         real = pl.ds(pl.multiple_of(index * step, step), step)
         imag = pl.ds(pl.multiple_of(rows + index * step, step), step)
-        width = x_ref.shape[1]
         first = (lax.broadcasted_iota(jnp.int32, (step, width), 0) + index * step) == 0
         for j in range(blocks):
             total_real = jnp.zeros((step, width), F32)
@@ -165,18 +188,281 @@
         return carry
 
     lax.fori_loop(0, rows // step, chunk, 0)
+
+
+def taps_back(blocks, rows, back_ref, scale_ref, tap_ref, dt_ref):
     for block in range(blocks):
-        where = pl.ds(block * rows, rows)
-        dx_ref[where, :] = jnp.dot(back_ref[...], out_ref[block], preferred_element_type=F32).astype(BF)
         total = tap_ref[block]
         if block + 1 < blocks:
             total = total + scale_ref[:, 1:2] * tap_ref[block + 1]
-        dt_ref[where, :] = jnp.dot(back_ref[...], total.astype(BF), preferred_element_type=F32)
-
-
-VMEM_SPEC = pl.BlockSpec(memory_space=pltpu.VMEM)
-SMEM_SPEC = pl.BlockSpec(memory_space=pltpu.SMEM)
-KERNEL_BYTES = 48 * 1024 * 1024
+        dt_ref[pl.ds(block * rows, rows), :] = jnp.dot(
+            back_ref[...], total.astype(BF), preferred_element_type=F32
+        )
+
+
+class Peers:
+    def __init__(self, send, recv):
+        self.core, self.here, self.plane = lax.axis_index("section"), lax.axis_index("seq"), lax.axis_index("dp")
+        here = self.here
+        self.blocks = (3 - here, here + 1 - 2 * (here % 2), (here + 2) % 4)
+        self.send, self.recv = send, recv
+        barrier = pltpu.get_barrier_semaphore()
+        for block in self.blocks:
+            pl.semaphore_signal(barrier, inc=1, device_id=self.at(block), device_id_type=MESH)
+        pl.semaphore_wait(barrier, 3)
+
+    def at(self, block):
+        return (self.core, block, self.plane)
+
+    def copy(self, number, source, target_ref, block):
+        return pltpu.make_async_remote_copy(
+            src_ref=source, dst_ref=target_ref, send_sem=self.send.at[number], recv_sem=self.recv.at[number],
+            device_id=self.at(block), device_id_type=MESH,
+        )
+
+
+def delayed(values, distance, before):
+    index = lax.broadcasted_iota(jnp.int32, values.shape, 0)
+    result = pltpu.roll(values, distance, 0)
+    for row in range(distance):
+        result = jnp.where(index == row, before[row], result)
+    return result
+
+
+def advanced(values, distance):
+    rows = values.shape[0]
+    index = lax.broadcasted_iota(jnp.int32, values.shape, 0)
+    return jnp.where(index >= rows - distance, 0.0, pltpu.roll(values, rows - distance, 0))
+
+
+def mixed_part(proj_ref, rim_ref, weight_ref, carried, columns):
+    now = proj_ref[:, columns].astype(F32)
+    rim = rim_ref[:, columns].astype(F32) * carried
+    size = rim.shape[0]
+    last, before_last = rim[size - 1 : size, :], rim[size - 2 : size - 1, :]
+    one = delayed(now, 1, (last,))
+    two = delayed(now, 2, (before_last, last))
+    mixed = weight_ref[0:1, columns] * now + weight_ref[1:2, columns] * one + weight_ref[2:3, columns] * two
+    return mixed, now, one, two
+
+
+def mix_kernel(
+    blocks, rows, step, same_ref, carried_ref, table_ref, back_ref, filt_ref, proj_ref, weight_ref, bias_ref, valid_ref,
+    rim_out_ref, x_out_ref, filtered_ref, gated_ref,
+    rim_ref, x_ref, mask_ref, signal_ref, second_ref, spec_ref, out_ref, y_ref, y_in_ref, send, recv,
+):
+    peers = Peers(send, recv)
+    here, width = peers.here, proj_ref.shape[1] // 3
+    group = width // blocks
+    tail = rim_ref.shape[0]
+    rim_copy = peers.copy(0, proj_ref.at[pl.ds(rows - tail, tail)], rim_ref, (here + 1) % 4)
+    rim_copy.start()
+    rim_copy.wait()
+    carried, valid = carried_ref[0], valid_ref[...]
+
+    def at_rows(block):
+        return pl.ds(pl.multiple_of(block * rows, rows), rows)
+
+    outgoing = []
+    for number, block in enumerate(peers.blocks + (here,)):
+        start = block * group
+
+        def part(which):
+            columns = pl.ds(pl.multiple_of(which * width + start, 128), group)
+            return mixed_part(proj_ref, rim_ref, weight_ref, carried, columns)[0]
+
+        signal = part(0) * part(2)
+        signal_ref[block] = signal
+        second_ref[block] = part(1)
+        masked = (signal * valid).astype(BF)
+        if number < 3:
+            mask_ref[block] = masked
+            item = peers.copy(1 + number, mask_ref.at[block], x_ref.at[at_rows(here)], block)
+            item.start()
+            outgoing.append(item)
+        else:
+            x_ref[at_rows(here), :] = masked
+    for item in outgoing:
+        item.wait()
+    spectra_rows(table_ref, x_ref, spec_ref, blocks, rows)
+    convolve_spectra(blocks, rows, step, same_ref, filt_ref, spec_ref, out_ref)
+    rim_out_ref[...] = rim_ref[...]
+    x_out_ref[...] = x_ref[...]
+
+    def result(block):
+        return jnp.dot(back_ref[...], out_ref[block], preferred_element_type=F32).astype(BF)
+
+    outgoing = []
+    for number, block in enumerate(peers.blocks):
+        y_ref[block] = result(block)
+        item = peers.copy(4 + number, y_ref.at[block], y_in_ref.at[here], block)
+        item.start()
+        outgoing.append(item)
+    y_in_ref[here] = result(here)
+    for number, block in enumerate((here,) + peers.blocks):
+        if number:
+            outgoing[number - 1].wait()
+        columns = pl.ds(pl.multiple_of(block * group, 128), group)
+        filtered = y_in_ref[block].astype(F32) * valid + bias_ref[:, columns] * signal_ref[block]
+        filtered_ref[:, columns] = filtered
+        gated_ref[:, columns] = (second_ref[block] * filtered).astype(BF)
+
+
+def mix(same, carried, table, back, filt, projected, weights, bias, valid, blocks, rows, number):
+    width = projected.shape[1] // 3
+    group = width // blocks
+    return pl.pallas_call(
+        functools.partial(mix_kernel, blocks, rows, 32),
+        out_shape=(
+            jax.ShapeDtypeStruct((16, 3 * width), BF),
+            jax.ShapeDtypeStruct((blocks * rows, group), BF),
+            jax.ShapeDtypeStruct((rows, width), F32),
+            jax.ShapeDtypeStruct((rows, width), BF),
+        ),
+        in_specs=[SMEM_SPEC] * 2 + [VMEM_SPEC] * 7,
+        out_specs=(VMEM_SPEC,) * 4,
+        scratch_shapes=[
+            pltpu.VMEM((16, 3 * width), BF),
+            pltpu.VMEM((blocks * rows, group), BF),
+            pltpu.VMEM((blocks, rows, group), BF),
+            pltpu.VMEM((blocks, rows, group), F32),
+            pltpu.VMEM((blocks, rows, group), F32),
+            pltpu.VMEM((blocks, 2 * rows, group), F32),
+            pltpu.VMEM((blocks, 2 * rows, group), BF),
+            pltpu.VMEM((blocks, rows, group), BF),
+            pltpu.VMEM((blocks, rows, group), BF),
+            pltpu.SemaphoreType.DMA((7,)),
+            pltpu.SemaphoreType.DMA((7,)),
+        ],
+        compiler_params=pltpu.CompilerParams(
+            collective_id=number, has_side_effects=True, vmem_limit_bytes=KERNEL_BYTES
+        ),
+        name="mix",
+        cost_estimate=lasting(22),
+    )(same, carried, table, back, filt, projected, weights, bias, valid)
+
+
+def unmix_kernel(
+    blocks, rows, step, same_ref, carried_ref, table_ref, back_ref, scale_ref, filt_ref, proj_ref, rim_ref, weight_ref,
+    bias_ref, valid_ref, x_ref, filtered_ref, gate_ref,
+    dproj_ref, dweight_ref, dbias_ref, dt_ref,
+    g_ref, mask_ref, signal_ref, spec_ref, grad_ref, out_ref, tap_ref, dx_ref, dx_in_ref, edge_ref, edge_in_ref, end_ref,
+    send, recv,
+):
+    peers = Peers(send, recv)
+    here, width = peers.here, proj_ref.shape[1] // 3
+    group = width // blocks
+    carried, valid = carried_ref[0], valid_ref[...]
+
+    def at_rows(block):
+        return pl.ds(pl.multiple_of(block * rows, rows), rows)
+
+    def columns_of(which, block):
+        return pl.ds(pl.multiple_of(which * width + block * group, 128), group)
+
+    def part(which, block):
+        return mixed_part(proj_ref, rim_ref, weight_ref, carried, columns_of(which, block))
+
+    outgoing = []
+    for number, block in enumerate(peers.blocks + (here,)):
+        columns = columns_of(0, block)
+        signal = part(0, block)[0] * part(2, block)[0]
+        through = gate_ref[:, columns].astype(F32) * part(1, block)[0]
+        dbias_ref[:, columns] = jnp.sum(through * signal, axis=0, keepdims=True)
+        signal_ref[block] = bias_ref[:, columns] * through
+        masked = (through * valid).astype(BF)
+        if number < 3:
+            mask_ref[block] = masked
+            item = peers.copy(number, mask_ref.at[block], g_ref.at[at_rows(here)], block)
+            item.start()
+            outgoing.append(item)
+        else:
+            g_ref[at_rows(here), :] = masked
+    spectra_rows(table_ref, x_ref, spec_ref, blocks, rows)
+    for item in outgoing:
+        item.wait()
+    spectra_rows(table_ref, g_ref, grad_ref, blocks, rows)
+    correlate_spectra(blocks, rows, step, same_ref, scale_ref, filt_ref, spec_ref, grad_ref, out_ref, tap_ref)
+
+    def result(block):
+        return jnp.dot(back_ref[...], out_ref[block], preferred_element_type=F32).astype(BF)
+
+    outgoing = []
+    for number, block in enumerate(peers.blocks):
+        dx_ref[block] = result(block)
+        item = peers.copy(3 + number, dx_ref.at[block], dx_in_ref.at[here], block)
+        item.start()
+        outgoing.append(item)
+    dx_in_ref[here] = result(here)
+    taps_back(blocks, rows, back_ref, scale_ref, tap_ref, dt_ref)
+    tail = end_ref.shape[0]
+    for number, block in enumerate((here,) + peers.blocks):
+        if number:
+            outgoing[number - 1].wait()
+        d_signal = dx_in_ref[block].astype(F32) * valid + signal_ref[block]
+        gate = gate_ref[:, columns_of(0, block)].astype(F32)
+        first, third = part(0, block), part(2, block)
+        second_views = part(1, block)
+        d_parts = (d_signal * third[0], gate * filtered_ref[:, columns_of(0, block)], d_signal * first[0])
+        for which, (grad, views) in enumerate(zip(d_parts, (first, second_views, third))):
+            columns = columns_of(which, block)
+            weights = [weight_ref[k : k + 1, columns] for k in range(3)]
+            for k in range(3):
+                dweight_ref[k : k + 1, columns] = jnp.sum(grad * views[1 + k], axis=0, keepdims=True)
+            back_one, back_two = advanced(grad, 1), advanced(grad, 2)
+            d_proj = weights[0] * grad + weights[1] * back_one + weights[2] * back_two
+            dproj_ref[:, columns] = d_proj.astype(BF)
+            end_ref[:, columns] = d_proj[rows - tail :, :]
+            head = grad[0:8, :]
+            index = lax.broadcasted_iota(jnp.int32, head.shape, 0)
+            row_zero, row_one = grad[0:1, :], grad[1:2, :]
+            older = weights[2] * row_zero
+            newer = weights[1] * row_zero + weights[2] * row_one
+            edge = jnp.where(index == 6, older, jnp.where(index == 7, newer, 0.0))
+            edge_ref[:, columns] = edge * carried
+    edge_copy = peers.copy(6, edge_ref, edge_in_ref, (here + 3) % 4)
+    edge_copy.start()
+    edge_copy.wait()
+    ending = end_ref[...]
+    extra = jnp.concatenate([jnp.zeros((tail - 8, 3 * width), F32), edge_in_ref[...]], axis=0)
+    dproj_ref[pl.ds(rows - tail, tail), :] = (ending + extra).astype(BF)
+
+
+def unmix(same, carried, table, back, scale, filt, projected, rim, weights, bias, valid, x_cols, filtered, gate, blocks, rows, number):
+    width = projected.shape[1] // 3
+    group = width // blocks
+    return pl.pallas_call(
+        functools.partial(unmix_kernel, blocks, rows, 32),
+        out_shape=(
+            jax.ShapeDtypeStruct((rows, 3 * width), BF),
+            jax.ShapeDtypeStruct((3, 3 * width), F32),
+            jax.ShapeDtypeStruct((1, width), F32),
+            jax.ShapeDtypeStruct((blocks * rows, group), F32),
+        ),
+        in_specs=[SMEM_SPEC] * 2 + [VMEM_SPEC] * 12,
+        out_specs=(VMEM_SPEC,) * 4,
+        scratch_shapes=[
+            pltpu.VMEM((blocks * rows, group), BF),
+            pltpu.VMEM((blocks, rows, group), BF),
+            pltpu.VMEM((blocks, rows, group), F32),
+            pltpu.VMEM((blocks, 2 * rows, group), F32),
+            pltpu.VMEM((blocks, 2 * rows, group), F32),
+            pltpu.VMEM((blocks, 2 * rows, group), BF),
+            pltpu.VMEM((blocks, 2 * rows, group), F32),
+            pltpu.VMEM((blocks, rows, group), BF),
+            pltpu.VMEM((blocks, rows, group), BF),
+            pltpu.VMEM((8, 3 * width), F32),
+            pltpu.VMEM((8, 3 * width), F32),
+            pltpu.VMEM((16, 3 * width), F32),
+            pltpu.SemaphoreType.DMA((7,)),
+            pltpu.SemaphoreType.DMA((7,)),
+        ],
+        compiler_params=pltpu.CompilerParams(
+            collective_id=number, has_side_effects=True, vmem_limit_bytes=KERNEL_BYTES
+        ),
+        name="unmix",
+        cost_estimate=lasting(28),
+    )(same, carried, table, back, scale, filt, projected, rim, weights, bias, valid, x_cols, filtered, gate)
 
 
 def convolve(same, table, back, filt, x_cols, blocks, rows):
@@ -226,17 +512,15 @@
     return lax.ppermute(block, "section", [(0, 1), (1, 0)])
 
 
-MESH = pl.DeviceIdType.MESH
-
-
 def shared_rows(rows):
     return rows // 48 * 16 if rows >= 96 else 0
 
 
-def gather_kernel(sizes, count, *refs):
-    total = len(sizes)
-    own_refs, out_refs = refs[:total], refs[total : 2 * total]
-    send, recv, local = refs[2 * total :]
+def gather_kernel(chunks, heights, count, *refs):
+    total, arrays = len(chunks), len(heights)
+    own_refs, out_refs = refs[:arrays], refs[arrays : 2 * arrays]
+    send, recv, local, stage = refs[2 * arrays :]
+    sizes = [chunk[2] for chunk in chunks]
     core, here, plane = lax.axis_index("section"), lax.axis_index("seq"), lax.axis_index("dp")
     by_x, by_y, far = here + 1 - 2 * (here % 2), (here + 2) % 4, 3 - here
     odd = plane % 2
@@ -248,8 +532,13 @@
     pl.semaphore_wait(barrier, 4)
 
     def window(m, block, start, length):
-        first = (core * count + block) * sizes[m] + start
-        return out_refs[m].at[pl.ds(pl.multiple_of(first, 16), length)]
+        which, base, _, left, wide = chunks[m]
+        first = (core * count + block) * heights[which] + base + start
+        return out_refs[which].at[pl.ds(pl.multiple_of(first, 16), length), pl.ds(left, wide)]
+
+    def own_window(m, start, length):
+        which, base, _, left, wide = chunks[m]
+        return own_refs[which].at[pl.ds(pl.multiple_of(base + start, 16), length), pl.ds(left, wide)]
 
     def copy(kind, m, source, target_ref, target):
         return pltpu.make_async_remote_copy(
@@ -269,8 +558,7 @@
         return item
 
     def from_own(kind, m, start, length, target):
-        source = own_refs[m].at[pl.ds(pl.multiple_of(start, 16), length)]
-        return go(copy(kind, m, source, window(m, here, start, length), target))
+        return go(copy(kind, m, own_window(m, start, length), window(m, here, start, length), target))
 
     kept, thirds, lows, begins = [], [], [], []
     for m in range(total):
@@ -320,16 +608,20 @@
 
     first_hop(0)
     first_hop(1)
-    locals_ = []
+    def through(m, out):
+        held = stage.at[m, pl.ds(0, sizes[m])]
+        source, target = (held, window(m, here, 0, sizes[m])) if out else (own_window(m, 0, sizes[m]), held)
+        return pltpu.make_async_copy(source, target, local.at[m])
+
     for m in range(total):
-        mine = pltpu.make_async_copy(own_refs[m], window(m, here, 0, sizes[m]), local.at[m])
-        mine.start()
-        locals_.append(mine)
+        through(m, False).start()
     for m in range(total):
         second_hop(m)
         if m + 2 < total:
             first_hop(m + 2)
         kept.append(from_own(13, m, 0, sizes[m], to_core))
+        through(m, False).wait()
+        through(m, True).start()
         if m >= 1:
             third_hop(m - 1)
         if m >= 2:
@@ -337,8 +629,8 @@
     third_hop(total - 1)
     for m in range(max(total - 2, 0), total):
         last_hop(m)
-    for mine in locals_:
-        mine.wait()
+    for m in range(total):
+        through(m, True).wait()
     for item in kept:
         item.wait_recv()
     for item in started:
@@ -356,19 +648,28 @@
             low = jnp.where(core == 0, whole, other)
             result.append(jnp.concatenate([low, jnp.where(core == 0, other, whole)], axis=0))
         return result
-    sizes = [shard.shape[0] for shard in shards]
+    heights = [shard.shape[0] for shard in shards]
+    chunks = []
+    for which, shard in enumerate(shards):
+        high, wide = min(shard.shape[0], 256), min(shard.shape[1], 1024)
+        for base in range(0, shard.shape[0], high):
+            chunks += [(which, base, high, left, wide) for left in range(0, shard.shape[1], wide)]
     return pl.pallas_call(
-        functools.partial(gather_kernel, sizes, count),
+        functools.partial(gather_kernel, chunks, heights, count),
         out_shape=[jax.ShapeDtypeStruct((2 * count * a.shape[0], a.shape[1]), a.dtype) for a in shards],
         in_specs=[pl.BlockSpec(memory_space=pl.ANY)] * len(shards),
         out_specs=[pl.BlockSpec(memory_space=pl.ANY)] * len(shards),
         scratch_shapes=[
-            pltpu.SemaphoreType.DMA((14, len(shards))),
-            pltpu.SemaphoreType.DMA((14, len(shards))),
-            pltpu.SemaphoreType.DMA((len(shards),)),
+            pltpu.SemaphoreType.DMA((14, len(chunks))),
+            pltpu.SemaphoreType.DMA((14, len(chunks))),
+            pltpu.SemaphoreType.DMA((len(chunks),)),
+            pltpu.VMEM((len(chunks), max(c[2] for c in chunks), max(c[4] for c in chunks)), shards[0].dtype),
         ],
-        compiler_params=pltpu.CompilerParams(collective_id=0, has_side_effects=True),
+        compiler_params=pltpu.CompilerParams(
+            collective_id=0, has_side_effects=True, vmem_limit_bytes=KERNEL_BYTES
+        ),
         name="gather_shards",
+        cost_estimate=lasting(190),
     )(*shards)
 
 
@@ -382,18 +683,24 @@
 
 X_FIRST = (0, 2, 1, 3)
 Y_FIRST = (0, 1, 2, 3)
-
-
-def reduce_kernel(items, halves, planes, *refs):
-    total = len(items)
+PARTS = 4
+
+
+def reduce_kernel(items, rest, halves, planes, order, *refs):
+    whole = len(items)
+    total = whole + len(rest)
     sides = len(halves) * 2 + 1
-    inputs, refs = refs[:sides], refs[sides:]
-    own_out, refs = refs[:total], refs[total:]
-    other_out, refs = (refs[:total], refs[total:]) if planes else (own_out, refs)
-    hold, inbox, far_in, near_in, plane_in, cross_in, refs = (
-        refs[:total], refs[total : 2 * total], refs[2 * total : 3 * total], refs[3 * total : 4 * total],
-        refs[4 * total : 5 * total], refs[5 * total : 6 * total], refs[6 * total :],
-    )
+
+    def take(number):
+        nonlocal refs
+        first, refs = refs[:number], refs[number:]
+        return first
+
+    inputs, rest_in = take(sides), take(len(rest))
+    own_out = take(total)
+    other_out = dict(zip(planes, take(len(planes))))
+    hold, inbox, far_in, near_in = take(total), take(whole), take(whole), take(whole)
+    plane_in, cross_in = dict(zip(planes, take(len(planes)))), dict(zip(planes, take(len(planes))))
     send, recv, local = refs
     core, here, plane = lax.axis_index("section"), lax.axis_index("seq"), lax.axis_index("dp")
     by_x, by_y, far = here + 1 - 2 * (here % 2), (here + 2) % 4, 3 - here
@@ -432,13 +739,16 @@
             device_id=target, device_id_type=MESH,
         )
 
+    heights = [item[0] for item in items] + [shape[0] for shape in rest]
+
     def rows_of(ref, m, slot, slots=1):
-        rows = items[m][0]
+        rows = heights[m]
         return ref[m].at[pl.ds(slot * rows, slots * rows)]
 
     def copies(m):
-        along_x = items[m][5] == X_FIRST
+        along_x = m < whole and items[m][5] == X_FIRST
         return dict(
+            load=lambda: pltpu.make_async_copy(rest_in[m - whole], hold[m], local.at[m]),
             core=lambda: copy(0, m, hold[m], inbox[m], to_core),
             far=lambda: copy(1, m, rows_of(hold, m, 2, 2), far_in[m], to_x if along_x else to_y),
             near=lambda: copy(2, m, rows_of(hold, m, 1), near_in[m], to_y if along_x else to_x),
@@ -479,7 +789,7 @@
         lax.fori_loop(0, rows // high * across, step, 0)
 
     def add_plane(m, ref):
-        rows = items[m][0]
+        rows = heights[m]
         high = min(rows, 64)
 
         def step(index, carry):
@@ -495,21 +805,25 @@
             fill(m, slot, 1 - core, [])
         moves[m]["core"]().start()
 
-    def first_hop(m):
+    def prepare(m):
         moves[m]["core"]().wait()
         for slot in (2, 3):
             fill(m, slot, core, [(inbox, slot)])
+
+    def first_hop(m):
         moves[m]["far"]().start()
 
+    def landed(m):
+        moves[m]["far"]().wait_recv()
+
     def second_hop(m):
-        moves[m]["far"]().wait_recv()
         fill(m, 1, core, [(inbox, 1), (far_in, 1)])
         moves[m]["near"]().start()
 
     def arrive(m):
         moves[m]["near"]().wait_recv()
         fill(m, 0, core, [(inbox, 0), (far_in, 0), (near_in, 0)])
-        if planes:
+        if m in planes:
 
             @pl.when(outer)
             def _():
@@ -540,20 +854,28 @@
             moves[m]["last_got"]().start()
             moves[m]["got"]().start()
 
-    stages = [to_other_core, first_hop, second_hop, arrive]
-    if planes:
-        stages = stages + [meet, settle, finish]
-    for when in range(total // 2 + len(stages) - 1):
-        for number in reversed(range(len(stages))):
-            pair = when - number
-            if 0 <= pair < total // 2:
-                stages[number](2 * pair)
-                stages[number](2 * pair + 1)
+    def begin(m):
+        moves[m]["load"]().wait()
+
+        @pl.when(outer)
+        def _():
+            moves[m]["inward"]().start()
+
+    names = dict(
+        core=to_other_core, fill=prepare, go=first_hop, wait=landed, turn=second_hop, own=arrive, meet=meet, settle=settle,
+        finish=finish, load=begin,
+    )
+    for m in range(whole, total):
+        moves[m]["load"]().start()
+    for step, pair in order:
+        for m in (2 * pair, 2 * pair + 1):
+            names[step](m)
 
     for m in range(total):
-        moves[m]["far"]().wait_send()
-        moves[m]["near"]().wait_send()
-        if planes:
+        if m < whole:
+            moves[m]["far"]().wait_send()
+            moves[m]["near"]().wait_send()
+        if m in planes:
 
             @pl.when(inner)
             def _():
@@ -569,7 +891,36 @@
             moves[m]["held"]().wait()
 
 
-def reduce_layer(lefts, rights, packed, planes, number):
+def reduce_order(pairs, summed, rest):
+    steps = [("load", k) for k in rest] + [("core", pairs[0]), ("fill", pairs[0]), ("go", pairs[0])]
+    steps += [("core", k) for k in pairs[1:3]] + [("fill", pairs[1])]
+    groups = [list(rest)] + [[pair] if pair in summed else [] for pair in pairs]
+
+    def at(name, number):
+        if 0 <= number < len(groups):
+            steps.extend((name, k) for k in groups[number])
+
+    for i, pair in enumerate(pairs):
+        steps.append(("wait", pair))
+        if i + 1 < len(pairs):
+            steps.append(("go", pairs[i + 1]))
+        steps.append(("turn", pair))
+        if i + 3 < len(pairs):
+            steps.append(("core", pairs[i + 3]))
+        if i + 2 < len(pairs):
+            steps.append(("fill", pairs[i + 2]))
+        at("meet", i)
+        steps.append(("own", pair))
+        at("settle", i - 1)
+        at("finish", i - 2)
+    for i in range(len(pairs), len(pairs) + 3):
+        at("meet", i)
+        at("settle", i - 1)
+        at("finish", i - 2)
+    return steps
+
+
+def reduce_layer(lefts, rights, packed, rest, planes, order, number):
     count = lax.axis_size("seq")
     halves = [right.shape[1] // 2 for right in rights]
     small_rows, small_width = packed.shape[0] // count, packed.shape[1] // 2
@@ -579,48 +930,61 @@
         (small_rows, small_width, -1, -1, 0, Y_FIRST),
         (enter, halves[2] // 2, 2, 2, 0, X_FIRST),
         (enter, halves[2] // 2, 2, 2, halves[2] // 2, Y_FIRST),
-        (up, halves[0] // 2, 0, 0, 0, X_FIRST),
-        (down, halves[1] // 2, 1, 1, 0, Y_FIRST),
-        (up, halves[0] // 2, 0, 0, halves[0] // 2, X_FIRST),
-        (down, halves[1] // 2, 1, 1, halves[1] // 2, Y_FIRST),
     ]
-    shapes = [jax.ShapeDtypeStruct((item[0], item[1]), BF) for item in items]
-
-    def buffers(slots):
-        return [pltpu.VMEM((slots * item[0], item[1]), BF) for item in items]
+    for part in range(PARTS):
+        items += [
+            (up, halves[0] // PARTS, 0, 0, part * halves[0] // PARTS, X_FIRST),
+            (down, halves[1] // PARTS, 1, 1, part * halves[1] // PARTS, Y_FIRST),
+        ]
+    pieces = [item[:2] for item in items] + [piece.shape for piece in rest]
+
+    def buffers(slots, shapes):
+        return [pltpu.VMEM((slots * shape[0], shape[1]), BF) for shape in shapes]
 
     hbm = pl.BlockSpec(memory_space=pl.ANY)
-    total = len(items)
-    outs = 2 if planes else 1
+    whole, total = len(items), len(pieces)
+    planes = list(planes) + list(range(whole, total))
+    across = [pieces[m] for m in planes]
+    scratch = buffers(4, pieces[:whole]) + buffers(1, pieces[whole:])
+    for slots in (4, 2, 1):
+        scratch += buffers(slots, pieces[:whole])
+    scratch += buffers(1, across) + buffers(1, across)
+    semaphores = [pltpu.SemaphoreType.DMA((6, total)), pltpu.SemaphoreType.DMA((6, total)), pltpu.SemaphoreType.DMA((total,))]
     result = pl.pallas_call(
-        functools.partial(reduce_kernel, items, halves, planes),
-        out_shape=shapes * outs,
-        in_specs=[VMEM_SPEC] * (2 * len(lefts) + 1),
-        out_specs=[hbm] * (outs * total),
-        scratch_shapes=buffers(4) + buffers(4) + buffers(2) + buffers(1) + buffers(1) + buffers(1)
-        + [pltpu.SemaphoreType.DMA((6, total)), pltpu.SemaphoreType.DMA((6, total)), pltpu.SemaphoreType.DMA((total,))],
+        functools.partial(reduce_kernel, items, pieces[whole:], halves, planes, order),
+        out_shape=[jax.ShapeDtypeStruct(shape, BF) for shape in pieces + across],
+        in_specs=[VMEM_SPEC] * (2 * len(lefts) + 1) + [hbm] * len(rest),
+        out_specs=[hbm] * (total + len(planes)),
+        scratch_shapes=scratch + semaphores,
         compiler_params=pltpu.CompilerParams(
-            collective_id=number, has_side_effects=True, vmem_limit_bytes=58 * 1024 * 1024
+            collective_id=number, has_side_effects=True, vmem_limit_bytes=60 * 1024 * 1024
         ),
         name="reduce_layer",
-    )(*lefts, *rights, packed)
-    joined = []
-    for part in range(outs):
-        out, small, in_low, in_high, up_low, down_low, up_high, down_high = result[part * total : (part + 1) * total]
-        pairs = ((up_low, up_high), (down_low, down_high), (in_low, in_high))
-        joined.append([jnp.concatenate(pair, axis=1) for pair in pairs] + [out, small])
-    return joined
+        cost_estimate=lasting(150),
+    )(*lefts, *rights, packed, *rest)
+    return result[:total], dict(zip(planes, result[total:]))
+
+
+def join_pieces(pieces):
+    ups, downs = pieces[4::2], pieces[5::2]
+    return [jnp.concatenate(group, axis=1) for group in (ups, downs, pieces[2:4])] + list(pieces[:2])
 
 
 def reduce_plain(lefts, rights, packed, core):
+    count = lax.axis_size("seq")
+    chips = []
+    for left, right in zip(lefts, rights):
+        keep, send = core_halves(core, right)
+        chips.append(dot(left, keep) + core_swap(dot(left, send).astype(BF)).astype(F32))
+    keep, send = core_halves(core, packed)
+    small = (keep + core_swap(send.astype(BF)).astype(F32)).astype(BF)
+    up, down, enter, leave = (chip.astype(BF) for chip in chips)
+    out_rows, half = leave.shape[0] // count, leave.shape[1]
+    leave = jnp.concatenate([leave.reshape(count, out_rows, half), small.reshape(count, -1, half)], axis=1)
     own = []
-    for left, right in [*zip(lefts, rights), (None, packed)]:
-        full = right if left is None else dot(left, right)
-        keep, send = core_halves(core, full.astype(BF))
-        chip = (keep.astype(F32) + core_swap(send).astype(F32)).astype(BF)
-        summed = lax.psum_scatter(chip, "seq", scatter_dimension=0, tiled=True)
-        own.append(lax.psum(summed, "dp"))
-    return own
+    for chip in (up, down, enter, leave.reshape(-1, half)):
+        own.append(lax.psum(lax.psum_scatter(chip, "seq", scatter_dimension=0, tiled=True), "dp"))
+    return own[:3] + [own[3][:out_rows], own[3][out_rows:]]
 
 
 def body(
@@ -631,6 +995,7 @@
     count = lax.axis_size("seq")
     here = lax.axis_index("seq")
     core = lax.axis_index("section")
+    routed = count == 4 and lax.axis_size("dp") == 4
     slots = rows * count
     col_width = width // count
     hidden = mlp_up.shape[2]
@@ -710,28 +1075,33 @@
         filt, pull = filter_stage(layer)
         normed = layer_norm(layer_in, gain_one).astype(BF)
         projected = dot(normed, in_matrix).astype(BF)
-        rim = shifted(projected[rows - 2 :], "seq", 1)
-        mixed = short_mix(rim.astype(F32), projected.astype(F32), short_weights, carried_on)
-        first, second, third = mixed[:, :width], mixed[:, width : 2 * width], mixed[:, 2 * width :]
-        signal = first * third
-        x_cols = to_columns(signal * valid)
-        y_cols = convolve(same, table, back, filt, x_cols, count, rows)
-        filtered = to_rows(y_cols) * valid + bias * signal
-        gated = (second * filtered).astype(BF)
+        if routed:
+            rim, x_cols, filtered, gated = mix(
+                same, carried_on.reshape(1), table, back, filt, projected, short_weights, bias[None], valid, count, rows, 3 + layer
+            )
+        else:
+            rim = shifted(projected[rows - 2 :], "seq", 1)
+            mixed = short_mix(rim.astype(F32), projected.astype(F32), short_weights, carried_on)
+            first, second, third = mixed[:, :width], mixed[:, width : 2 * width], mixed[:, 2 * width :]
+            signal = first * third
+            x_cols = to_columns(signal * valid)
+            y_cols = convolve(same, table, back, filt, x_cols, count, rows)
+            filtered = to_rows(y_cols) * valid + bias * signal
+            gated = (second * filtered).astype(BF)
         residual = layer_in + dot(gated, out_matrix)
         normed_two = layer_norm(residual, gain_two).astype(BF)
         upward = dot(normed_two, up_matrix)
         active = gelu_tanh(upward).astype(BF)
         layer_out = residual + dot(active, down_matrix)
         stored = (
-            layer_in, normed, projected, rim, mixed, signal, filtered, gated, residual, normed_two,
+            layer_in, normed, projected, rim, filtered, gated, residual, normed_two,
             upward, active, x_cols, filt, pull,
         )
         return layer_out.astype(BF), stored
 
     def backward(upstream, stored, layer):
         (
-            layer_in, normed, projected, rim, mixed, signal, filtered, gated, residual, normed_two,
+            layer_in, normed, projected, rim, filtered, gated, residual, normed_two,
             upward, active, x_cols, filt, pull,
         ) = stored
         gain_one, short_weights, in_w, shift_w, freq_w, out_w, decay_w, bias, gain_two = small_of(layer)
@@ -742,22 +1112,31 @@
         grad_residual = upstream.astype(F32) + grad_resid_norm
         grad_branch = grad_residual.astype(BF)
         grad_gated = dot_right(grad_branch, out_matrix)
-        first, second, third = mixed[:, :width], mixed[:, width : 2 * width], mixed[:, 2 * width :]
-        grad_second = grad_gated * filtered
-        grad_filtered = grad_gated * second
-        grad_bias = jnp.sum(grad_filtered * signal, axis=0)
-        g_cols = to_columns(grad_filtered * valid)
-        dx_cols, grad_taps = correlate(same, table, back, scale, filt, x_cols, g_cols, count, rows)
-        grad_signal = to_rows(dx_cols) * valid + bias * grad_filtered
-        grad_mixed = jnp.concatenate([grad_signal * third, grad_second, grad_signal * first], axis=1)
-        short_pull = jax.vjp(
-            lambda a, b, c: short_mix(a, b, c, carried_on), rim.astype(F32), projected.astype(F32), short_weights
-        )[1]
-        grad_rim, grad_proj, grad_short = short_pull(grad_mixed)
-        returned = shifted(grad_rim, "seq", -1)
-        tail = grad_proj[rows - 2 :] + returned
-        grad_proj = jnp.concatenate([grad_proj[: rows - 2], tail], axis=0)
-        grad_proj = grad_proj.astype(BF)
+        if routed:
+            grad_proj, grad_short, grad_bias, grad_taps = unmix(
+                same, carried_on.reshape(1), table, back, scale, filt, projected, rim, short_weights, bias[None], valid,
+                x_cols, filtered, grad_gated, count, rows, 5 + layer,
+            )
+            grad_bias = grad_bias[0]
+        else:
+            mixed = short_mix(rim.astype(F32), projected.astype(F32), short_weights, carried_on)
+            first, second, third = mixed[:, :width], mixed[:, width : 2 * width], mixed[:, 2 * width :]
+            signal = first * third
+            grad_second = grad_gated * filtered
+            grad_filtered = grad_gated * second
+            grad_bias = jnp.sum(grad_filtered * signal, axis=0)
+            g_cols = to_columns(grad_filtered * valid)
+            dx_cols, grad_taps = correlate(same, table, back, scale, filt, x_cols, g_cols, count, rows)
+            grad_signal = to_rows(dx_cols) * valid + bias * grad_filtered
+            grad_mixed = jnp.concatenate([grad_signal * third, grad_second, grad_signal * first], axis=1)
+            short_pull = jax.vjp(
+                lambda a, b, c: short_mix(a, b, c, carried_on), rim.astype(F32), projected.astype(F32), short_weights
+            )[1]
+            grad_rim, grad_proj, grad_short = short_pull(grad_mixed)
+            returned = shifted(grad_rim, "seq", -1)
+            tail = grad_proj[rows - 2 :] + returned
+            grad_proj = jnp.concatenate([grad_proj[: rows - 2], tail], axis=0)
+            grad_proj = grad_proj.astype(BF)
         grad_normed = dot_right(grad_proj, in_matrix)
         grad_norm_in, grad_gain_one = jax.vjp(layer_norm, layer_in, gain_one)[1](grad_normed)
         grad_layer_in = (grad_residual + grad_norm_in).astype(BF)
@@ -784,18 +1163,26 @@
     out_first, stored_first = forward(row_of(tokens).astype(F32), 0)
     out_second, stored_second = forward(out_first.astype(F32), 1)
     grad_second, factors_second = backward(row_of(out_grad), stored_second, 1)
-    routed = count == 4 and lax.axis_size("dp") == 4
     if routed:
-        own_second = [lax.psum(part, "dp") for part in reduce_layer(*factors_second, False, 1)[0]]
+        whole, held_back = 4 + 2 * PARTS, 2
+        ready = whole - 2 * held_back
+        pairs = [1, *range(2, 2 + PARTS - held_back), 0, *range(2 + PARTS - held_back, 2 + PARTS)]
+        order = reduce_order(pairs, range(ready // 2), [])
+        own_second, other_second = reduce_layer(*factors_second, [], range(ready), order, 1)
+        grad_first, factors_first = backward(grad_second, stored_first, 0)
+        order = reduce_order([1, *range(2, 2 + PARTS), 0], range(whole // 2), range(whole // 2, whole // 2 + held_back))
+        own_first, other_first = reduce_layer(*factors_first, own_second[ready:], range(whole), order, 2)
+        other_second = [other_second[m] for m in range(ready)] + [other_first[m] for m in range(whole, whole + 2 * held_back)]
+        own_second = list(own_second[:ready]) + list(own_first[whole:])
+        own_first, other_first = own_first[:whole], [other_first[m] for m in range(whole)]
+        own_first, own_second, other_first, other_second = (
+            join_pieces(part) for part in (own_first, own_second, other_first, other_second)
+        )
     else:
         own_second = reduce_plain(*factors_second, core)
-    grad_first, factors_first = backward(grad_second, stored_first, 0)
-    if routed:
-        own_first, other_first = reduce_layer(*factors_first, True, 2)
-    else:
+        grad_first, factors_first = backward(grad_second, stored_first, 0)
         own_first = reduce_plain(*factors_first, core)
-        other_first = [lax.ppermute(part, "section", [(1, 0)]) for part in own_first]
-    other_second = [lax.ppermute(part, "section", [(0, 1)]) for part in own_second]
+        other_first, other_second = ([core_swap(part) for part in own] for own in (own_first, own_second))
 
     def both_rows(of_first, of_second):
         kept = jnp.where(core == 0, of_first, of_second)

time: 927 us -> 786 us (0.85)
  Pallas kernels: 521 us -> 580 us
  starting transfers between devices: 54.2 us -> 0.01 us
  local copies, waits for them, and re-layouts: 97.9 us -> 46.2 us
  other arithmetic: 81 us -> 50.3 us
  blocking collectives: 20 us -> 0 us
  waiting for transfers between devices: 18 us -> 0.01 us
  between operations: 19.2 us -> 4.7 us
  matrix products: 105 us -> 94.4 us
    pallas_call x7, Pallas kernels: 521 us -> 580 us  [the longest x2 312 us: reduce_layer(): pl.pallas_call(functools.partial(reduce_kernel, items, pieces[whole:], ha...]
    all_to_all x8 -> x0, starting transfers between devices: 34.9 us -> none  [the longest x4 17.8 us: to_columns(): lax.all_to_all(values.astype(BF), 'seq', split_axis=1, concat_axis=0, til...]
    unnamed x398 -> x196, local copies, waits for them, and re-layouts: 42.9 us -> 9.8 us
    psum x1 -> x0, blocking collectives: 20 us -> none  [body(): lax.psum(part, 'dp')]
    ppermute x9 -> x0, starting transfers between devices: 18.7 us -> none  [the longest x4 9.68 us: shifted(): return lax.ppermute(block, axis, route)]
    all_to_all x8 -> x0, waiting for transfers between devices: 11.5 us -> none  [the longest x4 6.9 us: to_rows(): lax.all_to_all(values, 'seq', split_axis=0, concat_axis=1, tiled=True)]
    add x2 -> x0, other arithmetic: 9.73 us -> none  [short_mix(): weight_values[0] * extended[2:]]
  transfers between devices with their start and end apart: 20 -> 2, of which waited for: 6 -> 0; matrix products, arithmetic and copies ran while one was open for 12% -> 16% of each run, Pallas kernels for 34% -> 48%
where the time goes in v3:
time: 786 us; the launch traced here: 776 us
  Pallas kernels  580 us (74%)
  matrix products  94.4 us (12%)
  other arithmetic  50.3 us (6%)
  local copies, waits for them, and re-layouts  46.2 us (6%)
    pallas_call x2, Pallas kernels, reduce_layer(): pl.pallas_call(functools.partial(reduce_kernel, items, pieces[whole:], ha...  312 us
    pallas_call x1, Pallas kernels, gather_shards(): pl.pallas_call(functools.partial(gather_kernel, chunks, heights, count),...  161 us
    pallas_call x2, Pallas kernels, unmix(): pl.pallas_call(functools.partial(unmix_kernel, blocks, rows, 32), out_sha...  56.5 us
    pallas_call x2, Pallas kernels, mix(): pl.pallas_call(functools.partial(mix_kernel, blocks, rows, 32), out_shape...  50.5 us
    dot_general x8, matrix products, dot_right(): lax.dot_general(left, right, (((1,), (1,)), ((), ())), preferred_element_...  40.6 us
    dot_general x8, matrix products, dot(): return jnp.dot(left, right, preferred_element_type=F32)  35.4 us
  transfers between devices with their start and end apart: 2, of which 0 were waited for; matrix products, arithmetic and copies ran while one was open for 16% of the time, Pallas kernels for 48%

profile of v3, /device:TPU:0, one launch (start us, length us, event | category | flops | bytes accessed | tf_op | source)
XLA Modules:
  0.0 775.5 jit_solution(17033117827821249958)
XLA Ops:
  7.2 1.5 concatenate.182
  8.7 1.6 copy-done.4
  10.3 1.4 copy-done.5
  12.7 160.7 %gather_shards.1 = (bf16[256,1024]{1,0:T(8,128)(2,1)S(1)}, bf16[2048,1024]{1,0:T(8,128)(2,1)}, bf16[2048,3072]{1,0:T(8,128)(2,1)}, bf16[2048,4096]{1,0:T(8,128)(2,1)}, bf16[8192,1024]{1,0:T(8,128)(2,1)}) custom-call(bf16[32,1024]{1,0:T(8,128)(2,1)S(1)} %reshape.884.refs_0_, bf16[256,1024]{1,0:T(8,128)(2,1)S(1)} %bitcast.193, ...), custom_call_target="tpu_custom_call" | custom-call | bytes 701100032 | tf_op jit(solution)/shard_map/gather_shards/pallas_call | solution.py:657
  180.0 1.5 fusion.146
  181.5 2.7 multiply_convert_fusion.13
  185.9 1.3 fusion.154.valid_ref
  187.6 1.9 fusion.54.proj_ref
  189.6 2.6 add_multiply_fusion
  192.3 25.7 %mix.2 = (bf16[16,3072]{1,0:T(8,128)(2,1)S(1)}, bf16[1024,256]{1,0:T(8,128)(2,1)S(1)}, f32[256,1024]{1,0:T(8,128)S(1)}, bf16[256,1024]{1,0:T(8,128)(2,1)S(1)}) custom-call(f32[4,4]{1,0:T(4,128)S(1)} %compare_convert_fusion.same_ref, f32[1]{0:T(128)} %bitcast.2.carried_ref, bf16[512,256]{1,0:T(8,128)(2,1)S(1)} %copy-done.3, bf16[256,512]{1,0:T(8,128)(2,1)S(1)} %copy-done.2, ...), custom_call_target="tpu_custom_call" | custom-call | bytes 81180000 | tf_op jit(solution)/shard_map/mix/pallas_call | solution.py:314
  219.2 6.0 fusion.14
  225.1 7.8 %convert_reduce_fusion = (f32[256]{0:T(256)S(1)}, bf16[256,1024]{1,0:T(8,128)(2,1)S(1)}) fusion(f32[256,1024]{1,0:T(8,128)S(1)} %get-tuple-element.237, bf16[8192,1024]{1,0:T(8,128)(2,1)} %get-tuple-element.93, f32[256,4096]{1,0:T(8,128)S(1)} %fusion.14), kind=kOutput, calls=%fused_computation.93 | convolution fusion | flops 2157969152 | bytes 14156800 | tf_op jit(solution)/shard_map/dot_general | solution.py:20
  233.3 1.9 fusion.57.proj_ref
  235.3 24.8 %mix.3 = (bf16[16,3072]{1,0:T(8,128)(2,1)S(1)}, bf16[1024,256]{1,0:T(8,128)(2,1)S(1)}, f32[256,1024]{1,0:T(8,128)S(1)}, bf16[256,1024]{1,0:T(8,128)(2,1)S(1)}) custom-call(f32[4,4]{1,0:T(4,128)S(1)} %compare_convert_fusion.same_ref, f32[1]{0:T(128)} %bitcast.2.carried_ref, bf16[512,256]{1,0:T(8,128)(2,1)S(1)} %copy-done.3, bf16[256,512]{1,0:T(8,128)(2,1)S(1)} %copy-done.2, ...), custom_call_target="tpu_custom_call" | custom-call | bytes 81180000 | tf_op jit(solution)/shard_map/mix/pallas_call | solution.py:314
  260.1 2.4 fusion.195
  262.8 5.8 fusion.6
  268.6 8.7 %broadcast_select_fusion.2 = (bf16[256,1024]{1,0:T(8,128)(2,1)}, bf16[256,1024]{1,0:T(8,128)(2,1)}) fusion(bf16[256,1024]{1,0:T(8,128)(2,1)S(1)} %get-tuple-element.239, pred[]{:T(512)S(6)} %eq.20, f32[256,1024]{1,0:T(8,128)S(1)} %get-tuple-element.241, bf16[8192,1024]{1,0:T(8,128)(2,1)} %get-tuple-element.93, f32[256,4096]{1,0:T(8,128)S(1)} %fusion.6), kind=kOutput, calls=%fused_computation.182 | convolution fusion | flops 2157707264 | bytes 15204353 | tf_op jit(solution)/shard_map/dot_general | solution.py:20
  277.4 7.7 fusion.37.refs_4_
  285.1 6.7 multiply_reduce_fusion
  295.0 29.7 %unmix.2 = (bf16[256,3072]{1,0:T(8,128)(2,1)}, f32[3,3072]{1,0:T(4,128)S(1)}, f32[1,1024]{1,0:T(1,128)S(1)}, f32[1024,256]{1,0:T(8,128)S(1)}) custom-call(f32[4,4]{1,0:T(4,128)S(1)} %compare_convert_fusion.same_ref, f32[1]{0:T(128)} %bitcast.2.carried_ref, bf16[512,256]{1,0:T(8,128)(2,1)S(1)} %copy-done.3, bf16[256,512]{1,0:T(8,128)(2,1)S(1)} %copy-done.2, ...), custom_call_target="tpu_custom_call" | custom-call | bytes 103320000 | tf_op jit(solution)/shard_map/unmix/pallas_call | solution.py:434
  324.8 5.2 fusion.119
  330.6 1.3 fusion.180
  331.9 7.5 fusion.30.refs_4_
  339.4 6.7 multiply_reduce_fusion.2
  346.2 1.2 fusion.188
  349.4 26.8 %unmix.3 = (bf16[256,3072]{1,0:T(8,128)(2,1)}, f32[3,3072]{1,0:T(4,128)S(1)}, f32[1,1024]{1,0:T(1,128)S(1)}, f32[1024,256]{1,0:T(8,128)S(1)}) custom-call(f32[4,4]{1,0:T(4,128)S(1)} %compare_convert_fusion.same_ref, f32[1]{0:T(128)} %bitcast.2.carried_ref, bf16[512,256]{1,0:T(8,128)(2,1)S(1)} %copy-done.3, bf16[256,512]{1,0:T(8,128)(2,1)S(1)} %copy-done.2, ...), custom_call_target="tpu_custom_call" | custom-call | bytes 103320000 | tf_op jit(solution)/shard_map/unmix/pallas_call | solution.py:434
  376.2 5.2 fusion.117
  381.5 1.3 fusion.115
  382.8 1.6 broadcast_select_fusion
  386.4 5.6 copy.62
  392.0 6.0 copy.58
  398.1 4.9 fusion.53.refs_1_
  402.9 2.0 copy.66.refs_0_
  405.0 2.4 multiply_reduce_fusion.8
  407.5 1.7 convolution_dynamic-update-slice_fusion
  412.7 1.4 fusion.142
  414.3 2.1 copy.67.refs_2_
  416.4 4.9 fusion.45.refs_1_
  421.3 3.2 multiply_reduce_fusion.9
  424.5 1.8 multiply_reduce_fusion.1
  427.5 2.3 convolution_dynamic-update-slice_fusion.1
  431.9 1.4 fusion.144
  439.5 144.2 %reduce_layer.2 = (bf16[256,512]{1,0:T(8,128)(2,1)}, bf16[32,512]{1,0:T(8,128)(2,1)}, bf16[256,768]{1,0:T(8,128)(2,1)}, bf16[256,768]{1,0:T(8,128)(2,1)}, bf16[2...) custom-call(bf16[1024,256]{1,0:T(8,128)(2,1)} %copy.66.refs_0_, ...), custom_call_target="tpu_custom_call" | custom-call | bytes 553500032 | tf_op jit(solution)/shard_map/reduce_layer/pallas_call | solution.py:953
  583.7 168.0 %reduce_layer.3 = (bf16[256,512]{1,0:T(8,128)(2,1)}, bf16[32,512]{1,0:T(8,128)(2,1)}, bf16[256,768]{1,0:T(8,128)(2,1)}, bf16[256,768]{1,0:T(8,128)(2,1)}, bf16[2...) custom-call(bf16[1024,256]{1,0:T(8,128)(2,1)} %copy.68.refs_0_, ...), custom_call_target="tpu_custom_call" | custom-call | bytes 553500032 | tf_op jit(solution)/shard_map/reduce_layer/pallas_call | solution.py:953
  758.9 1.7 fusion.122
  761.2 2.6 maximum_convert_fusion.1
  764.6 2.5 maximum_convert_fusion
  767.5 2.0 maximum_convert_fusion.2
  (331 shorter events, 50.6 us)
Async XLA Ops:
  12.7 164.5 %copy-start.19 = (bf16[2,256,1024]{2,1,0:T(8,128)(2,1)S(1)}, bf16[2,256,1024]{2,1,0:T(8,128)(2,1)}, u32[]{:S(2)}) copy-start(bf16[2,256,1024]{2,1,0:T(8,128)(2,1)} %param.20) | copy-start | bytes 3145732
  12.7 166.2 %copy-start.15 = (f32[1024,33]{1,0:T(8,128)S(1)}, f32[1024,33]{1,0:T(8,128)}, u32[]{:S(2)}) copy-start(f32[1024,33]{1,0:T(8,128)} %constant.90.clone) | copy-start | bytes 405508
  177.3 6.9 copy-start.36
  177.7 9.5 %copy-start.79 = (f32[256]{0:T(256)}, f32[256]{0:T(256)S(1)}, u32[]{:S(2)}) copy-start(f32[256]{0:T(256)S(1)} %fusion.164) | copy-start | bytes 3076
  179.0 5.6 copy-start.46
  179.9 5.2 copy-start.24
  181.5 6.1 copy-start.84
  192.3 25.8 %copy-start.85 = (bf16[2048,1024]{1,0:T(8,128)(2,1)S(1)}, bf16[2048,1024]{1,0:T(8,128)(2,1)}, u32[]{:S(2)}) copy-start(bf16[2048,1024]{1,0:T(8,128)(2,1)} %get-tuple-element.91) | copy-start | bytes 12582916
  219.1 14.2 %slice-start.1 = ((s8[12582912]{0:T(1024)(128)(4,1)}), s8[4194304]{0:T(1024)(128)(4,1)S(1)}, s32[]{:S(2)}) async-start(s8[12582912]{0:T(1024)(128)(4,1)} %bitcast.246), calls=%async_computation.1 | async-start | bytes 8388608
  219.1 14.2 %slice-start.2 = ((s8[12582912]{0:T(1024)(128)(4,1)}), s8[4194304]{0:T(1024)(128)(4,1)S(1)}, s32[]{:S(2)}) async-start(s8[12582912]{0:T(1024)(128)(4,1)} %bitcast.246), calls=%async_computation.2 | async-start | bytes 8388608
  225.1 106.8 %copy-start.17 = (f32[256,4096]{1,0:T(8,128)}, f32[256,4096]{1,0:T(8,128)S(1)}, u32[]{:S(2)}) copy-start(f32[256,4096]{1,0:T(8,128)S(1)} %fusion.14) | copy-start | bytes 12582916
  225.1 8.2 %slice-start.3 = ((s8[12582912]{0:T(1024)(128)(4,1)}), s8[4194304]{0:T(1024)(128)(4,1)S(1)}, s32[]{:S(2)}) async-start(s8[12582912]{0:T(1024)(128)(4,1)} %bitcast.246), calls=%async_computation.3 | async-start | bytes 8388608
  233.0 97.6 %copy-start.13 = (bf16[256,1024]{1,0:T(8,128)(2,1)}, bf16[256,1024]{1,0:T(8,128)(2,1)S(1)}, u32[]{:S(2)}) copy-start(bf16[256,1024]{1,0:T(8,128)(2,1)S(1)} %get-tuple-element.239) | copy-start | bytes 1572868
  235.3 27.2 %copy-start.1 = (bf16[256,3072]{1,0:T(8,128)(2,1)}, bf16[256,3072]{1,0:T(8,128)(2,1)S(1)}, u32[]{:S(2)}) copy-start(bf16[256,3072]{1,0:T(8,128)(2,1)S(1)} %fusion.57.proj_ref) | copy-start | bytes 4718596
  268.6 8.8 %copy-start.18 = (f32[256,4096]{1,0:T(8,128)}, f32[256,4096]{1,0:T(8,128)S(1)}, u32[]{:S(2)}) copy-start(f32[256,4096]{1,0:T(8,128)S(1)} %fusion.6) | copy-start | bytes 12582916
  268.6 8.7 %copy-start.26 = (bf16[2,256,1024]{2,1,0:T(8,128)(2,1)S(1)}, bf16[2,256,1024]{2,1,0:T(8,128)(2,1)}, u32[]{:S(2)}) copy-start(bf16[2,256,1024]{2,1,0:T(8,128)(2,1)} %param.21) | copy-start | bytes 3145732
  277.3 493.3 %collective-permute-start = (bf16[256,1024]{1,0:T(8,128)(2,1)}, bf16[256,1024]{1,0:T(8,128)(2,1)}, u32[]{:S(2)}, u32[]{:S(2)}) collective-permute-start(bf16[256,1024]{1,0:T(8,128)(2,1)} %get-tuple-element.242), channel_id=1, source_target_pairs={{0,16},{16,0},{1,17},{17,1},{2,18},{18,2},{3,19},{19,3},{4,20},{20... | collective-permute-start | bytes 1572872 | tf_op jit(solution)/shard_map/ppermute | solution.py:512
  277.4 7.7 copy-start.31
  285.1 6.8 copy-start.27
  294.2 30.5 %copy-start.32 = (bf16[256,1024]{1,0:T(8,128)(2,1)}, bf16[256,1024]{1,0:T(8,128)(2,1)S(1)}, u32[]{:S(2)}) copy-start(bf16[256,1024]{1,0:T(8,128)(2,1)S(1)} %fusion.132.refs_7_) | copy-start | bytes 1572868
  331.9 50.8 %copy-start.10 = (bf16[256,1024]{1,0:T(8,128)(2,1)}, bf16[256,1024]{1,0:T(8,128)(2,1)S(1)}, u32[]{:S(2)}) copy-start(bf16[256,1024]{1,0:T(8,128)(2,1)S(1)} %get-tuple-element.206.refs_5_) | copy-start | bytes 1572868
  339.4 6.8 copy-start.28
  349.3 26.8 %copy-start.20 = (bf16[2,256,1024]{2,1,0:T(8,128)(2,1)S(1)}, bf16[2,256,1024]{2,1,0:T(8,128)(2,1)}, u32[]{:S(2)}) copy-start(bf16[2,256,1024]{2,1,0:T(8,128)(2,1)} %param.20) | copy-start | bytes 3145732
  376.2 5.2 copy-start.78
  376.2 5.3 copy-start.80
  384.4 388.5 %collective-permute-start.1 = (bf16[256,1024]{1,0:T(8,128)(2,1)}, bf16[256,1024]{1,0:T(8,128)(2,1)}, u32[]{:S(2)}, u32[]{:S(2)}) collective-permute-start(bf16[256,1024]{1,0:T(8,128)(2,1)} %get-tuple-element.192), channel_id=1, source_target_pairs={{0,16},{16,0},{1,17},{17,1},{2,18},{18,2},{3,19},{19,3},{4,20},{20... | collective-permute-start | bytes 1572872 | tf_op jit(solution)/shard_map/ppermute | solution.py:512
  398.0 6.9 copy-start.25
  398.1 14.6 %copy-start.16 = (f32[1024,33]{1,0:T(8,128)S(1)}, f32[1024,33]{1,0:T(8,128)}, u32[]{:S(2)}) copy-start(f32[1024,33]{1,0:T(8,128)} %constant.90.clone) | copy-start | bytes 405508
  412.6 8.6 %copy-start.23 = (f32[1024,64]{0,1:T(8,128)S(1)}, f32[1024,64]{0,1:T(8,128)}, u32[]{:S(2)}) copy-start(f32[1024,64]{0,1:T(8,128)} %copy-done.22) | copy-start | bytes 786436
  416.4 8.1 %copy-start.21 = (f32[1024,256]{1,0:T(8,128)S(1)}, f32[1024,256]{1,0:T(8,128)}, u32[]{:S(2)}) copy-start(f32[1024,256]{1,0:T(8,128)} %get-tuple-element.235) | copy-start | bytes 3145732
  421.3 12.3 %copy-start.35 = (f32[4,16384]{1,0:T(4,128)S(1)}, f32[4,16384]{1,0:T(4,128)}, u32[]{:S(2)}) copy-start(f32[4,16384]{1,0:T(4,128)} %reshape_reshape.7) | copy-start | bytes 786436
  421.3 12.3 %copy-start.81 = (f32[4,16]{1,0:T(4,128)S(1)}, f32[4,16]{1,0:T(4,128)}, u32[]{:S(2)}) copy-start(f32[4,16]{1,0:T(4,128)} %reshape.906) | copy-start | bytes 772
  426.4 9.5 %copy-start.29 = (bf16[1024,256]{0,1:T(8,128)(2,1)S(1)}, bf16[1024,256]{0,1:T(8,128)(2,1)}, u32[]{:S(2)}) copy-start(bf16[1024,256]{0,1:T(8,128)(2,1)} %get-tuple-element.204) | copy-start | bytes 1572868
  429.8 8.6 %copy-start.30 = (bf16[1024,256]{0,1:T(8,128)(2,1)S(1)}, bf16[1024,256]{0,1:T(8,128)(2,1)}, u32[]{:S(2)}) copy-start(bf16[1024,256]{0,1:T(8,128)(2,1)} %get-tuple-element.203) | copy-start | bytes 1572868
  583.7 168.2 %copy-start.76 = (bf16[32,512]{1,0:T(8,128)(2,1)S(1)}, bf16[32,512]{1,0:T(8,128)(2,1)}, u32[]{:S(2)}) copy-start(bf16[32,512]{1,0:T(8,128)(2,1)} %get-tuple-element.114) | copy-start | bytes 98308
  583.7 169.1 %copy-start.75 = (bf16[32,512]{1,0:T(8,128)(2,1)S(1)}, bf16[32,512]{1,0:T(8,128)(2,1)}, u32[]{:S(2)}) copy-start(bf16[32,512]{1,0:T(8,128)(2,1)} %get-tuple-element.116) | copy-start | bytes 98308
  583.7 173.2 %copy-start.48 = (bf16[256,512]{1,0:T(8,128)(2,1)S(1)}, bf16[256,512]{1,0:T(8,128)(2,1)}, u32[]{:S(2)}) copy-start(bf16[256,512]{1,0:T(8,128)(2,1)} %get-tuple-element.128) | copy-start | bytes 786436
  583.7 174.2 %copy-start.47 = (bf16[256,512]{1,0:T(8,128)(2,1)S(1)}, bf16[256,512]{1,0:T(8,128)(2,1)}, u32[]{:S(2)}) copy-start(bf16[256,512]{1,0:T(8,128)(2,1)} %get-tuple-element.126) | copy-start | bytes 786436
  583.7 175.2 %copy-start.55 = (bf16[1024,128]{1,0:T(8,128)(2,1)S(1)}, bf16[1024,128]{1,0:T(8,128)(2,1)}, u32[]{:S(2)}) copy-start(bf16[1024,128]{1,0:T(8,128)(2,1)} %get-tuple-element.149) | copy-start | bytes 786436
  583.7 175.2 %copy-start.56 = (bf16[1024,128]{1,0:T(8,128)(2,1)S(1)}, bf16[1024,128]{1,0:T(8,128)(2,1)}, u32[]{:S(2)}) copy-start(bf16[1024,128]{1,0:T(8,128)(2,1)} %get-tuple-element.150) | copy-start | bytes 786436
  751.7 8.9 %copy-start.53 = (bf16[1024,128]{1,0:T(8,128)(2,1)S(1)}, bf16[1024,128]{1,0:T(8,128)(2,1)}, u32[]{:S(2)}) copy-start(bf16[1024,128]{1,0:T(8,128)(2,1)} %get-tuple-element.157) | copy-start | bytes 786436
  751.8 8.9 %copy-start.54 = (bf16[1024,128]{1,0:T(8,128)(2,1)S(1)}, bf16[1024,128]{1,0:T(8,128)(2,1)}, u32[]{:S(2)}) copy-start(bf16[1024,128]{1,0:T(8,128)(2,1)} %get-tuple-element.158) | copy-start | bytes 786436
  751.8 8.9 %copy-start.69 = (bf16[1024,128]{1,0:T(8,128)(2,1)S(1)}, bf16[1024,128]{1,0:T(8,128)(2,1)}, u32[]{:S(2)}) copy-start(bf16[1024,128]{1,0:T(8,128)(2,1)} %get-tuple-element.159) | copy-start | bytes 786436
  751.8 8.9 %copy-start.70 = (bf16[1024,128]{1,0:T(8,128)(2,1)S(1)}, bf16[1024,128]{1,0:T(8,128)(2,1)}, u32[]{:S(2)}) copy-start(bf16[1024,128]{1,0:T(8,128)(2,1)} %get-tuple-element.160) | copy-start | bytes 786436
  751.8 8.9 %copy-start.71 = (bf16[1024,128]{1,0:T(8,128)(2,1)S(1)}, bf16[1024,128]{1,0:T(8,128)(2,1)}, u32[]{:S(2)}) copy-start(bf16[1024,128]{1,0:T(8,128)(2,1)} %get-tuple-element.153) | copy-start | bytes 786436
  751.8 8.9 %copy-start.72 = (bf16[1024,128]{1,0:T(8,128)(2,1)S(1)}, bf16[1024,128]{1,0:T(8,128)(2,1)}, u32[]{:S(2)}) copy-start(bf16[1024,128]{1,0:T(8,128)(2,1)} %get-tuple-element.154) | copy-start | bytes 786436
  751.8 8.9 %copy-start.73 = (bf16[1024,128]{1,0:T(8,128)(2,1)S(1)}, bf16[1024,128]{1,0:T(8,128)(2,1)}, u32[]{:S(2)}) copy-start(bf16[1024,128]{1,0:T(8,128)(2,1)} %get-tuple-element.155) | copy-start | bytes 786436
  751.8 8.9 %copy-start.74 = (bf16[1024,128]{1,0:T(8,128)(2,1)S(1)}, bf16[1024,128]{1,0:T(8,128)(2,1)}, u32[]{:S(2)}) copy-start(bf16[1024,128]{1,0:T(8,128)(2,1)} %get-tuple-element.156) | copy-start | bytes 786436
  (46 other events, 123.6 us)

commit v4 on v3

--- a/solution.py
+++ b/solution.py
@@ -85,7 +85,7 @@
     for block in range(blocks):
         target_ref[block] = jnp.dot(
             table_ref[...], source_ref[pl.ds(block * rows, rows), :], preferred_element_type=F32
-        )
+        ).astype(target_ref.dtype)
 
 
 def convolve_kernel(blocks, rows, step, same_ref, table_ref, back_ref, filt_ref, x_ref, y_ref, spec_ref, out_ref):
@@ -178,8 +178,8 @@
                 weight = same_ref[i, i - lag]
                 gr = grad_ref[i, real, :] * weight
                 gi = grad_ref[i, imag, :] * weight
-                xr = spec_ref[i - lag, real, :]
-                xi = spec_ref[i - lag, imag, :]
+                xr = spec_ref[i - lag, real, :].astype(F32)
+                xi = spec_ref[i - lag, imag, :].astype(F32)
                 one = one + xr * gr
                 two = two + xi * gi
                 three = three + (xr * gi - xi * gr)
@@ -304,7 +304,7 @@
             outgoing[number - 1].wait()
         columns = pl.ds(pl.multiple_of(block * group, 128), group)
         filtered = y_in_ref[block].astype(F32) * valid + bias_ref[:, columns] * signal_ref[block]
-        filtered_ref[:, columns] = filtered
+        filtered_ref[:, columns] = filtered.astype(filtered_ref.dtype)
         gated_ref[:, columns] = (second_ref[block] * filtered).astype(BF)
 
 
@@ -316,7 +316,7 @@
         out_shape=(
             jax.ShapeDtypeStruct((16, 3 * width), BF),
             jax.ShapeDtypeStruct((blocks * rows, group), BF),
-            jax.ShapeDtypeStruct((rows, width), F32),
+            jax.ShapeDtypeStruct((rows, width), BF),
             jax.ShapeDtypeStruct((rows, width), BF),
         ),
         in_specs=[SMEM_SPEC] * 2 + [VMEM_SPEC] * 7,
@@ -342,17 +342,15 @@
     )(same, carried, table, back, filt, projected, weights, bias, valid)
 
 
-def unmix_kernel(
-    blocks, rows, step, same_ref, carried_ref, table_ref, back_ref, scale_ref, filt_ref, proj_ref, rim_ref, weight_ref,
-    bias_ref, valid_ref, x_ref, filtered_ref, gate_ref,
-    dproj_ref, dweight_ref, dbias_ref, dt_ref,
-    g_ref, mask_ref, signal_ref, spec_ref, grad_ref, out_ref, tap_ref, dx_ref, dx_in_ref, edge_ref, edge_in_ref, end_ref,
-    send, recv,
-):
-    peers = Peers(send, recv)
-    here, width = peers.here, proj_ref.shape[1] // 3
+def unmix_stages(blocks, rows, step, copy, here, others, refs):
+    (
+        same_ref, carried_ref, table_ref, back_ref, scale_ref, filt_ref, proj_ref, rim_ref, weight_ref, bias_ref, valid_ref,
+        x_ref, filtered_ref, gate_ref, dproj_ref, dweight_ref, dbias_ref, dt_ref, g_ref, mask_ref, signal_ref, spec_ref,
+        grad_ref, out_ref, tap_ref, dx_ref, dx_in_ref, edge_ref, edge_in_ref, end_ref,
+    ) = refs
+    width = proj_ref.shape[1] // 3
     group = width // blocks
-    carried, valid = carried_ref[0], valid_ref[...]
+    tail = end_ref.shape[0]
 
     def at_rows(block):
         return pl.ds(pl.multiple_of(block * rows, rows), rows)
@@ -361,108 +359,76 @@
         return pl.ds(pl.multiple_of(which * width + block * group, 128), group)
 
     def part(which, block):
-        return mixed_part(proj_ref, rim_ref, weight_ref, carried, columns_of(which, block))
-
-    outgoing = []
-    for number, block in enumerate(peers.blocks + (here,)):
-        columns = columns_of(0, block)
-        signal = part(0, block)[0] * part(2, block)[0]
-        through = gate_ref[:, columns].astype(F32) * part(1, block)[0]
-        dbias_ref[:, columns] = jnp.sum(through * signal, axis=0, keepdims=True)
-        signal_ref[block] = bias_ref[:, columns] * through
-        masked = (through * valid).astype(BF)
-        if number < 3:
-            mask_ref[block] = masked
-            item = peers.copy(number, mask_ref.at[block], g_ref.at[at_rows(here)], block)
-            item.start()
-            outgoing.append(item)
-        else:
-            g_ref[at_rows(here), :] = masked
-    spectra_rows(table_ref, x_ref, spec_ref, blocks, rows)
-    for item in outgoing:
-        item.wait()
-    spectra_rows(table_ref, g_ref, grad_ref, blocks, rows)
-    correlate_spectra(blocks, rows, step, same_ref, scale_ref, filt_ref, spec_ref, grad_ref, out_ref, tap_ref)
-
-    def result(block):
-        return jnp.dot(back_ref[...], out_ref[block], preferred_element_type=F32).astype(BF)
-
-    outgoing = []
-    for number, block in enumerate(peers.blocks):
-        dx_ref[block] = result(block)
-        item = peers.copy(3 + number, dx_ref.at[block], dx_in_ref.at[here], block)
-        item.start()
-        outgoing.append(item)
-    dx_in_ref[here] = result(here)
-    taps_back(blocks, rows, back_ref, scale_ref, tap_ref, dt_ref)
-    tail = end_ref.shape[0]
-    for number, block in enumerate((here,) + peers.blocks):
-        if number:
-            outgoing[number - 1].wait()
-        d_signal = dx_in_ref[block].astype(F32) * valid + signal_ref[block]
-        gate = gate_ref[:, columns_of(0, block)].astype(F32)
-        first, third = part(0, block), part(2, block)
-        second_views = part(1, block)
-        d_parts = (d_signal * third[0], gate * filtered_ref[:, columns_of(0, block)], d_signal * first[0])
-        for which, (grad, views) in enumerate(zip(d_parts, (first, second_views, third))):
-            columns = columns_of(which, block)
-            weights = [weight_ref[k : k + 1, columns] for k in range(3)]
-            for k in range(3):
-                dweight_ref[k : k + 1, columns] = jnp.sum(grad * views[1 + k], axis=0, keepdims=True)
-            back_one, back_two = advanced(grad, 1), advanced(grad, 2)
-            d_proj = weights[0] * grad + weights[1] * back_one + weights[2] * back_two
-            dproj_ref[:, columns] = d_proj.astype(BF)
-            end_ref[:, columns] = d_proj[rows - tail :, :]
-            head = grad[0:8, :]
-            index = lax.broadcasted_iota(jnp.int32, head.shape, 0)
-            row_zero, row_one = grad[0:1, :], grad[1:2, :]
-            older = weights[2] * row_zero
-            newer = weights[1] * row_zero + weights[2] * row_one
-            edge = jnp.where(index == 6, older, jnp.where(index == 7, newer, 0.0))
-            edge_ref[:, columns] = edge * carried
-    edge_copy = peers.copy(6, edge_ref, edge_in_ref, (here + 3) % 4)
-    edge_copy.start()
-    edge_copy.wait()
-    ending = end_ref[...]
-    extra = jnp.concatenate([jnp.zeros((tail - 8, 3 * width), F32), edge_in_ref[...]], axis=0)
-    dproj_ref[pl.ds(rows - tail, tail), :] = (ending + extra).astype(BF)
-
-
-def unmix(same, carried, table, back, scale, filt, projected, rim, weights, bias, valid, x_cols, filtered, gate, blocks, rows, number):
-    width = projected.shape[1] // 3
-    group = width // blocks
-    return pl.pallas_call(
-        functools.partial(unmix_kernel, blocks, rows, 32),
-        out_shape=(
-            jax.ShapeDtypeStruct((rows, 3 * width), BF),
-            jax.ShapeDtypeStruct((3, 3 * width), F32),
-            jax.ShapeDtypeStruct((1, width), F32),
-            jax.ShapeDtypeStruct((blocks * rows, group), F32),
-        ),
-        in_specs=[SMEM_SPEC] * 2 + [VMEM_SPEC] * 12,
-        out_specs=(VMEM_SPEC,) * 4,
-        scratch_shapes=[
-            pltpu.VMEM((blocks * rows, group), BF),
-            pltpu.VMEM((blocks, rows, group), BF),
-            pltpu.VMEM((blocks, rows, group), F32),
-            pltpu.VMEM((blocks, 2 * rows, group), F32),
-            pltpu.VMEM((blocks, 2 * rows, group), F32),
-            pltpu.VMEM((blocks, 2 * rows, group), BF),
-            pltpu.VMEM((blocks, 2 * rows, group), F32),
-            pltpu.VMEM((blocks, rows, group), BF),
-            pltpu.VMEM((blocks, rows, group), BF),
-            pltpu.VMEM((8, 3 * width), F32),
-            pltpu.VMEM((8, 3 * width), F32),
-            pltpu.VMEM((16, 3 * width), F32),
-            pltpu.SemaphoreType.DMA((7,)),
-            pltpu.SemaphoreType.DMA((7,)),
-        ],
-        compiler_params=pltpu.CompilerParams(
-            collective_id=number, has_side_effects=True, vmem_limit_bytes=KERNEL_BYTES
-        ),
-        name="unmix",
-        cost_estimate=lasting(28),
-    )(same, carried, table, back, scale, filt, projected, rim, weights, bias, valid, x_cols, filtered, gate)
+        return mixed_part(proj_ref, rim_ref, weight_ref, carried_ref[0], columns_of(which, block))
+
+    there = [copy(k, mask_ref.at[block], g_ref.at[at_rows(here)], block) for k, block in enumerate(others)]
+    again = [copy(3 + k, dx_ref.at[block], dx_in_ref.at[here], block) for k, block in enumerate(others)]
+    edge_copy = copy(6, edge_ref, edge_in_ref, (here + 3) % 4)
+
+    def gate():
+        valid = valid_ref[...]
+        for number, block in enumerate((*others, here)):
+            columns = columns_of(0, block)
+            signal = part(0, block)[0] * part(2, block)[0]
+            through = gate_ref[:, columns].astype(F32) * part(1, block)[0]
+            dbias_ref[:, columns] = jnp.sum(through * signal, axis=0, keepdims=True)
+            signal_ref[block] = bias_ref[:, columns] * through
+            masked = (through * valid).astype(BF)
+            if number < 3:
+                mask_ref[block] = masked
+                there[number].start()
+            else:
+                g_ref[at_rows(here), :] = masked
+
+    def convolve_back():
+        spectra_rows(table_ref, x_ref, spec_ref, blocks, rows)
+        for item in there:
+            item.wait()
+        spectra_rows(table_ref, g_ref, grad_ref, blocks, rows)
+        correlate_spectra(blocks, rows, step, same_ref, scale_ref, filt_ref, spec_ref, grad_ref, out_ref, tap_ref)
+
+        def result(block):
+            return jnp.dot(back_ref[...], out_ref[block], preferred_element_type=F32).astype(BF)
+
+        for number, block in enumerate(others):
+            dx_ref[block] = result(block)
+            again[number].start()
+        dx_in_ref[here] = result(here)
+        taps_back(blocks, rows, back_ref, scale_ref, tap_ref, dt_ref)
+
+    def unfilter():
+        valid, carried = valid_ref[...], carried_ref[0]
+        for number, block in enumerate((here, *others)):
+            if number:
+                again[number - 1].wait()
+            d_signal = dx_in_ref[block].astype(F32) * valid + signal_ref[block]
+            gate_values = gate_ref[:, columns_of(0, block)].astype(F32)
+            first, second, third = part(0, block), part(1, block), part(2, block)
+            d_second = gate_values * filtered_ref[:, columns_of(0, block)].astype(F32)
+            d_parts = (d_signal * third[0], d_second, d_signal * first[0])
+            for which, (grad, views) in enumerate(zip(d_parts, (first, second, third))):
+                columns = columns_of(which, block)
+                weights = [weight_ref[k : k + 1, columns] for k in range(3)]
+                for k in range(3):
+                    dweight_ref[k : k + 1, columns] = jnp.sum(grad * views[1 + k], axis=0, keepdims=True)
+                back_one, back_two = advanced(grad, 1), advanced(grad, 2)
+                d_proj = weights[0] * grad + weights[1] * back_one + weights[2] * back_two
+                dproj_ref[:, columns] = d_proj.astype(BF)
+                end_ref[:, columns] = d_proj[rows - tail :, :]
+                index = lax.broadcasted_iota(jnp.int32, (8, group), 0)
+                row_zero, row_one = grad[0:1, :], grad[1:2, :]
+                older = weights[2] * row_zero
+                newer = weights[1] * row_zero + weights[2] * row_one
+                edge = jnp.where(index == 6, older, jnp.where(index == 7, newer, 0.0))
+                edge_ref[:, columns] = edge * carried
+        edge_copy.start()
+
+    def edges():
+        edge_copy.wait()
+        extra = jnp.concatenate([jnp.zeros((tail - 8, 3 * width), F32), edge_in_ref[...]], axis=0)
+        dproj_ref[pl.ds(rows - tail, tail), :] = (end_ref[...] + extra).astype(BF)
+
+    return gate, convolve_back, unfilter, edges
 
 
 def convolve(same, table, back, filt, x_cols, blocks, rows):
@@ -686,22 +652,25 @@
 PARTS = 4
 
 
-def reduce_kernel(items, rest, halves, planes, order, *refs):
+def reduce_kernel(items, rest, halves, counts, planes, order, mixing, *refs):
     whole = len(items)
     total = whole + len(rest)
-    sides = len(halves) * 2 + 1
 
     def take(number):
         nonlocal refs
         first, refs = refs[:number], refs[number:]
         return first
 
-    inputs, rest_in = take(sides), take(len(rest))
+    mix_in = take(14 if mixing else 0)
+    lefts, rights, packs, rest_in = take(counts[0]), take(counts[1]), take(counts[2]), take(len(rest))
+    mix_out = take(4 if mixing else 0)
     own_out = take(total)
     other_out = dict(zip(planes, take(len(planes))))
+    mix_scratch = take(12 if mixing else 0)
     hold, inbox, far_in, near_in = take(total), take(whole), take(whole), take(whole)
     plane_in, cross_in = dict(zip(planes, take(len(planes)))), dict(zip(planes, take(len(planes))))
-    send, recv, local = refs
+    turned = take(counts[0])
+    send, recv, local = take(3)
     core, here, plane = lax.axis_index("section"), lax.axis_index("seq"), lax.axis_index("dp")
     by_x, by_y, far = here + 1 - 2 * (here % 2), (here + 2) % 4, 3 - here
     to_x, to_y, to_core = (core, by_x, plane), (core, by_y, plane), (1 - core, here, plane)
@@ -716,22 +685,32 @@
     def greet(target):
         pl.semaphore_signal(barrier, inc=1, device_id=target, device_id_type=MESH)
 
-    for target in (to_x, to_y, to_core):
+    in_plane = [to_x, to_y, to_core] + ([(core, far, plane)] if mixing else [])
+    for target in in_plane:
         greet(target)
-    if planes:
-
-        @pl.when(outer)
-        def _():
-            greet(to_inner)
-            pl.semaphore_wait(barrier, 4)
-
-        @pl.when(inner)
-        def _():
-            greet(to_outer)
-            greet(to_cross)
-            pl.semaphore_wait(barrier, 5)
-    else:
-        pl.semaphore_wait(barrier, 3)
+
+    @pl.when(outer)
+    def _():
+        greet(to_inner)
+        pl.semaphore_wait(barrier, len(in_plane) + 1)
+
+    @pl.when(inner)
+    def _():
+        greet(to_outer)
+        greet(to_cross)
+        pl.semaphore_wait(barrier, len(in_plane) + 2)
+
+    stages = ()
+    if mixing:
+        mix_send, mix_recv = take(2)
+
+        def mix_copy(number, source, target_ref, block):
+            return pltpu.make_async_remote_copy(
+                src_ref=source, dst_ref=target_ref, send_sem=mix_send.at[number], recv_sem=mix_recv.at[number],
+                device_id=(core, block, plane), device_id_type=MESH,
+            )
+
+        stages = unmix_stages(*mixing, mix_copy, here, (far, by_x, by_y), (*mix_in, *mix_out, *mix_scratch))
 
     def copy(kind, m, source, target_ref, target):
         return pltpu.make_async_remote_copy(
@@ -766,20 +745,19 @@
     def fill(m, slot, side, adds):
         rows, columns, left, right, first, order = items[m]
         block = {0: here, 1: by_x, 2: by_y, 3: far}[order[slot]]
-        high, wide = min(rows, 256), columns if columns <= 768 else 512
+        wide = columns if columns <= 768 else 512
+        high = min(rows, max(256, 131072 // wide))
         across = columns // wide
         start = side * halves[right] + first if right >= 0 else side * columns
 
         def step(index, carry):
             down, along = index // across, index % across
-            picked = pl.ds(pl.multiple_of(block * rows + down * high, 16), high)
+            picked = pl.ds(pl.multiple_of(block * rows + down * high, 128 if right >= 0 else 16), high)
             which = pl.ds(pl.multiple_of(start + along * wide, 128), wide)
             if right >= 0:
-                value = jnp.dot(
-                    inputs[left][picked, :], inputs[len(halves) + right][:, which], preferred_element_type=F32
-                )
+                value = dot(turned[left][picked, :], rights[right][:, which])
             else:
-                value = inputs[-1][picked, which]
+                value = packs[left][picked, which]
             where = pl.ds(pl.multiple_of(along * wide, 128), wide)
             for ref, base in adds:
                 value = value + ref[m][pl.ds(pl.multiple_of(base * rows + down * high, 16), high), where].astype(F32)
@@ -867,7 +845,20 @@
     )
     for m in range(whole, total):
         moves[m]["load"]().start()
+    def turn_over(left, target):
+        def step(index, carry):
+            where = pl.ds(pl.multiple_of(index * 256, 256), 256)
+            target[where, :] = left[:, where].T
+            return carry
+
+        lax.fori_loop(0, left.shape[1] // 256, step, 0)
+
+    for left, target in zip(lefts, turned):
+        turn_over(left, target)
     for step, pair in order:
+        if step == "mix":
+            stages[pair]()
+            continue
         for m in (2 * pair, 2 * pair + 1):
             names[step](m)
 
@@ -891,83 +882,123 @@
             moves[m]["held"]().wait()
 
 
-def reduce_order(pairs, summed, rest):
-    steps = [("load", k) for k in rest] + [("core", pairs[0]), ("fill", pairs[0]), ("go", pairs[0])]
+def reduce_order(pairs, rest):
+    steps = [("load", k) for k in rest[:1]] + [("core", pairs[0]), ("fill", pairs[0]), ("go", pairs[0])]
     steps += [("core", k) for k in pairs[1:3]] + [("fill", pairs[1])]
-    groups = [list(rest)] + [[pair] if pair in summed else [] for pair in pairs]
-
-    def at(name, number):
-        if 0 <= number < len(groups):
-            steps.extend((name, k) for k in groups[number])
+
+    def across(step):
+        for name, late in (("meet", 0), ("settle", 1), ("finish", 2)):
+            for flow in (rest, [None, *pairs]):
+                if 0 <= step - late < len(flow) and flow[step - late] is not None:
+                    yield name, flow[step - late]
 
     for i, pair in enumerate(pairs):
         steps.append(("wait", pair))
         if i + 1 < len(pairs):
             steps.append(("go", pairs[i + 1]))
         steps.append(("turn", pair))
+        steps += [("load", k) for k in rest[i + 1 : i + 2]]
         if i + 3 < len(pairs):
             steps.append(("core", pairs[i + 3]))
         if i + 2 < len(pairs):
             steps.append(("fill", pairs[i + 2]))
-        at("meet", i)
+        waiting = list(across(i))
+        steps += [item for item in waiting if item[0] == "meet"]
         steps.append(("own", pair))
-        at("settle", i - 1)
-        at("finish", i - 2)
-    for i in range(len(pairs), len(pairs) + 3):
-        at("meet", i)
-        at("settle", i - 1)
-        at("finish", i - 2)
+        steps += [item for item in waiting if item[0] != "meet"]
+    for i in range(len(pairs), max(len(pairs), len(rest)) + 3):
+        steps += across(i)
     return steps
 
 
-def reduce_layer(lefts, rights, packed, rest, planes, order, number):
-    count = lax.axis_size("seq")
-    halves = [right.shape[1] // 2 for right in rights]
-    small_rows, small_width = packed.shape[0] // count, packed.shape[1] // 2
-    up, down, enter, leave = (left.shape[0] // count for left in lefts)
-    items = [
-        (leave, halves[3], 3, 3, 0, X_FIRST),
-        (small_rows, small_width, -1, -1, 0, Y_FIRST),
-        (enter, halves[2] // 2, 2, 2, 0, X_FIRST),
-        (enter, halves[2] // 2, 2, 2, halves[2] // 2, Y_FIRST),
-    ]
+def mixing_order(rest, summed):
+    words = (
+        "load0 mix0 core0 core1 fill0 go0 load1 core2 fill1 go1 core3 mix1 load2 fill2 wait0 turn0 go2 meet0 fill3 wait1 turn1 "
+        "go3 meet1 load3 own0 mix2 settle0 meet2 own1 wait2 turn2 settle1 finish0 meet3 own2 Meet0 wait3 turn3 settle2 finish1 "
+        "Meet1 mix3 own3 settle3 Settle0 finish2 Settle1 finish3 Finish0 Finish1"
+    )
+    steps = []
+    for word in words.split():
+        name, number = word[:-1], int(word[-1])
+        if name in ("load", "meet", "settle", "finish"):
+            steps += [(name, rest[number])] if number < len(rest) else []
+        elif name in ("Meet", "Settle", "Finish"):
+            steps += [(name.lower(), number)] if number < summed else []
+        else:
+            steps.append((name, number))
+    return steps
+
+
+def mlp_items(up, down, wide_up, wide_down):
+    items = []
     for part in range(PARTS):
         items += [
-            (up, halves[0] // PARTS, 0, 0, part * halves[0] // PARTS, X_FIRST),
-            (down, halves[1] // PARTS, 1, 1, part * halves[1] // PARTS, Y_FIRST),
+            (up, wide_up // PARTS, 0, 0, part * wide_up // PARTS, X_FIRST),
+            (down, wide_down // PARTS, 1, 1, part * wide_down // PARTS, Y_FIRST),
         ]
+    return items
+
+
+def reduce_call(items, lefts, rights, packs, rest, planes, order, number, mixing=None, mix_in=()):
+    halves = [right.shape[1] // 2 for right in rights]
     pieces = [item[:2] for item in items] + [piece.shape for piece in rest]
-
-    def buffers(slots, shapes):
-        return [pltpu.VMEM((slots * shape[0], shape[1]), BF) for shape in shapes]
-
-    hbm = pl.BlockSpec(memory_space=pl.ANY)
     whole, total = len(items), len(pieces)
     planes = list(planes) + list(range(whole, total))
     across = [pieces[m] for m in planes]
-    scratch = buffers(4, pieces[:whole]) + buffers(1, pieces[whole:])
+
+    def buffers(slots, shapes):
+        return [pltpu.VMEM((slots * shape[0], shape[1]), BF) for shape in shapes]
+
+    mix_out, scratch = [], []
+    if mixing:
+        blocks, rows, _ = mixing
+        width = mix_in[6].shape[1] // 3
+        group = width // blocks
+        mix_out = [
+            jax.ShapeDtypeStruct((rows, 3 * width), BF),
+            jax.ShapeDtypeStruct((3, 3 * width), F32),
+            jax.ShapeDtypeStruct((1, width), F32),
+            jax.ShapeDtypeStruct((blocks * rows, group), F32),
+        ]
+        scratch = [
+            pltpu.VMEM((blocks * rows, group), BF),
+            pltpu.VMEM((blocks, rows, group), BF),
+            pltpu.VMEM((blocks, rows, group), F32),
+            pltpu.VMEM((blocks, 2 * rows, group), BF),
+            pltpu.VMEM((blocks, 2 * rows, group), F32),
+            pltpu.VMEM((blocks, 2 * rows, group), BF),
+            pltpu.VMEM((blocks, 2 * rows, group), F32),
+            pltpu.VMEM((blocks, rows, group), BF),
+            pltpu.VMEM((blocks, rows, group), BF),
+            pltpu.VMEM((8, 3 * width), F32),
+            pltpu.VMEM((8, 3 * width), F32),
+            pltpu.VMEM((16, 3 * width), F32),
+        ]
+    hbm = pl.BlockSpec(memory_space=pl.ANY)
+    scratch += buffers(4, pieces[:whole]) + buffers(1, pieces[whole:])
     for slots in (4, 2, 1):
         scratch += buffers(slots, pieces[:whole])
     scratch += buffers(1, across) + buffers(1, across)
-    semaphores = [pltpu.SemaphoreType.DMA((6, total)), pltpu.SemaphoreType.DMA((6, total)), pltpu.SemaphoreType.DMA((total,))]
+    scratch += [pltpu.VMEM((left.shape[1], left.shape[0]), left.dtype) for left in lefts]
+    scratch += [pltpu.SemaphoreType.DMA((6, total)), pltpu.SemaphoreType.DMA((6, total)), pltpu.SemaphoreType.DMA((total,))]
+    if mixing:
+        scratch += [pltpu.SemaphoreType.DMA((7,)), pltpu.SemaphoreType.DMA((7,))]
+    counts = (len(lefts), len(rights), len(packs))
     result = pl.pallas_call(
-        functools.partial(reduce_kernel, items, pieces[whole:], halves, planes, order),
-        out_shape=[jax.ShapeDtypeStruct(shape, BF) for shape in pieces + across],
-        in_specs=[VMEM_SPEC] * (2 * len(lefts) + 1) + [hbm] * len(rest),
-        out_specs=[hbm] * (total + len(planes)),
-        scratch_shapes=scratch + semaphores,
+        functools.partial(reduce_kernel, items, pieces[whole:], halves, counts, planes, order, mixing),
+        out_shape=mix_out + [jax.ShapeDtypeStruct(shape, BF) for shape in pieces + across],
+        in_specs=[SMEM_SPEC] * min(len(mix_in), 2) + [VMEM_SPEC] * max(len(mix_in) - 2, 0)
+        + [VMEM_SPEC] * sum(counts) + [hbm] * len(rest),
+        out_specs=[VMEM_SPEC] * len(mix_out) + [hbm] * (total + len(planes)),
+        scratch_shapes=scratch,
         compiler_params=pltpu.CompilerParams(
             collective_id=number, has_side_effects=True, vmem_limit_bytes=60 * 1024 * 1024
         ),
-        name="reduce_layer",
-        cost_estimate=lasting(150),
-    )(*lefts, *rights, packed, *rest)
-    return result[:total], dict(zip(planes, result[total:]))
-
-
-def join_pieces(pieces):
-    ups, downs = pieces[4::2], pieces[5::2]
-    return [jnp.concatenate(group, axis=1) for group in (ups, downs, pieces[2:4])] + list(pieces[:2])
+        name="unmix_reduce" if mixing else "reduce",
+        cost_estimate=lasting(90),
+    )(*mix_in, *lefts, *rights, *packs, *rest)
+    mixed, own, other = result[: len(mix_out)], result[len(mix_out) : len(mix_out) + total], result[len(mix_out) + total :]
+    return mixed, list(own), dict(zip(planes, other))
 
 
 def reduce_plain(lefts, rights, packed, core):
@@ -975,7 +1006,7 @@
     chips = []
     for left, right in zip(lefts, rights):
         keep, send = core_halves(core, right)
-        chips.append(dot(left, keep) + core_swap(dot(left, send).astype(BF)).astype(F32))
+        chips.append(dot_left(left, keep) + core_swap(dot_left(left, send).astype(BF)).astype(F32))
     keep, send = core_halves(core, packed)
     small = (keep + core_swap(send.astype(BF)).astype(F32)).astype(BF)
     up, down, enter, leave = (chip.astype(BF) for chip in chips)
@@ -1007,15 +1038,25 @@
     scale = jnp.asarray(np.concatenate([weight_np, parity_np], axis=1))
     embedding = jnp.asarray(positions_embedding(slots, FREQS))
 
-    small = (ln1_gain, short_w, filt_in, filt_shift, sine_freq, filt_out, decay, filter_bias, ln2_gain)
-    small_shapes = [a.shape[1:] for a in small]
-    small_sizes = [math.prod(s) for s in small_shapes]
-    lane = 1024
-    packed_rows = -(-sum(small_sizes) // (lane * 16)) * 16
-    flat = jnp.concatenate([a.reshape(-1) for a in small])
-    flat = jnp.pad(flat, (0, packed_rows * lane - flat.shape[0])).reshape(packed_rows, lane)
+    others = (ln1_gain, short_w, filt_in, filt_shift, sine_freq, decay, filter_bias, ln2_gain)
+    other_shapes = [a.shape[1:] for a in others]
+    other_sizes = [math.prod(shape) for shape in other_shapes]
+    other_axis = (0, 1, 1, 0, 0, 0, 0, 0)
+    lane, out_rows = width, filt_out.shape[1]
+    other_rows = -(-sum(other_sizes) // lane)
+    packed_rows = -(-(out_rows + other_rows) // 16) * 16
+
+    def packed_small(top, parts):
+        flat = jnp.concatenate(parts, axis=-1)
+        lead = flat.shape[:-1]
+        none = ((0, 0),) * len(lead)
+        flat = jnp.pad(flat, none + ((0, other_rows * lane - flat.shape[-1]),)).reshape(lead + (other_rows, lane))
+        flat = jnp.pad(flat, none + ((0, packed_rows - out_rows - other_rows), (0, 0)))
+        return jnp.concatenate([top, flat], axis=-2)
+
+    flat = packed_small(filt_out[0], [a.reshape(-1) for a in others])
     flat_all, out_all, in_all, up_all, down_all = gather_shards([flat, w_out[0], w_in[0], mlp_up[0], mlp_down[0]])
-    everywhere = flat_all.reshape(2, count, packed_rows * lane)
+    everywhere = flat_all.reshape(2, count, packed_rows, lane)
     gathered = [
         (
             in_all[layer * width : (layer + 1) * width], out_all[layer * width : (layer + 1) * width],
@@ -1023,19 +1064,20 @@
         )
         for layer in range(2)
     ]
-    small_axis = (0, 1, 1, 0, 0, 0, 0, 0, 0)
 
     def small_of(layer):
         found = []
         offset = 0
-        for shape, size, axis in zip(small_shapes, small_sizes, small_axis):
-            part = everywhere[layer, :, offset : offset + size].reshape((count,) + shape)
+        below = everywhere[layer, :, out_rows : out_rows + other_rows].reshape(count, other_rows * lane)
+        for shape, size, axis in zip(other_shapes, other_sizes, other_axis):
+            part = below[:, offset : offset + size].reshape((count,) + shape)
             part = jnp.moveaxis(part, 0, axis)
             full = list(shape)
             full[axis] = shape[axis] * count
             found.append(part.reshape(full).astype(F32))
             offset += size
-        return found
+        top = everywhere[layer, :, :out_rows].reshape(count * out_rows, lane).astype(F32)
+        return found[:5] + [top] + found[5:]
 
     length_row = lax.dynamic_index_in_dim(lengths, core, 0, keepdims=False)
     index_all = jnp.arange(count, dtype=jnp.int32)
@@ -1099,7 +1141,7 @@
         )
         return layer_out.astype(BF), stored
 
-    def backward(upstream, stored, layer):
+    def backward(upstream, stored, layer, rest):
         (
             layer_in, normed, projected, rim, filtered, gated, residual, normed_two,
             upward, active, x_cols, filt, pull,
@@ -1113,9 +1155,17 @@
         grad_branch = grad_residual.astype(BF)
         grad_gated = dot_right(grad_branch, out_matrix)
         if routed:
-            grad_proj, grad_short, grad_bias, grad_taps = unmix(
+            mix_in = (
                 same, carried_on.reshape(1), table, back, scale, filt, projected, rim, short_weights, bias[None], valid,
-                x_cols, filtered, grad_gated, count, rows, 5 + layer,
+                x_cols, filtered, grad_gated.astype(BF),
+            )
+            block_rows = width // count
+            items = mlp_items(block_rows, hidden_block, hidden // 2, width // 2)
+            summed = 0 if layer else PARTS // 2
+            order = mixing_order(list(range(PARTS, PARTS + len(rest) // 2)), summed)
+            (grad_proj, grad_short, grad_bias, grad_taps), own, other = reduce_call(
+                items, [normed_two, active], [grad_hidden, upstream], [], rest, range(2 * summed), order, 5 + layer,
+                (count, rows, 32), mix_in,
             )
             grad_bias = grad_bias[0]
         else:
@@ -1143,44 +1193,56 @@
         d_in, d_shift, d_freq, d_out_cols, d_decay_cols = pull(grad_taps)
         d_out = lax.dynamic_update_slice_in_dim(jnp.zeros_like(out_w), d_out_cols, here * col_width, 1)
         d_decay = lax.dynamic_update_slice_in_dim(jnp.zeros_like(decay_w), d_decay_cols, here * col_width, 0)
-        small_grads = (
-            grad_gain_one, grad_short, d_in, d_shift, d_freq, d_out, d_decay, grad_bias, grad_gain_two
-        )
         parts = []
-        for grad, shape, axis in zip(small_grads, small_shapes, small_axis):
+        other_grads = (grad_gain_one, grad_short, d_in, d_shift, d_freq, d_decay, grad_bias, grad_gain_two)
+        for grad, shape, axis in zip(other_grads, other_shapes, other_axis):
             split = list(grad.shape)
             split[axis : axis + 1] = [count, shape[axis]]
             parts.append(jnp.moveaxis(grad.reshape(split), axis, 0).reshape(count, -1))
-        packed = jnp.concatenate(parts, axis=1)
-        packed = jnp.pad(packed, ((0, 0), (0, packed_rows * lane - packed.shape[1])))
-        lefts = [normed_two.T, active.T, normed.T, gated.T]
-        rights = [grad_hidden, upstream, grad_proj, grad_branch]
-        return grad_layer_in, (lefts, rights, packed.reshape(count * packed_rows, lane))
+        packed = packed_small(d_out.reshape(count, out_rows, lane), parts).reshape(count * packed_rows, lane)
+        if routed:
+            return grad_layer_in, (own, other, normed, grad_proj, gated, grad_branch, packed)
+        factors = ([normed_two, active, normed, gated], [grad_hidden, upstream, grad_proj, grad_branch], packed)
+        return grad_layer_in, factors
 
     def row_of(values):
         return lax.dynamic_index_in_dim(values, core, 0, keepdims=False)
 
     out_first, stored_first = forward(row_of(tokens).astype(F32), 0)
     out_second, stored_second = forward(out_first.astype(F32), 1)
-    grad_second, factors_second = backward(row_of(out_grad), stored_second, 1)
     if routed:
-        whole, held_back = 4 + 2 * PARTS, 2
-        ready = whole - 2 * held_back
-        pairs = [1, *range(2, 2 + PARTS - held_back), 0, *range(2 + PARTS - held_back, 2 + PARTS)]
-        order = reduce_order(pairs, range(ready // 2), [])
-        own_second, other_second = reduce_layer(*factors_second, [], range(ready), order, 1)
-        grad_first, factors_first = backward(grad_second, stored_first, 0)
-        order = reduce_order([1, *range(2, 2 + PARTS), 0], range(whole // 2), range(whole // 2, whole // 2 + held_back))
-        own_first, other_first = reduce_layer(*factors_first, own_second[ready:], range(whole), order, 2)
-        other_second = [other_second[m] for m in range(ready)] + [other_first[m] for m in range(whole, whole + 2 * held_back)]
-        own_second = list(own_second[:ready]) + list(own_first[whole:])
-        own_first, other_first = own_first[:whole], [other_first[m] for m in range(whole)]
-        own_first, own_second, other_first, other_second = (
-            join_pieces(part) for part in (own_first, own_second, other_first, other_second)
-        )
+        grad_second, kept_second = backward(row_of(out_grad), stored_second, 1, [])
+        grad_first, kept_first = backward(grad_second, stored_first, 0, kept_second[0])
+        items, lefts, rights, packs = [], [], [], []
+        for k, (_, _, normed, grad_proj, gated, grad_branch, packed) in enumerate((kept_second, kept_first)):
+            lefts += [normed, gated]
+            rights += [grad_proj, grad_branch]
+            packs.append(packed)
+            block_rows, part = width // count, 3 * width // 2 // PARTS
+            for piece in range(PARTS):
+                order = Y_FIRST if piece % 2 else X_FIRST
+                items.append((block_rows, part, 2 * k, 2 * k, piece * part, order))
+            items.append((block_rows, width // 2, 2 * k + 1, 2 * k + 1, 0, X_FIRST))
+            items.append((packed_rows, lane // 2, k, -1, 0, Y_FIRST))
+        each, mlp = PARTS + 2, 2 * PARTS
+        done = 2 * (PARTS // 2)
+        order = reduce_order([0, 1, 3, 4, 2, 5], list(range(each, each + PARTS - done // 2)))
+        _, own, other = reduce_call(items, lefts, rights, packs, kept_first[0][done:mlp], range(2 * each), order, 1)
+        other = [other[m] for m in range(2 * each + mlp - done)]
+
+        def assembled(late, mlp_part):
+            groups = (mlp_part[::2], mlp_part[1::2], late[:PARTS])
+            return [jnp.concatenate(group, axis=1) for group in groups] + list(late[PARTS:])
+
+        second_other = [kept_first[1][m] for m in range(mlp, 2 * mlp)]
+        own_second, other_second = assembled(own[:each], kept_first[0][mlp:]), assembled(other[:each], second_other)
+        own_first = assembled(own[each : 2 * each], kept_first[0][:done] + own[2 * each :])
+        first_other = [kept_first[1][m] for m in range(done)]
+        other_first = assembled(other[each : 2 * each], first_other + other[2 * each :])
     else:
+        grad_second, factors_second = backward(row_of(out_grad), stored_second, 1, [])
         own_second = reduce_plain(*factors_second, core)
-        grad_first, factors_first = backward(grad_second, stored_first, 0)
+        grad_first, factors_first = backward(grad_second, stored_first, 0, [])
         own_first = reduce_plain(*factors_first, core)
         other_first, other_second = ([core_swap(part) for part in own] for own in (own_first, own_second))
 
@@ -1198,13 +1260,15 @@
         return jnp.concatenate([low, high], axis=1).astype(F32)
 
     grad_up, grad_down, grad_in, grad_out = (finish(index) for index in range(4))
-    small_total = finish(4).reshape(-1)
-    small_out = []
+    small_total = finish(4)
+    below = small_total[out_rows : out_rows + other_rows].reshape(-1)
+    other_out = []
     offset = 0
-    for shape, size in zip(small_shapes, small_sizes):
-        small_out.append(small_total[offset : offset + size].reshape((1,) + shape))
+    for shape, size in zip(other_shapes, other_sizes):
+        other_out.append(below[offset : offset + size].reshape((1,) + shape))
         offset += size
-    g_ln1, g_short, g_fin, g_shift, g_freq, g_fout, g_decay, g_bias, g_ln2 = small_out
+    g_ln1, g_short, g_fin, g_shift, g_freq, g_decay, g_bias, g_ln2 = other_out
+    g_fout = small_total[:out_rows][None]
     return (
         layer_outputs, input_grads, g_ln1, grad_in[None], g_short, g_fin, g_shift, g_freq, g_fout, g_decay, g_bias,
         grad_out[None], g_ln2, grad_up[None], grad_down[None],

time: 786 us -> 754 us (0.959)
  local copies, waits for them, and re-layouts: 46.2 us -> 27.6 us
  Pallas kernels: 580 us -> 570 us
  other arithmetic: 50.3 us -> 41.9 us
    dot_general x2 -> x0, local copies, waits for them, and re-layouts: 11.6 us -> none  [dot(): return jnp.dot(left, right, preferred_element_type=F32)]
    convert_element_type x2 -> x5, other arithmetic: 9.75 us -> 1.51 us  [the longest x2 0.58 us: forward(): normed = layer_norm(layer_in, gain_one).astype(BF)]
    pallas_call x4 -> x3, Pallas kernels: 369 us -> 361 us  [reduce_call(): pl.pallas_call(functools.partial(reduce_kernel, items, pieces[whole:], ha...]
    unnamed x196 -> x352, local copies, waits for them, and re-layouts: 9.8 us -> 16.2 us
  transfers between devices with their start and end apart: 2 -> 2, of which waited for: 0 -> 0; matrix products, arithmetic and copies ran while one was open for 16% -> 7% of each run, Pallas kernels for 48% -> 17%
where the time goes in v4:
time: 754 us; the launch traced here: 744 us
  Pallas kernels  570 us (76%)
  matrix products  98.4 us (13%)
  other arithmetic  41.9 us (6%)
  local copies, waits for them, and re-layouts  27.6 us (4%)
    pallas_call x3, Pallas kernels, reduce_call(): pl.pallas_call(functools.partial(reduce_kernel, items, pieces[whole:], ha...  361 us
    pallas_call x1, Pallas kernels, gather_shards(): pl.pallas_call(functools.partial(gather_kernel, chunks, heights, count),...  161 us
    pallas_call x2, Pallas kernels, mix(): pl.pallas_call(functools.partial(mix_kernel, blocks, rows, 32), out_shape...  47.9 us
    dot_general x8, matrix products, dot(): return jnp.dot(left, right, preferred_element_type=F32)  41.3 us
    dot_general x8, matrix products, dot_right(): lax.dot_general(left, right, (((1,), (1,)), ((), ())), preferred_element_...  38.8 us
    unnamed x352, local copies, waits for them, and re-layouts  16.2 us
  transfers between devices with their start and end apart: 2, of which 0 were waited for; matrix products, arithmetic and copies ran while one was open for 7% of the time, Pallas kernels for 17%

profile of v4, /device:TPU:0, one launch (start us, length us, event | category | flops | bytes accessed | tf_op | source)
XLA Modules:
  0.0 744.0 jit_solution(14856761739544943675)
XLA Ops:
  5.0 1.4 concatenate.191
  7.2 1.6 copy-done.7
  8.8 1.4 copy-done.8
  10.2 1.0 copy-done.9
  11.3 160.7 %gather_shards.1 = (bf16[256,1024]{1,0:T(8,128)(2,1)S(1)}, bf16[2048,1024]{1,0:T(8,128)(2,1)}, bf16[2048,3072]{1,0:T(8,128)(2,1)}, bf16[2048,4096]{1,0:T(8,128)(2,1)}, bf16[8192,1024]{1,0:T(8,128)(2,1)}) custom-call(bf16[32,1024]{1,0:T(8,128)(2,1)S(1)} %fusion.138.refs_0_, bf16[256,1024]{1,0:T(8,128)(2,1)S(1)} %bitcast.202, bf16[256,3072]{1,0:T(8,128)(2,1)S(1)} %bitcast.201, ...), custom_call_target="tpu_custom_call" | custom-call | bytes 701100032 | tf_op jit(solution)/shard_map/gather_shards/pallas_call | solution.py:623
  176.2 1.5 fusion.128
  177.7 2.7 multiply_convert_fusion.3
  187.9 4.8 fusion.38.proj_ref.refs_6_
  194.4 24.4 %mix.2 = (bf16[16,3072]{1,0:T(8,128)(2,1)S(1)}, bf16[1024,256]{1,0:T(8,128)(2,1)S(1)}, bf16[256,1024]{1,0:T(8,128)(2,1)S(1)}, bf16[256,1024]{1,0:T(8,128)(2,1)S(1)}) custom-call(f32[4,4]{1,0:T(4,128)S(1)} %compare_convert_fusion.same_ref.refs_0_, f32[1]{0:T(128)} %bitcast.2.carried_ref.refs_1_, bf16[512,256]{1,0:T(8,128)(2,1)S(1)} %copy-done.4, ...), custom_call_target="tpu_custom_call" | custom-call | bytes 81180000 | tf_op jit(solution)/shard_map/mix/pallas_call | solution.py:314
  218.9 3.0 fusion.162
  222.5 8.9 %multiply_convert_fusion.1 = (bf16[256,4096]{1,0:T(8,128)(2,1)S(1)}, f32[256,4096]{1,0:T(8,128)}) fusion(bf16[256,1024]{1,0:T(8,128)(2,1)S(1)} %multiply_convert_fusion.4.refs_14_, bf16[2048,4096]{1,0:T(8,128)(2,1)} %get-tuple-element.108), kind=kOutput, calls=%fused_computation.43 | convolution fusion | flops 2156920832 | bytes 15204352 | tf_op jit(solution)/shard_map/dot_general | solution.py:20
  231.5 2.5 convert_reduce_fusion
  235.2 4.8 fusion.41.proj_ref.refs_6_
  240.2 23.5 %mix.3 = (bf16[16,3072]{1,0:T(8,128)(2,1)S(1)}, bf16[1024,256]{1,0:T(8,128)(2,1)S(1)}, bf16[256,1024]{1,0:T(8,128)(2,1)S(1)}, bf16[256,1024]{1,0:T(8,128)(2,1)S(1)}) custom-call(f32[4,4]{1,0:T(4,128)S(1)} %compare_convert_fusion.same_ref.refs_0_, f32[1]{0:T(128)} %bitcast.2.carried_ref.refs_1_, bf16[512,256]{1,0:T(8,128)(2,1)S(1)} %copy-done.4, ...), custom_call_target="tpu_custom_call" | custom-call | bytes 81180000 | tf_op jit(solution)/shard_map/mix/pallas_call | solution.py:314
  265.2 9.8 %multiply_convert_fusion = (bf16[256,4096]{1,0:T(8,128)(2,1)}, f32[256,4096]{1,0:T(8,128)}) fusion(bf16[256,1024]{1,0:T(8,128)(2,1)S(1)} %multiply_convert_fusion.2.refs_14_, bf16[2048,4096]{1,0:T(8,128)(2,1)} %get-tuple-element.108), kind=kOutput, calls=%fused_computation.42 | convolution fusion | flops 2156920832 | bytes 15204352 | tf_op jit(solution)/shard_map/dot_general | solution.py:20
  275.1 6.6 fusion.37.refs_16_
  281.8 7.6 %multiply_reduce_fusion.2 = (f32[1024]{0:T(1024)}, f32[256]{0:T(256)S(1)}, f32[256,1024]{1,0:T(8,128)S(1)}) fusion(f32[256,1024]{1,0:T(8,128)S(1)} %get-tuple-element.268, f32[256]{0:T(256)S(1)} %fusion.151, f32[256]{0:T(256)S(1)} %broadcast_multiply_fusion, f32[1024]{0:T(1024)S(1)} %bitcast.258, bf16[256,4096]{1,0:T(8,128)(2,1)S(1)} %fusion.37.refs_16_, ...), kind=kOutput, calls=%fused_computation.118 | convolution fusion | flops 2149317376 | bytes 12594176 | tf_op jit(solution)/shard_map/dot_general | solution.py:28
  291.8 1.5 fusion.85.refs_13_
  293.3 98.6 %unmix_reduce.2 = (bf16[256,3072]{1,0:T(8,128)(2,1)}, f32[3,3072]{1,0:T(4,128)}, f32[1,1024]{1,0:T(1,128)}, f32[1024,256]{1,0:T(8,128)}, bf16[256,512]{1,0:T(8,1...) custom-call(f32[4,4]{1,0:T(4,128)} %copy-done.20, ...), custom_call_target="tpu_custom_call" | custom-call | bytes 332100000 | tf_op jit(solution)/shard_map/unmix_reduce/pallas_call | solution.py:987
  392.0 5.5 fusion.101
  397.5 1.1 fusion.95
  399.7 7.5 %fusion.30.refs_16_ = bf16[256,4096]{1,0:T(8,128)(2,1)S(1)} fusion(f32[256,4096]{1,0:T(8,128)S(1)} %copy-done.155, bf16[256,1024]{1,0:T(8,128)(2,1)S(1)} %add_convert_fusion.1.refs_17_, bf16[8192,1024]{1,0:T(8,128)(2,1)} %get-tuple-element.109), kind=kOutput, calls=%fused_computation.34 | convolution fusion | flops 2168455168 | bytes 15204352 | tf_op jit(solution)/shard_map/dot_general | solution.py:28
  407.6 3.2 multiply_reduce_fusion
  413.4 1.5 fusion.82.refs_13_
  414.9 139.3 %unmix_reduce.3 = (bf16[256,3072]{1,0:T(8,128)(2,1)}, f32[3,3072]{1,0:T(4,128)}, f32[1,1024]{1,0:T(1,128)}, f32[1024,256]{1,0:T(8,128)}, bf16[256,512]{1,0:T(8,1...) custom-call(f32[4,4]{1,0:T(4,128)} %copy-done.20, ...), custom_call_target="tpu_custom_call" | custom-call | bytes 332100000 | tf_op jit(solution)/shard_map/unmix_reduce/pallas_call | solution.py:987
  554.3 5.4 fusion.99
  559.7 1.1 fusion.97
  560.8 1.6 broadcast_select_fusion
  562.8 6.7 broadcast_select_fusion.2
  569.9 3.2 multiply_reduce_fusion.8
  573.2 1.7 convolution_dynamic-update-slice_fusion
  577.1 1.3 reshape.1015
  578.5 3.7 multiply_reduce_fusion.9
  582.2 2.7 multiply_reduce_fusion.1
  585.8 1.3 reduce.13
  588.7 1.7 convolution_dynamic-update-slice_fusion.1
  591.2 1.6 fusion.126
  595.8 123.4 %reduce.14 = (bf16[256,384]{1,0:T(8,128)(2,1)}, bf16[256,384]{1,0:T(8,128)(2,1)}, bf16[256,384]{1,0:T(8,128)(2,1)}, bf16[256,384]{1,0:T(8,128)(2,1)}, bf16[256,5...) custom-call(bf16[256,1024]{1,0:T(8,128)(2,1)} %copy-done.48, ...), custom_call_target="tpu_custom_call" | custom-call | bytes 332100000 | tf_op jit(solution)/shard_map/reduce/pallas_call | solution.py:987
  723.6 1.9 fusion.104
  725.6 1.4 fusion.105
  727.0 2.6 maximum_convert_fusion.1
  731.4 2.5 maximum_convert_fusion
  734.2 1.1 maximum_convert_fusion.3
  736.5 2.0 maximum_convert_fusion.2
  739.1 1.1 select_bitcast_fusion.1
  740.3 1.1 maximum_bitcast_fusion.1
  741.4 1.1 select_bitcast_fusion.3
  742.5 1.1 maximum_bitcast_fusion
  (484 shorter events, 42.8 us)
Async XLA Ops:
  11.3 162.4 %copy-start.154 = (s32[2,4]{1,0:T(2,128)S(1)}, s32[2,4]{1,0:T(2,128)}, u32[]{:S(2)}) copy-start(s32[2,4]{1,0:T(2,128)} %param.22) | copy-start | bytes 100
  11.3 163.8 %copy-start.37 = (f32[1024,33]{1,0:T(8,128)S(1)}, f32[1024,33]{1,0:T(8,128)}, u32[]{:S(2)}) copy-start(f32[1024,33]{1,0:T(8,128)} %constant.90.clone) | copy-start | bytes 405508
  172.2 8.2 %copy-start.64 = (bf16[1,4,16,1024]{3,2,1,0:T(8,128)(2,1)}, bf16[1,4,16,1024]{3,2,1,0:T(8,128)(2,1)S(1)}, u32[]{:S(2)}) copy-start(bf16[1,4,16,1024]{3,2,1,0:T(8,128)(2,1)S(1)} %get-tuple-element.234) | copy-start | bytes 393220
  183.0 57.1 %copy-start.20 = (f32[4,4]{1,0:T(4,128)}, f32[4,4]{1,0:T(4,128)S(1)}, u32[]{:S(2)}) copy-start(f32[4,4]{1,0:T(4,128)S(1)} %compare_convert_fusion.same_ref.refs_0_) | copy-start | bytes 196
  187.6 52.6 %copy-start.6 = (f32[256,1]{1,0:T(8,128)}, f32[256,1]{1,0:T(8,128)S(1)}, u32[]{:S(2)}) copy-start(f32[256,1]{1,0:T(8,128)S(1)} %fusion.136.valid_ref.refs_10_) | copy-start | bytes 3076
  193.7 28.2 %copy-start = (f32[4,512,256]{2,1,0:T(8,128)}, f32[4,512,256]{2,1,0:T(8,128)S(1)}, u32[]{:S(2)}) copy-start(f32[4,512,256]{2,1,0:T(8,128)S(1)} %get-tuple-element.257.filt_ref.refs_5_) | copy-start | bytes 6291460
  193.7 46.4 %copy-start.1 = (f32[4,512,256]{2,1,0:T(8,128)}, f32[4,512,256]{2,1,0:T(8,128)S(1)}, u32[]{:S(2)}) copy-start(f32[4,512,256]{2,1,0:T(8,128)S(1)} %get-tuple-element.256.filt_ref.refs_5_) | copy-start | bytes 6291460
  193.7 25.2 %copy-start.40 = (bf16[2,256,1024]{2,1,0:T(8,128)(2,1)S(1)}, bf16[2,256,1024]{2,1,0:T(8,128)(2,1)}, u32[]{:S(2)}) copy-start(bf16[2,256,1024]{2,1,0:T(8,128)(2,1)} %param.20) | copy-start | bytes 3145732
  221.9 9.6 %copy-start.29 = (f32[256,1024]{1,0:T(8,128)}, f32[256,1024]{1,0:T(8,128)S(1)}, u32[]{:S(2)}) copy-start(f32[256,1024]{1,0:T(8,128)S(1)} %get-tuple-element.262) | copy-start | bytes 3145732
  221.9 9.5 %copy-start.127 = (f32[256]{0:T(256)}, f32[256]{0:T(256)S(1)}, u32[]{:S(2)}) copy-start(f32[256]{0:T(256)S(1)} %broadcast_multiply_fusion.2) | copy-start | bytes 3076
  222.2 9.3 %copy-start.143 = (f32[256]{0:T(256)}, f32[256]{0:T(256)S(1)}, u32[]{:S(2)}) copy-start(f32[256]{0:T(256)S(1)} %multiply_reduce_fusion.7) | copy-start | bytes 3076
  222.2 9.3 %copy-start.137 = (f32[256]{0:T(256)}, f32[256]{0:T(256)S(1)}, u32[]{:S(2)}) copy-start(f32[256]{0:T(256)S(1)} %fusion.149) | copy-start | bytes 3076
  222.2 9.3 %slice-start.2 = ((s8[16777216]{0:T(1024)(128)(4,1)}), s8[4194304]{0:T(1024)(128)(4,1)S(1)}, s32[]{:S(2)}) async-start(s8[16777216]{0:T(1024)(128)(4,1)} %bitcast.269), calls=%async_computation.2 | async-start | bytes 8388608
  222.5 9.0 %copy-start.49 = (bf16[256,1024]{1,0:T(8,128)(2,1)}, bf16[256,1024]{1,0:T(8,128)(2,1)S(1)}, u32[]{:S(2)}) copy-start(bf16[256,1024]{1,0:T(8,128)(2,1)S(1)} %multiply_convert_fusion.4.refs_14_) | copy-start | bytes 1572868
  222.5 9.0 %slice-start.3 = ((s8[16777216]{0:T(1024)(128)(4,1)}), s8[4194304]{0:T(1024)(128)(4,1)S(1)}, s32[]{:S(2)}) async-start(s8[16777216]{0:T(1024)(128)(4,1)} %bitcast.269), calls=%async_computation.3 | async-start | bytes 8388608
  222.5 9.0 %slice-start.4 = ((s8[16777216]{0:T(1024)(128)(4,1)}), s8[4194304]{0:T(1024)(128)(4,1)S(1)}, s32[]{:S(2)}) async-start(s8[16777216]{0:T(1024)(128)(4,1)} %bitcast.269), calls=%async_computation.4 | async-start | bytes 8388608
  222.5 9.0 %slice-start.5 = ((s8[16777216]{0:T(1024)(128)(4,1)}), s8[4194304]{0:T(1024)(128)(4,1)S(1)}, s32[]{:S(2)}) async-start(s8[16777216]{0:T(1024)(128)(4,1)} %bitcast.269), calls=%async_computation.5 | async-start | bytes 8388608
  240.0 24.5 %copy-start.2 = (bf16[256,3072]{1,0:T(8,128)(2,1)}, bf16[256,3072]{1,0:T(8,128)(2,1)S(1)}, u32[]{:S(2)}) copy-start(bf16[256,3072]{1,0:T(8,128)(2,1)S(1)} %fusion.41.proj_ref.refs_6_) | copy-start | bytes 4718596
  240.0 23.7 %copy-start.151 = (bf16[2048,1024]{1,0:T(8,128)(2,1)S(1)}, bf16[2048,1024]{1,0:T(8,128)(2,1)}, u32[]{:S(2)}) copy-start(bf16[2048,1024]{1,0:T(8,128)(2,1)} %get-tuple-element.107) | copy-start | bytes 12582916
  240.1 24.5 %copy-start.22 = (f32[1,1,4,256]{3,1,2,0:T(1,128)}, f32[1,1,4,256]{3,1,2,0:T(1,128)S(1)}, u32[]{:S(2)}) copy-start(f32[1,1,4,256]{3,1,2,0:T(1,128)S(1)} %copy.69) | copy-start | bytes 12292
  240.1 24.5 %copy-start.17 = (f32[1,3,4,768]{3,1,2,0:T(4,128)}, f32[1,3,4,768]{3,1,2,0:T(4,128)S(1)}, u32[]{:S(2)}) copy-start(f32[1,3,4,768]{3,1,2,0:T(4,128)S(1)} %copy.68) | copy-start | bytes 110596
  264.6 10.5 %slice-start.6 = ((s8[16777216]{0:T(1024)(128)(4,1)}), s8[4194304]{0:T(1024)(128)(4,1)S(1)}, s32[]{:S(2)}) async-start(s8[16777216]{0:T(1024)(128)(4,1)} %bitcast.271), calls=%async_computation.6 | async-start | bytes 8388608
  265.1 9.9 %copy-start.50 = (bf16[256,1024]{1,0:T(8,128)(2,1)}, bf16[256,1024]{1,0:T(8,128)(2,1)S(1)}, u32[]{:S(2)}) copy-start(bf16[256,1024]{1,0:T(8,128)(2,1)S(1)} %multiply_convert_fusion.2.refs_14_) | copy-start | bytes 1572868
  265.2 9.9 %copy-start.46 = (bf16[2,256,1024]{2,1,0:T(8,128)(2,1)S(1)}, bf16[2,256,1024]{2,1,0:T(8,128)(2,1)}, u32[]{:S(2)}) copy-start(bf16[2,256,1024]{2,1,0:T(8,128)(2,1)} %param.21) | copy-start | bytes 3145732
  265.2 9.9 %slice-start.7 = ((s8[16777216]{0:T(1024)(128)(4,1)}), s8[4194304]{0:T(1024)(128)(4,1)S(1)}, s32[]{:S(2)}) async-start(s8[16777216]{0:T(1024)(128)(4,1)} %bitcast.271), calls=%async_computation.7 | async-start | bytes 8388608
  265.2 9.9 %slice-start.8 = ((s8[16777216]{0:T(1024)(128)(4,1)}), s8[4194304]{0:T(1024)(128)(4,1)S(1)}, s32[]{:S(2)}) async-start(s8[16777216]{0:T(1024)(128)(4,1)} %bitcast.271), calls=%async_computation.8 | async-start | bytes 8388608
  265.2 9.9 %slice-start.9 = ((s8[16777216]{0:T(1024)(128)(4,1)}), s8[4194304]{0:T(1024)(128)(4,1)S(1)}, s32[]{:S(2)}) async-start(s8[16777216]{0:T(1024)(128)(4,1)} %bitcast.271), calls=%async_computation.9 | async-start | bytes 8388608
  293.3 98.6 %copy-start.114 = (f32[256]{0:T(256)S(1)}, f32[256]{0:T(256)}, u32[]{:S(2)}) copy-start(f32[256]{0:T(256)} %copy-done.113) | copy-start | bytes 3076
  398.6 8.6 %slice-start.10 = ((s8[16777216]{0:T(1024)(128)(4,1)}), s8[4194304]{0:T(1024)(128)(4,1)S(1)}, s32[]{:S(2)}) async-start(s8[16777216]{0:T(1024)(128)(4,1)} %bitcast.273), calls=%async_computation.10 | async-start | bytes 8388608
  399.1 12.1 %copy-start.27 = (bf16[256,1024]{1,0:T(8,128)(2,1)}, bf16[256,1024]{1,0:T(8,128)(2,1)S(1)}, u32[]{:S(2)}) copy-start(bf16[256,1024]{1,0:T(8,128)(2,1)S(1)} %add_convert_fusion.1.refs_17_) | copy-start | bytes 1572868
  413.4 140.9 %copy-start.54 = (bf16[256,1024]{1,0:T(8,128)(2,1)}, bf16[256,1024]{1,0:T(8,128)(2,1)S(1)}, u32[]{:S(2)}) copy-start(bf16[256,1024]{1,0:T(8,128)(2,1)S(1)} %fusion.115.refs_7_) | copy-start | bytes 1572868
  414.9 139.3 %copy-start.116 = (f32[256]{0:T(256)S(1)}, f32[256]{0:T(256)}, u32[]{:S(2)}) copy-start(f32[256]{0:T(256)} %copy-done.115) | copy-start | bytes 3076
  562.4 176.7 %collective-permute-start.1 = (bf16[256,1024]{1,0:T(8,128)(2,1)}, bf16[256,1024]{1,0:T(8,128)(2,1)}, u32[]{:S(2)}, u32[]{:S(2)}) collective-permute-start(bf16[256,1024]{1,0:T(8,128)(2,1)} %get-tuple-element.224), channel_id=1, source_target_pairs={{0,16},{16,0},{1,17},{17,1},{2,18},{18,2},{3,19},{19,3},{4,20},{20... | collective-permute-start | bytes 1572872 | tf_op jit(solution)/shard_map/ppermute | solution.py:478
  569.6 8.9 %copy-start.31 = (f32[1024,256]{1,0:T(8,128)S(1)}, f32[1024,256]{1,0:T(8,128)}, u32[]{:S(2)}) copy-start(f32[1024,256]{1,0:T(8,128)} %get-tuple-element.127) | copy-start | bytes 3145732
  569.6 8.9 %copy-start.45 = (f32[1024,64]{0,1:T(8,128)S(1)}, f32[1024,64]{0,1:T(8,128)}, u32[]{:S(2)}) copy-start(f32[1024,64]{0,1:T(8,128)} %copy-done.44) | copy-start | bytes 786436
  569.6 8.9 %copy-start.118 = (f32[256]{0:T(256)S(1)}, f32[256]{0:T(256)}, u32[]{:S(2)}) copy-start(f32[256]{0:T(256)} %copy-done.117) | copy-start | bytes 3076
  569.6 12.6 %copy-start.33 = (f32[1024,256]{1,0:T(8,128)S(1)}, f32[1024,256]{1,0:T(8,128)}, u32[]{:S(2)}) copy-start(f32[1024,256]{1,0:T(8,128)} %get-tuple-element.130) | copy-start | bytes 3145732
  569.6 171.8 %collective-permute-start = (bf16[256,1024]{1,0:T(8,128)(2,1)}, bf16[256,1024]{1,0:T(8,128)(2,1)}, u32[]{:S(2)}, u32[]{:S(2)}) collective-permute-start(bf16[256,1024]{1,0:T(8,128)(2,1)} %get-tuple-element.271), channel_id=1, source_target_pairs={{0,16},{16,0},{1,17},{17,1},{2,18},{18,2},{3,19},{19,3},{4,20},{20... | collective-permute-start | bytes 1572872 | tf_op jit(solution)/shard_map/ppermute | solution.py:478
  575.6 9.6 %copy-start.122 = (f32[1024]{0:T(1024)S(1)}, f32[1024]{0:T(1024)}, u32[]{:S(2)}) copy-start(f32[1024]{0:T(1024)} %get-tuple-element.208) | copy-start | bytes 12292
  575.7 9.6 %copy-start.111 = (f32[3,3072]{1,0:T(4,128)S(1)}, f32[3,3072]{1,0:T(4,128)}, u32[]{:S(2)}) copy-start(f32[3,3072]{1,0:T(4,128)} %get-tuple-element.131) | copy-start | bytes 110596
  576.4 11.5 %copy-start.112 = (f32[4,528]{1,0:T(4,128)S(1)}, f32[4,528]{1,0:T(4,128)}, u32[]{:S(2)}) copy-start(f32[4,528]{1,0:T(4,128)} %reshape.1013) | copy-start | bytes 25348
  578.4 10.3 %copy-start.136 = (f32[64]{0:T(128)S(1)}, f32[64]{0:T(128)}, u32[]{:S(2)}) copy-start(f32[64]{0:T(128)} %copy-done.135) | copy-start | bytes 772
  582.2 11.0 %copy-start.121 = (f32[1024]{0:T(1024)S(1)}, f32[1024]{0:T(1024)}, u32[]{:S(2)}) copy-start(f32[1024]{0:T(1024)} %get-tuple-element.214) | copy-start | bytes 12292
  582.2 11.0 %copy-start.110 = (f32[3,3072]{1,0:T(4,128)S(1)}, f32[3,3072]{1,0:T(4,128)}, u32[]{:S(2)}) copy-start(f32[3,3072]{1,0:T(4,128)} %get-tuple-element.128) | copy-start | bytes 110596
  584.9 8.2 %copy-start.147 = (f32[64]{0:T(128)S(1)}, f32[64]{0:T(128)}, u32[]{:S(2)}) copy-start(f32[64]{0:T(128)} %get-tuple-element.218) | copy-start | bytes 772
  584.9 8.4 %copy-start.146 = (f32[1,1024]{1,0:T(1,128)S(1)}, f32[1,1024]{1,0:T(1,128)}, u32[]{:S(2)}) copy-start(f32[1,1024]{1,0:T(1,128)} %get-tuple-element.129) | copy-start | bytes 12292
  584.9 9.1 %copy-start.145 = (f32[1024]{0:T(1024)S(1)}, f32[1024]{0:T(1024)}, u32[]{:S(2)}) copy-start(f32[1024]{0:T(1024)} %get-tuple-element.212) | copy-start | bytes 12292
  584.9 9.3 %copy-start.61 = (f32[64,1024]{1,0:T(8,128)S(1)}, f32[64,1024]{1,0:T(8,128)}, u32[]{:S(2)}) copy-start(f32[64,1024]{1,0:T(8,128)} %copy-done.60) | copy-start | bytes 786436
  (124 other events, 458.3 us)

commit v5 on v4

--- a/solution.py
+++ b/solution.py
@@ -913,13 +913,16 @@
 
 def mixing_order(rest, summed):
     words = (
-        "load0 mix0 core0 core1 fill0 go0 load1 core2 fill1 go1 core3 mix1 load2 fill2 wait0 turn0 go2 meet0 fill3 wait1 turn1 "
-        "go3 meet1 load3 own0 mix2 settle0 meet2 own1 wait2 turn2 settle1 finish0 meet3 own2 Meet0 wait3 turn3 settle2 finish1 "
-        "Meet1 mix3 own3 settle3 Settle0 finish2 Settle1 finish3 Finish0 Finish1"
+        ("load", 0), ("mix", 0), ("core", 0), ("core", 1), ("fill", 0), ("go", 0), ("load", 1), ("core", 2),
+        ("fill", 1), ("go", 1), ("core", 3), ("mix", 1), ("load", 2), ("fill", 2), ("wait", 0), ("turn", 0),
+        ("go", 2), ("meet", 0), ("fill", 3), ("wait", 1), ("turn", 1), ("go", 3), ("meet", 1), ("load", 3),
+        ("own", 0), ("mix", 2), ("settle", 0), ("meet", 2), ("own", 1), ("wait", 2), ("turn", 2), ("settle", 1),
+        ("finish", 0), ("meet", 3), ("own", 2), ("Meet", 0), ("wait", 3), ("turn", 3), ("settle", 2), ("finish", 1),
+        ("Meet", 1), ("mix", 3), ("own", 3), ("settle", 3), ("Settle", 0), ("finish", 2), ("Settle", 1),
+        ("finish", 3), ("Finish", 0), ("Finish", 1),
     )
     steps = []
-    for word in words.split():
-        name, number = word[:-1], int(word[-1])
+    for name, number in words:
         if name in ("load", "meet", "settle", "finish"):
             steps += [(name, rest[number])] if number < len(rest) else []
         elif name in ("Meet", "Settle", "Finish"):

time: 754 us -> 754 us (level)
  no operation moved by 1% of the time
where the time goes in v5:
time: 754 us; the launch traced here: 744 us
  Pallas kernels  570 us (76%)
  matrix products  98.4 us (13%)
  other arithmetic  41.9 us (6%)
  local copies, waits for them, and re-layouts  27.6 us (4%)
    pallas_call x3, Pallas kernels, reduce_call(): pl.pallas_call(functools.partial(reduce_kernel, items, pieces[whole:], ha...  361 us
    pallas_call x1, Pallas kernels, gather_shards(): pl.pallas_call(functools.partial(gather_kernel, chunks, heights, count),...  161 us
    pallas_call x2, Pallas kernels, mix(): pl.pallas_call(functools.partial(mix_kernel, blocks, rows, 32), out_shape...  47.9 us
    dot_general x8, matrix products, dot(): return jnp.dot(left, right, preferred_element_type=F32)  41.3 us
    dot_general x8, matrix products, dot_right(): lax.dot_general(left, right, (((1,), (1,)), ((), ())), preferred_element_...  38.8 us
    unnamed x352, local copies, waits for them, and re-layouts  16.2 us
  transfers between devices with their start and end apart: 2, of which 0 were waited for; matrix products, arithmetic and copies ran while one was open for 7% of the time, Pallas kernels for 17%

profile of v5, /device:TPU:0, one launch (start us, length us, event | category | flops | bytes accessed | tf_op | source)
XLA Modules:
  0.0 744.0 jit_solution(14856761739544943675)
XLA Ops:
  5.0 1.4 concatenate.191
  7.2 1.6 copy-done.7
  8.8 1.4 copy-done.8
  10.2 1.0 copy-done.9
  11.3 160.7 %gather_shards.1 = (bf16[256,1024]{1,0:T(8,128)(2,1)S(1)}, bf16[2048,1024]{1,0:T(8,128)(2,1)}, bf16[2048,3072]{1,0:T(8,128)(2,1)}, bf16[2048,4096]{1,0:T(8,128)(2,1)}, bf16[8192,1024]{1,0:T(8,128)(2,1)}) custom-call(bf16[32,1024]{1,0:T(8,128)(2,1)S(1)} %fusion.138.refs_0_, bf16[256,1024]{1,0:T(8,128)(2,1)S(1)} %bitcast.202, bf16[256,3072]{1,0:T(8,128)(2,1)S(1)} %bitcast.201, ...), custom_call_target="tpu_custom_call" | custom-call | bytes 701100032 | tf_op jit(solution)/shard_map/gather_shards/pallas_call | solution.py:623
  176.2 1.5 fusion.128
  177.7 2.7 multiply_convert_fusion.3
  187.9 4.8 fusion.38.proj_ref.refs_6_
  194.4 24.4 %mix.2 = (bf16[16,3072]{1,0:T(8,128)(2,1)S(1)}, bf16[1024,256]{1,0:T(8,128)(2,1)S(1)}, bf16[256,1024]{1,0:T(8,128)(2,1)S(1)}, bf16[256,1024]{1,0:T(8,128)(2,1)S(1)}) custom-call(f32[4,4]{1,0:T(4,128)S(1)} %compare_convert_fusion.same_ref.refs_0_, f32[1]{0:T(128)} %bitcast.2.carried_ref.refs_1_, bf16[512,256]{1,0:T(8,128)(2,1)S(1)} %copy-done.4, ...), custom_call_target="tpu_custom_call" | custom-call | bytes 81180000 | tf_op jit(solution)/shard_map/mix/pallas_call | solution.py:314
  218.9 3.0 fusion.162
  222.5 8.9 %multiply_convert_fusion.1 = (bf16[256,4096]{1,0:T(8,128)(2,1)S(1)}, f32[256,4096]{1,0:T(8,128)}) fusion(bf16[256,1024]{1,0:T(8,128)(2,1)S(1)} %multiply_convert_fusion.4.refs_14_, bf16[2048,4096]{1,0:T(8,128)(2,1)} %get-tuple-element.108), kind=kOutput, calls=%fused_computation.43 | convolution fusion | flops 2156920832 | bytes 15204352 | tf_op jit(solution)/shard_map/dot_general | solution.py:20
  231.5 2.5 convert_reduce_fusion
  235.2 4.8 fusion.41.proj_ref.refs_6_
  240.2 23.5 %mix.3 = (bf16[16,3072]{1,0:T(8,128)(2,1)S(1)}, bf16[1024,256]{1,0:T(8,128)(2,1)S(1)}, bf16[256,1024]{1,0:T(8,128)(2,1)S(1)}, bf16[256,1024]{1,0:T(8,128)(2,1)S(1)}) custom-call(f32[4,4]{1,0:T(4,128)S(1)} %compare_convert_fusion.same_ref.refs_0_, f32[1]{0:T(128)} %bitcast.2.carried_ref.refs_1_, bf16[512,256]{1,0:T(8,128)(2,1)S(1)} %copy-done.4, ...), custom_call_target="tpu_custom_call" | custom-call | bytes 81180000 | tf_op jit(solution)/shard_map/mix/pallas_call | solution.py:314
  265.2 9.8 %multiply_convert_fusion = (bf16[256,4096]{1,0:T(8,128)(2,1)}, f32[256,4096]{1,0:T(8,128)}) fusion(bf16[256,1024]{1,0:T(8,128)(2,1)S(1)} %multiply_convert_fusion.2.refs_14_, bf16[2048,4096]{1,0:T(8,128)(2,1)} %get-tuple-element.108), kind=kOutput, calls=%fused_computation.42 | convolution fusion | flops 2156920832 | bytes 15204352 | tf_op jit(solution)/shard_map/dot_general | solution.py:20
  275.1 6.6 fusion.37.refs_16_
  281.8 7.6 %multiply_reduce_fusion.2 = (f32[1024]{0:T(1024)}, f32[256]{0:T(256)S(1)}, f32[256,1024]{1,0:T(8,128)S(1)}) fusion(f32[256,1024]{1,0:T(8,128)S(1)} %get-tuple-element.268, f32[256]{0:T(256)S(1)} %fusion.151, f32[256]{0:T(256)S(1)} %broadcast_multiply_fusion, f32[1024]{0:T(1024)S(1)} %bitcast.258, bf16[256,4096]{1,0:T(8,128)(2,1)S(1)} %fusion.37.refs_16_, ...), kind=kOutput, calls=%fused_computation.118 | convolution fusion | flops 2149317376 | bytes 12594176 | tf_op jit(solution)/shard_map/dot_general | solution.py:28
  291.8 1.5 fusion.85.refs_13_
  293.3 98.6 %unmix_reduce.2 = (bf16[256,3072]{1,0:T(8,128)(2,1)}, f32[3,3072]{1,0:T(4,128)}, f32[1,1024]{1,0:T(1,128)}, f32[1024,256]{1,0:T(8,128)}, bf16[256,512]{1,0:T(8,1...) custom-call(f32[4,4]{1,0:T(4,128)} %copy-done.20, ...), custom_call_target="tpu_custom_call" | custom-call | bytes 332100000 | tf_op jit(solution)/shard_map/unmix_reduce/pallas_call | solution.py:990
  392.0 5.5 fusion.101
  397.5 1.1 fusion.95
  399.7 7.5 %fusion.30.refs_16_ = bf16[256,4096]{1,0:T(8,128)(2,1)S(1)} fusion(f32[256,4096]{1,0:T(8,128)S(1)} %copy-done.155, bf16[256,1024]{1,0:T(8,128)(2,1)S(1)} %add_convert_fusion.1.refs_17_, bf16[8192,1024]{1,0:T(8,128)(2,1)} %get-tuple-element.109), kind=kOutput, calls=%fused_computation.34 | convolution fusion | flops 2168455168 | bytes 15204352 | tf_op jit(solution)/shard_map/dot_general | solution.py:28
  407.6 3.2 multiply_reduce_fusion
  413.4 1.5 fusion.82.refs_13_
  414.9 139.3 %unmix_reduce.3 = (bf16[256,3072]{1,0:T(8,128)(2,1)}, f32[3,3072]{1,0:T(4,128)}, f32[1,1024]{1,0:T(1,128)}, f32[1024,256]{1,0:T(8,128)}, bf16[256,512]{1,0:T(8,1...) custom-call(f32[4,4]{1,0:T(4,128)} %copy-done.20, ...), custom_call_target="tpu_custom_call" | custom-call | bytes 332100000 | tf_op jit(solution)/shard_map/unmix_reduce/pallas_call | solution.py:990
  554.3 5.4 fusion.99
  559.7 1.1 fusion.97
  560.8 1.6 broadcast_select_fusion
  562.8 6.7 broadcast_select_fusion.2
  569.9 3.2 multiply_reduce_fusion.8
  573.2 1.7 convolution_dynamic-update-slice_fusion
  577.1 1.3 reshape.1015
  578.5 3.7 multiply_reduce_fusion.9
  582.2 2.7 multiply_reduce_fusion.1
  585.8 1.3 reduce.13
  588.7 1.7 convolution_dynamic-update-slice_fusion.1
  591.2 1.6 fusion.126
  595.8 123.4 %reduce.14 = (bf16[256,384]{1,0:T(8,128)(2,1)}, bf16[256,384]{1,0:T(8,128)(2,1)}, bf16[256,384]{1,0:T(8,128)(2,1)}, bf16[256,384]{1,0:T(8,128)(2,1)}, bf16[256,5...) custom-call(bf16[256,1024]{1,0:T(8,128)(2,1)} %copy-done.48, ...), custom_call_target="tpu_custom_call" | custom-call | bytes 332100000 | tf_op jit(solution)/shard_map/reduce/pallas_call | solution.py:990
  723.6 1.9 fusion.104
  725.6 1.4 fusion.105
  727.0 2.6 maximum_convert_fusion.1
  731.4 2.5 maximum_convert_fusion
  734.2 1.1 maximum_convert_fusion.3
  736.5 2.0 maximum_convert_fusion.2
  739.1 1.1 select_bitcast_fusion.1
  740.3 1.1 maximum_bitcast_fusion.1
  741.4 1.1 select_bitcast_fusion.3
  742.5 1.1 maximum_bitcast_fusion
  (484 shorter events, 42.8 us)
Async XLA Ops:
  11.3 162.4 %copy-start.154 = (s32[2,4]{1,0:T(2,128)S(1)}, s32[2,4]{1,0:T(2,128)}, u32[]{:S(2)}) copy-start(s32[2,4]{1,0:T(2,128)} %param.22) | copy-start | bytes 100
  11.3 163.8 %copy-start.37 = (f32[1024,33]{1,0:T(8,128)S(1)}, f32[1024,33]{1,0:T(8,128)}, u32[]{:S(2)}) copy-start(f32[1024,33]{1,0:T(8,128)} %constant.90.clone) | copy-start | bytes 405508
  172.2 8.2 %copy-start.64 = (bf16[1,4,16,1024]{3,2,1,0:T(8,128)(2,1)}, bf16[1,4,16,1024]{3,2,1,0:T(8,128)(2,1)S(1)}, u32[]{:S(2)}) copy-start(bf16[1,4,16,1024]{3,2,1,0:T(8,128)(2,1)S(1)} %get-tuple-element.234) | copy-start | bytes 393220
  183.0 57.1 %copy-start.20 = (f32[4,4]{1,0:T(4,128)}, f32[4,4]{1,0:T(4,128)S(1)}, u32[]{:S(2)}) copy-start(f32[4,4]{1,0:T(4,128)S(1)} %compare_convert_fusion.same_ref.refs_0_) | copy-start | bytes 196
  187.6 52.6 %copy-start.6 = (f32[256,1]{1,0:T(8,128)}, f32[256,1]{1,0:T(8,128)S(1)}, u32[]{:S(2)}) copy-start(f32[256,1]{1,0:T(8,128)S(1)} %fusion.136.valid_ref.refs_10_) | copy-start | bytes 3076
  193.7 28.2 %copy-start = (f32[4,512,256]{2,1,0:T(8,128)}, f32[4,512,256]{2,1,0:T(8,128)S(1)}, u32[]{:S(2)}) copy-start(f32[4,512,256]{2,1,0:T(8,128)S(1)} %get-tuple-element.257.filt_ref.refs_5_) | copy-start | bytes 6291460
  193.7 46.4 %copy-start.1 = (f32[4,512,256]{2,1,0:T(8,128)}, f32[4,512,256]{2,1,0:T(8,128)S(1)}, u32[]{:S(2)}) copy-start(f32[4,512,256]{2,1,0:T(8,128)S(1)} %get-tuple-element.256.filt_ref.refs_5_) | copy-start | bytes 6291460
  193.7 25.2 %copy-start.40 = (bf16[2,256,1024]{2,1,0:T(8,128)(2,1)S(1)}, bf16[2,256,1024]{2,1,0:T(8,128)(2,1)}, u32[]{:S(2)}) copy-start(bf16[2,256,1024]{2,1,0:T(8,128)(2,1)} %param.20) | copy-start | bytes 3145732
  221.9 9.6 %copy-start.29 = (f32[256,1024]{1,0:T(8,128)}, f32[256,1024]{1,0:T(8,128)S(1)}, u32[]{:S(2)}) copy-start(f32[256,1024]{1,0:T(8,128)S(1)} %get-tuple-element.262) | copy-start | bytes 3145732
  221.9 9.5 %copy-start.127 = (f32[256]{0:T(256)}, f32[256]{0:T(256)S(1)}, u32[]{:S(2)}) copy-start(f32[256]{0:T(256)S(1)} %broadcast_multiply_fusion.2) | copy-start | bytes 3076
  222.2 9.3 %copy-start.143 = (f32[256]{0:T(256)}, f32[256]{0:T(256)S(1)}, u32[]{:S(2)}) copy-start(f32[256]{0:T(256)S(1)} %multiply_reduce_fusion.7) | copy-start | bytes 3076
  222.2 9.3 %copy-start.137 = (f32[256]{0:T(256)}, f32[256]{0:T(256)S(1)}, u32[]{:S(2)}) copy-start(f32[256]{0:T(256)S(1)} %fusion.149) | copy-start | bytes 3076
  222.2 9.3 %slice-start.2 = ((s8[16777216]{0:T(1024)(128)(4,1)}), s8[4194304]{0:T(1024)(128)(4,1)S(1)}, s32[]{:S(2)}) async-start(s8[16777216]{0:T(1024)(128)(4,1)} %bitcast.269), calls=%async_computation.2 | async-start | bytes 8388608
  222.5 9.0 %copy-start.49 = (bf16[256,1024]{1,0:T(8,128)(2,1)}, bf16[256,1024]{1,0:T(8,128)(2,1)S(1)}, u32[]{:S(2)}) copy-start(bf16[256,1024]{1,0:T(8,128)(2,1)S(1)} %multiply_convert_fusion.4.refs_14_) | copy-start | bytes 1572868
  222.5 9.0 %slice-start.3 = ((s8[16777216]{0:T(1024)(128)(4,1)}), s8[4194304]{0:T(1024)(128)(4,1)S(1)}, s32[]{:S(2)}) async-start(s8[16777216]{0:T(1024)(128)(4,1)} %bitcast.269), calls=%async_computation.3 | async-start | bytes 8388608
  222.5 9.0 %slice-start.4 = ((s8[16777216]{0:T(1024)(128)(4,1)}), s8[4194304]{0:T(1024)(128)(4,1)S(1)}, s32[]{:S(2)}) async-start(s8[16777216]{0:T(1024)(128)(4,1)} %bitcast.269), calls=%async_computation.4 | async-start | bytes 8388608
  222.5 9.0 %slice-start.5 = ((s8[16777216]{0:T(1024)(128)(4,1)}), s8[4194304]{0:T(1024)(128)(4,1)S(1)}, s32[]{:S(2)}) async-start(s8[16777216]{0:T(1024)(128)(4,1)} %bitcast.269), calls=%async_computation.5 | async-start | bytes 8388608
  240.0 24.5 %copy-start.2 = (bf16[256,3072]{1,0:T(8,128)(2,1)}, bf16[256,3072]{1,0:T(8,128)(2,1)S(1)}, u32[]{:S(2)}) copy-start(bf16[256,3072]{1,0:T(8,128)(2,1)S(1)} %fusion.41.proj_ref.refs_6_) | copy-start | bytes 4718596
  240.0 23.7 %copy-start.151 = (bf16[2048,1024]{1,0:T(8,128)(2,1)S(1)}, bf16[2048,1024]{1,0:T(8,128)(2,1)}, u32[]{:S(2)}) copy-start(bf16[2048,1024]{1,0:T(8,128)(2,1)} %get-tuple-element.107) | copy-start | bytes 12582916
  240.1 24.5 %copy-start.22 = (f32[1,1,4,256]{3,1,2,0:T(1,128)}, f32[1,1,4,256]{3,1,2,0:T(1,128)S(1)}, u32[]{:S(2)}) copy-start(f32[1,1,4,256]{3,1,2,0:T(1,128)S(1)} %copy.69) | copy-start | bytes 12292
  240.1 24.5 %copy-start.17 = (f32[1,3,4,768]{3,1,2,0:T(4,128)}, f32[1,3,4,768]{3,1,2,0:T(4,128)S(1)}, u32[]{:S(2)}) copy-start(f32[1,3,4,768]{3,1,2,0:T(4,128)S(1)} %copy.68) | copy-start | bytes 110596
  264.6 10.5 %slice-start.6 = ((s8[16777216]{0:T(1024)(128)(4,1)}), s8[4194304]{0:T(1024)(128)(4,1)S(1)}, s32[]{:S(2)}) async-start(s8[16777216]{0:T(1024)(128)(4,1)} %bitcast.271), calls=%async_computation.6 | async-start | bytes 8388608
  265.1 9.9 %copy-start.50 = (bf16[256,1024]{1,0:T(8,128)(2,1)}, bf16[256,1024]{1,0:T(8,128)(2,1)S(1)}, u32[]{:S(2)}) copy-start(bf16[256,1024]{1,0:T(8,128)(2,1)S(1)} %multiply_convert_fusion.2.refs_14_) | copy-start | bytes 1572868
  265.2 9.9 %copy-start.46 = (bf16[2,256,1024]{2,1,0:T(8,128)(2,1)S(1)}, bf16[2,256,1024]{2,1,0:T(8,128)(2,1)}, u32[]{:S(2)}) copy-start(bf16[2,256,1024]{2,1,0:T(8,128)(2,1)} %param.21) | copy-start | bytes 3145732
  265.2 9.9 %slice-start.7 = ((s8[16777216]{0:T(1024)(128)(4,1)}), s8[4194304]{0:T(1024)(128)(4,1)S(1)}, s32[]{:S(2)}) async-start(s8[16777216]{0:T(1024)(128)(4,1)} %bitcast.271), calls=%async_computation.7 | async-start | bytes 8388608
  265.2 9.9 %slice-start.8 = ((s8[16777216]{0:T(1024)(128)(4,1)}), s8[4194304]{0:T(1024)(128)(4,1)S(1)}, s32[]{:S(2)}) async-start(s8[16777216]{0:T(1024)(128)(4,1)} %bitcast.271), calls=%async_computation.8 | async-start | bytes 8388608
  265.2 9.9 %slice-start.9 = ((s8[16777216]{0:T(1024)(128)(4,1)}), s8[4194304]{0:T(1024)(128)(4,1)S(1)}, s32[]{:S(2)}) async-start(s8[16777216]{0:T(1024)(128)(4,1)} %bitcast.271), calls=%async_computation.9 | async-start | bytes 8388608
  293.3 98.6 %copy-start.114 = (f32[256]{0:T(256)S(1)}, f32[256]{0:T(256)}, u32[]{:S(2)}) copy-start(f32[256]{0:T(256)} %copy-done.113) | copy-start | bytes 3076
  398.6 8.6 %slice-start.10 = ((s8[16777216]{0:T(1024)(128)(4,1)}), s8[4194304]{0:T(1024)(128)(4,1)S(1)}, s32[]{:S(2)}) async-start(s8[16777216]{0:T(1024)(128)(4,1)} %bitcast.273), calls=%async_computation.10 | async-start | bytes 8388608
  399.1 12.1 %copy-start.27 = (bf16[256,1024]{1,0:T(8,128)(2,1)}, bf16[256,1024]{1,0:T(8,128)(2,1)S(1)}, u32[]{:S(2)}) copy-start(bf16[256,1024]{1,0:T(8,128)(2,1)S(1)} %add_convert_fusion.1.refs_17_) | copy-start | bytes 1572868
  413.4 140.9 %copy-start.54 = (bf16[256,1024]{1,0:T(8,128)(2,1)}, bf16[256,1024]{1,0:T(8,128)(2,1)S(1)}, u32[]{:S(2)}) copy-start(bf16[256,1024]{1,0:T(8,128)(2,1)S(1)} %fusion.115.refs_7_) | copy-start | bytes 1572868
  414.9 139.3 %copy-start.116 = (f32[256]{0:T(256)S(1)}, f32[256]{0:T(256)}, u32[]{:S(2)}) copy-start(f32[256]{0:T(256)} %copy-done.115) | copy-start | bytes 3076
  562.4 176.7 %collective-permute-start.1 = (bf16[256,1024]{1,0:T(8,128)(2,1)}, bf16[256,1024]{1,0:T(8,128)(2,1)}, u32[]{:S(2)}, u32[]{:S(2)}) collective-permute-start(bf16[256,1024]{1,0:T(8,128)(2,1)} %get-tuple-element.224), channel_id=1, source_target_pairs={{0,16},{16,0},{1,17},{17,1},{2,18},{18,2},{3,19},{19,3},{4,20},{20... | collective-permute-start | bytes 1572872 | tf_op jit(solution)/shard_map/ppermute | solution.py:478
  569.6 8.9 %copy-start.31 = (f32[1024,256]{1,0:T(8,128)S(1)}, f32[1024,256]{1,0:T(8,128)}, u32[]{:S(2)}) copy-start(f32[1024,256]{1,0:T(8,128)} %get-tuple-element.127) | copy-start | bytes 3145732
  569.6 8.9 %copy-start.45 = (f32[1024,64]{0,1:T(8,128)S(1)}, f32[1024,64]{0,1:T(8,128)}, u32[]{:S(2)}) copy-start(f32[1024,64]{0,1:T(8,128)} %copy-done.44) | copy-start | bytes 786436
  569.6 8.9 %copy-start.118 = (f32[256]{0:T(256)S(1)}, f32[256]{0:T(256)}, u32[]{:S(2)}) copy-start(f32[256]{0:T(256)} %copy-done.117) | copy-start | bytes 3076
  569.6 12.6 %copy-start.33 = (f32[1024,256]{1,0:T(8,128)S(1)}, f32[1024,256]{1,0:T(8,128)}, u32[]{:S(2)}) copy-start(f32[1024,256]{1,0:T(8,128)} %get-tuple-element.130) | copy-start | bytes 3145732
  569.6 171.8 %collective-permute-start = (bf16[256,1024]{1,0:T(8,128)(2,1)}, bf16[256,1024]{1,0:T(8,128)(2,1)}, u32[]{:S(2)}, u32[]{:S(2)}) collective-permute-start(bf16[256,1024]{1,0:T(8,128)(2,1)} %get-tuple-element.271), channel_id=1, source_target_pairs={{0,16},{16,0},{1,17},{17,1},{2,18},{18,2},{3,19},{19,3},{4,20},{20... | collective-permute-start | bytes 1572872 | tf_op jit(solution)/shard_map/ppermute | solution.py:478
  575.6 9.6 %copy-start.122 = (f32[1024]{0:T(1024)S(1)}, f32[1024]{0:T(1024)}, u32[]{:S(2)}) copy-start(f32[1024]{0:T(1024)} %get-tuple-element.208) | copy-start | bytes 12292
  575.7 9.6 %copy-start.111 = (f32[3,3072]{1,0:T(4,128)S(1)}, f32[3,3072]{1,0:T(4,128)}, u32[]{:S(2)}) copy-start(f32[3,3072]{1,0:T(4,128)} %get-tuple-element.131) | copy-start | bytes 110596
  576.4 11.5 %copy-start.112 = (f32[4,528]{1,0:T(4,128)S(1)}, f32[4,528]{1,0:T(4,128)}, u32[]{:S(2)}) copy-start(f32[4,528]{1,0:T(4,128)} %reshape.1013) | copy-start | bytes 25348
  578.4 10.3 %copy-start.136 = (f32[64]{0:T(128)S(1)}, f32[64]{0:T(128)}, u32[]{:S(2)}) copy-start(f32[64]{0:T(128)} %copy-done.135) | copy-start | bytes 772
  582.2 11.0 %copy-start.121 = (f32[1024]{0:T(1024)S(1)}, f32[1024]{0:T(1024)}, u32[]{:S(2)}) copy-start(f32[1024]{0:T(1024)} %get-tuple-element.214) | copy-start | bytes 12292
  582.2 11.0 %copy-start.110 = (f32[3,3072]{1,0:T(4,128)S(1)}, f32[3,3072]{1,0:T(4,128)}, u32[]{:S(2)}) copy-start(f32[3,3072]{1,0:T(4,128)} %get-tuple-element.128) | copy-start | bytes 110596
  584.9 8.2 %copy-start.147 = (f32[64]{0:T(128)S(1)}, f32[64]{0:T(128)}, u32[]{:S(2)}) copy-start(f32[64]{0:T(128)} %get-tuple-element.218) | copy-start | bytes 772
  584.9 8.4 %copy-start.146 = (f32[1,1024]{1,0:T(1,128)S(1)}, f32[1,1024]{1,0:T(1,128)}, u32[]{:S(2)}) copy-start(f32[1,1024]{1,0:T(1,128)} %get-tuple-element.129) | copy-start | bytes 12292
  584.9 9.1 %copy-start.145 = (f32[1024]{0:T(1024)S(1)}, f32[1024]{0:T(1024)}, u32[]{:S(2)}) copy-start(f32[1024]{0:T(1024)} %get-tuple-element.212) | copy-start | bytes 12292
  584.9 9.3 %copy-start.61 = (f32[64,1024]{1,0:T(8,128)S(1)}, f32[64,1024]{1,0:T(8,128)}, u32[]{:S(2)}) copy-start(f32[64,1024]{1,0:T(8,128)} %copy-done.60) | copy-start | bytes 786436
  (124 other events, 458.3 us)

commit v6 on v5

--- a/solution.py
+++ b/solution.py
@@ -10,7 +10,7 @@
 from jax.sharding import PartitionSpec as P
 
 FREQS = 16
-PRECISE = lax.Precision.HIGHEST
+PRECISE = lax.Precision.HIGH
 EPSILON = 1e-05
 BF = jnp.bfloat16
 F32 = jnp.float32
@@ -531,7 +531,8 @@
         third = shared_rows(sizes[m])
         thirds.append(third)
         begins.append(odd * third)
-        lows.append(-(-(sizes[m] - third) // 32) * 16)
+        longer = -(-(sizes[m] - third) // 32) * 16
+        lows.append(sizes[m] - third - longer if m % 2 else longer)
     direct, cross, side = {}, {}, {}
 
     def first_hop(m):

time: 754 us -> 751 us (level)
  no operation moved by 1% of the time
where the time goes in v6:
time: 751 us; the launch traced here: 740 us
  Pallas kernels  568 us (76%)
  matrix products  96.2 us (13%)
  other arithmetic  41.9 us (6%)
  local copies, waits for them, and re-layouts  27.9 us (4%)
    pallas_call x3, Pallas kernels, reduce_call(): pl.pallas_call(functools.partial(reduce_kernel, items, pieces[whole:], ha...  362 us
    pallas_call x1, Pallas kernels, gather_shards(): pl.pallas_call(functools.partial(gather_kernel, chunks, heights, count),...  159 us
    pallas_call x2, Pallas kernels, mix(): pl.pallas_call(functools.partial(mix_kernel, blocks, rows, 32), out_shape...  47 us
    dot_general x8, matrix products, dot(): return jnp.dot(left, right, preferred_element_type=F32)  41.3 us
    dot_general x8, matrix products, dot_right(): lax.dot_general(left, right, (((1,), (1,)), ((), ())), preferred_element_...  38.8 us
    unnamed x352, local copies, waits for them, and re-layouts  16.5 us
  transfers between devices with their start and end apart: 2, of which 0 were waited for; matrix products, arithmetic and copies ran while one was open for 7% of the time, Pallas kernels for 17%

profile of v6, /device:TPU:0, one launch (start us, length us, event | category | flops | bytes accessed | tf_op | source)
XLA Modules:
  0.0 740.5 jit_solution(16847697558069519261)
XLA Ops:
  5.0 1.4 concatenate.191
  7.2 1.6 copy-done.7
  8.8 1.4 copy-done.8
  10.2 1.0 copy-done.9
  11.3 158.9 %gather_shards.1 = (bf16[256,1024]{1,0:T(8,128)(2,1)S(1)}, bf16[2048,1024]{1,0:T(8,128)(2,1)}, bf16[2048,3072]{1,0:T(8,128)(2,1)}, bf16[2048,4096]{1,0:T(8,128)(2,1)}, bf16[8192,1024]{1,0:T(8,128)(2,1)}) custom-call(bf16[32,1024]{1,0:T(8,128)(2,1)S(1)} %fusion.138.refs_0_, bf16[256,1024]{1,0:T(8,128)(2,1)S(1)} %bitcast.202, bf16[256,3072]{1,0:T(8,128)(2,1)S(1)} %bitcast.201, ...), custom_call_target="tpu_custom_call" | custom-call | bytes 701100032 | tf_op jit(solution)/shard_map/gather_shards/pallas_call | solution.py:624
  174.3 1.2 fusion.128
  175.5 2.4 multiply_convert_fusion.3
  185.5 4.8 fusion.38.proj_ref.refs_6_
  192.0 25.0 %mix.2 = (bf16[16,3072]{1,0:T(8,128)(2,1)S(1)}, bf16[1024,256]{1,0:T(8,128)(2,1)S(1)}, bf16[256,1024]{1,0:T(8,128)(2,1)S(1)}, bf16[256,1024]{1,0:T(8,128)(2,1)S(1)}) custom-call(f32[4,4]{1,0:T(4,128)S(1)} %compare_convert_fusion.same_ref.refs_0_, f32[1]{0:T(128)} %bitcast.2.carried_ref.refs_1_, bf16[512,256]{1,0:T(8,128)(2,1)S(1)} %copy-done.4, ...), custom_call_target="tpu_custom_call" | custom-call | bytes 81180000 | tf_op jit(solution)/shard_map/mix/pallas_call | solution.py:314
  217.1 3.0 fusion.162
  220.7 8.9 %multiply_convert_fusion.1 = (bf16[256,4096]{1,0:T(8,128)(2,1)S(1)}, f32[256,4096]{1,0:T(8,128)}) fusion(bf16[256,1024]{1,0:T(8,128)(2,1)S(1)} %multiply_convert_fusion.4.refs_14_, bf16[2048,4096]{1,0:T(8,128)(2,1)} %get-tuple-element.108), kind=kOutput, calls=%fused_computation.43 | convolution fusion | flops 2156920832 | bytes 15204352 | tf_op jit(solution)/shard_map/dot_general | solution.py:20
  229.7 2.5 convert_reduce_fusion
  233.4 4.8 fusion.41.proj_ref.refs_6_
  238.3 22.0 %mix.3 = (bf16[16,3072]{1,0:T(8,128)(2,1)S(1)}, bf16[1024,256]{1,0:T(8,128)(2,1)S(1)}, bf16[256,1024]{1,0:T(8,128)(2,1)S(1)}, bf16[256,1024]{1,0:T(8,128)(2,1)S(1)}) custom-call(f32[4,4]{1,0:T(4,128)S(1)} %compare_convert_fusion.same_ref.refs_0_, f32[1]{0:T(128)} %bitcast.2.carried_ref.refs_1_, bf16[512,256]{1,0:T(8,128)(2,1)S(1)} %copy-done.4, ...), custom_call_target="tpu_custom_call" | custom-call | bytes 81180000 | tf_op jit(solution)/shard_map/mix/pallas_call | solution.py:314
  261.9 9.8 %multiply_convert_fusion = (bf16[256,4096]{1,0:T(8,128)(2,1)}, f32[256,4096]{1,0:T(8,128)}) fusion(bf16[256,1024]{1,0:T(8,128)(2,1)S(1)} %multiply_convert_fusion.2.refs_14_, bf16[2048,4096]{1,0:T(8,128)(2,1)} %get-tuple-element.108), kind=kOutput, calls=%fused_computation.42 | convolution fusion | flops 2156920832 | bytes 15204352 | tf_op jit(solution)/shard_map/dot_general | solution.py:20
  271.8 6.6 fusion.37.refs_16_
  278.5 7.6 %multiply_reduce_fusion.2 = (f32[1024]{0:T(1024)}, f32[256]{0:T(256)S(1)}, f32[256,1024]{1,0:T(8,128)S(1)}) fusion(f32[256,1024]{1,0:T(8,128)S(1)} %get-tuple-element.268, f32[256]{0:T(256)S(1)} %fusion.151, f32[256]{0:T(256)S(1)} %broadcast_multiply_fusion, f32[1024]{0:T(1024)S(1)} %bitcast.258, bf16[256,4096]{1,0:T(8,128)(2,1)S(1)} %fusion.37.refs_16_, ...), kind=kOutput, calls=%fused_computation.118 | convolution fusion | flops 2149317376 | bytes 12594176 | tf_op jit(solution)/shard_map/dot_general | solution.py:28
  288.4 1.5 fusion.85.refs_13_
  290.0 98.8 %unmix_reduce.2 = (bf16[256,3072]{1,0:T(8,128)(2,1)}, f32[3,3072]{1,0:T(4,128)}, f32[1,1024]{1,0:T(1,128)}, f32[1024,256]{1,0:T(8,128)}, bf16[256,512]{1,0:T(8,1...) custom-call(f32[4,4]{1,0:T(4,128)} %copy-done.20, ...), custom_call_target="tpu_custom_call" | custom-call | bytes 332100000 | tf_op jit(solution)/shard_map/unmix_reduce/pallas_call | solution.py:991
  388.8 5.5 fusion.101
  394.3 1.1 fusion.95
  396.5 7.5 %fusion.30.refs_16_ = bf16[256,4096]{1,0:T(8,128)(2,1)S(1)} fusion(f32[256,4096]{1,0:T(8,128)S(1)} %copy-done.155, bf16[256,1024]{1,0:T(8,128)(2,1)S(1)} %add_convert_fusion.1.refs_17_, bf16[8192,1024]{1,0:T(8,128)(2,1)} %get-tuple-element.109), kind=kOutput, calls=%fused_computation.34 | convolution fusion | flops 2168455168 | bytes 15204352 | tf_op jit(solution)/shard_map/dot_general | solution.py:28
  404.4 3.2 multiply_reduce_fusion
  410.2 1.5 fusion.82.refs_13_
  411.7 140.2 %unmix_reduce.3 = (bf16[256,3072]{1,0:T(8,128)(2,1)}, f32[3,3072]{1,0:T(4,128)}, f32[1,1024]{1,0:T(1,128)}, f32[1024,256]{1,0:T(8,128)}, bf16[256,512]{1,0:T(8,1...) custom-call(f32[4,4]{1,0:T(4,128)} %copy-done.20, ...), custom_call_target="tpu_custom_call" | custom-call | bytes 332100000 | tf_op jit(solution)/shard_map/unmix_reduce/pallas_call | solution.py:991
  552.1 5.4 fusion.99
  557.5 1.1 fusion.97
  558.6 1.6 broadcast_select_fusion
  560.6 6.7 broadcast_select_fusion.2
  567.7 2.9 multiply_reduce_fusion.8
  570.7 1.4 convolution_dynamic-update-slice_fusion
  574.3 1.3 reshape.1015
  575.7 3.5 multiply_reduce_fusion.9
  579.1 2.7 multiply_reduce_fusion.1
  582.7 1.3 reduce.13
  585.7 1.4 convolution_dynamic-update-slice_fusion.1
  587.9 1.4 fusion.126
  592.3 123.4 %reduce.14 = (bf16[256,384]{1,0:T(8,128)(2,1)}, bf16[256,384]{1,0:T(8,128)(2,1)}, bf16[256,384]{1,0:T(8,128)(2,1)}, bf16[256,384]{1,0:T(8,128)(2,1)}, bf16[256,5...) custom-call(bf16[256,1024]{1,0:T(8,128)(2,1)} %copy-done.48, ...), custom_call_target="tpu_custom_call" | custom-call | bytes 332100000 | tf_op jit(solution)/shard_map/reduce/pallas_call | solution.py:991
  720.1 1.9 fusion.104
  722.1 1.4 fusion.105
  723.5 2.6 maximum_convert_fusion.1
  727.9 2.5 maximum_convert_fusion
  730.7 1.1 maximum_convert_fusion.3
  733.0 2.0 maximum_convert_fusion.2
  735.6 1.1 select_bitcast_fusion.1
  736.8 1.1 maximum_bitcast_fusion.1
  737.8 1.1 select_bitcast_fusion.3
  739.0 1.1 maximum_bitcast_fusion
  (484 shorter events, 42.7 us)
Async XLA Ops:
  11.3 160.6 %copy-start.154 = (s32[2,4]{1,0:T(2,128)S(1)}, s32[2,4]{1,0:T(2,128)}, u32[]{:S(2)}) copy-start(s32[2,4]{1,0:T(2,128)} %param.22) | copy-start | bytes 100
  11.3 162.0 %copy-start.37 = (f32[1024,33]{1,0:T(8,128)S(1)}, f32[1024,33]{1,0:T(8,128)}, u32[]{:S(2)}) copy-start(f32[1024,33]{1,0:T(8,128)} %constant.90.clone) | copy-start | bytes 405508
  180.6 57.8 %copy-start.20 = (f32[4,4]{1,0:T(4,128)}, f32[4,4]{1,0:T(4,128)S(1)}, u32[]{:S(2)}) copy-start(f32[4,4]{1,0:T(4,128)S(1)} %compare_convert_fusion.same_ref.refs_0_) | copy-start | bytes 196
  185.1 53.2 %copy-start.6 = (f32[256,1]{1,0:T(8,128)}, f32[256,1]{1,0:T(8,128)S(1)}, u32[]{:S(2)}) copy-start(f32[256,1]{1,0:T(8,128)S(1)} %fusion.136.valid_ref.refs_10_) | copy-start | bytes 3076
  191.3 28.8 %copy-start = (f32[4,512,256]{2,1,0:T(8,128)}, f32[4,512,256]{2,1,0:T(8,128)S(1)}, u32[]{:S(2)}) copy-start(f32[4,512,256]{2,1,0:T(8,128)S(1)} %get-tuple-element.257.filt_ref.refs_5_) | copy-start | bytes 6291460
  191.3 47.1 %copy-start.1 = (f32[4,512,256]{2,1,0:T(8,128)}, f32[4,512,256]{2,1,0:T(8,128)S(1)}, u32[]{:S(2)}) copy-start(f32[4,512,256]{2,1,0:T(8,128)S(1)} %get-tuple-element.256.filt_ref.refs_5_) | copy-start | bytes 6291460
  191.3 25.8 %copy-start.40 = (bf16[2,256,1024]{2,1,0:T(8,128)(2,1)S(1)}, bf16[2,256,1024]{2,1,0:T(8,128)(2,1)}, u32[]{:S(2)}) copy-start(bf16[2,256,1024]{2,1,0:T(8,128)(2,1)} %param.20) | copy-start | bytes 3145732
  220.0 9.6 %copy-start.29 = (f32[256,1024]{1,0:T(8,128)}, f32[256,1024]{1,0:T(8,128)S(1)}, u32[]{:S(2)}) copy-start(f32[256,1024]{1,0:T(8,128)S(1)} %get-tuple-element.262) | copy-start | bytes 3145732
  220.1 9.5 %copy-start.127 = (f32[256]{0:T(256)}, f32[256]{0:T(256)S(1)}, u32[]{:S(2)}) copy-start(f32[256]{0:T(256)S(1)} %broadcast_multiply_fusion.2) | copy-start | bytes 3076
  220.3 9.3 %copy-start.143 = (f32[256]{0:T(256)}, f32[256]{0:T(256)S(1)}, u32[]{:S(2)}) copy-start(f32[256]{0:T(256)S(1)} %multiply_reduce_fusion.7) | copy-start | bytes 3076
  220.3 9.3 %copy-start.137 = (f32[256]{0:T(256)}, f32[256]{0:T(256)S(1)}, u32[]{:S(2)}) copy-start(f32[256]{0:T(256)S(1)} %fusion.149) | copy-start | bytes 3076
  220.4 9.3 %slice-start.2 = ((s8[16777216]{0:T(1024)(128)(4,1)}), s8[4194304]{0:T(1024)(128)(4,1)S(1)}, s32[]{:S(2)}) async-start(s8[16777216]{0:T(1024)(128)(4,1)} %bitcast.269), calls=%async_computation.2 | async-start | bytes 8388608
  220.6 9.0 %copy-start.49 = (bf16[256,1024]{1,0:T(8,128)(2,1)}, bf16[256,1024]{1,0:T(8,128)(2,1)S(1)}, u32[]{:S(2)}) copy-start(bf16[256,1024]{1,0:T(8,128)(2,1)S(1)} %multiply_convert_fusion.4.refs_14_) | copy-start | bytes 1572868
  220.7 9.0 %slice-start.3 = ((s8[16777216]{0:T(1024)(128)(4,1)}), s8[4194304]{0:T(1024)(128)(4,1)S(1)}, s32[]{:S(2)}) async-start(s8[16777216]{0:T(1024)(128)(4,1)} %bitcast.269), calls=%async_computation.3 | async-start | bytes 8388608
  220.7 9.0 %slice-start.4 = ((s8[16777216]{0:T(1024)(128)(4,1)}), s8[4194304]{0:T(1024)(128)(4,1)S(1)}, s32[]{:S(2)}) async-start(s8[16777216]{0:T(1024)(128)(4,1)} %bitcast.269), calls=%async_computation.4 | async-start | bytes 8388608
  220.7 9.0 %slice-start.5 = ((s8[16777216]{0:T(1024)(128)(4,1)}), s8[4194304]{0:T(1024)(128)(4,1)S(1)}, s32[]{:S(2)}) async-start(s8[16777216]{0:T(1024)(128)(4,1)} %bitcast.269), calls=%async_computation.5 | async-start | bytes 8388608
  238.2 23.0 %copy-start.2 = (bf16[256,3072]{1,0:T(8,128)(2,1)}, bf16[256,3072]{1,0:T(8,128)(2,1)S(1)}, u32[]{:S(2)}) copy-start(bf16[256,3072]{1,0:T(8,128)(2,1)S(1)} %fusion.41.proj_ref.refs_6_) | copy-start | bytes 4718596
  238.2 22.2 %copy-start.151 = (bf16[2048,1024]{1,0:T(8,128)(2,1)S(1)}, bf16[2048,1024]{1,0:T(8,128)(2,1)}, u32[]{:S(2)}) copy-start(bf16[2048,1024]{1,0:T(8,128)(2,1)} %get-tuple-element.107) | copy-start | bytes 12582916
  238.2 23.0 %copy-start.22 = (f32[1,1,4,256]{3,1,2,0:T(1,128)}, f32[1,1,4,256]{3,1,2,0:T(1,128)S(1)}, u32[]{:S(2)}) copy-start(f32[1,1,4,256]{3,1,2,0:T(1,128)S(1)} %copy.69) | copy-start | bytes 12292
  238.3 22.9 %copy-start.17 = (f32[1,3,4,768]{3,1,2,0:T(4,128)}, f32[1,3,4,768]{3,1,2,0:T(4,128)S(1)}, u32[]{:S(2)}) copy-start(f32[1,3,4,768]{3,1,2,0:T(4,128)S(1)} %copy.68) | copy-start | bytes 110596
  261.3 10.5 %slice-start.6 = ((s8[16777216]{0:T(1024)(128)(4,1)}), s8[4194304]{0:T(1024)(128)(4,1)S(1)}, s32[]{:S(2)}) async-start(s8[16777216]{0:T(1024)(128)(4,1)} %bitcast.271), calls=%async_computation.6 | async-start | bytes 8388608
  261.8 9.9 %copy-start.50 = (bf16[256,1024]{1,0:T(8,128)(2,1)}, bf16[256,1024]{1,0:T(8,128)(2,1)S(1)}, u32[]{:S(2)}) copy-start(bf16[256,1024]{1,0:T(8,128)(2,1)S(1)} %multiply_convert_fusion.2.refs_14_) | copy-start | bytes 1572868
  261.8 9.9 %copy-start.46 = (bf16[2,256,1024]{2,1,0:T(8,128)(2,1)S(1)}, bf16[2,256,1024]{2,1,0:T(8,128)(2,1)}, u32[]{:S(2)}) copy-start(bf16[2,256,1024]{2,1,0:T(8,128)(2,1)} %param.21) | copy-start | bytes 3145732
  261.8 9.9 %slice-start.7 = ((s8[16777216]{0:T(1024)(128)(4,1)}), s8[4194304]{0:T(1024)(128)(4,1)S(1)}, s32[]{:S(2)}) async-start(s8[16777216]{0:T(1024)(128)(4,1)} %bitcast.271), calls=%async_computation.7 | async-start | bytes 8388608
  261.8 9.9 %slice-start.8 = ((s8[16777216]{0:T(1024)(128)(4,1)}), s8[4194304]{0:T(1024)(128)(4,1)S(1)}, s32[]{:S(2)}) async-start(s8[16777216]{0:T(1024)(128)(4,1)} %bitcast.271), calls=%async_computation.8 | async-start | bytes 8388608
  261.9 9.9 %slice-start.9 = ((s8[16777216]{0:T(1024)(128)(4,1)}), s8[4194304]{0:T(1024)(128)(4,1)S(1)}, s32[]{:S(2)}) async-start(s8[16777216]{0:T(1024)(128)(4,1)} %bitcast.271), calls=%async_computation.9 | async-start | bytes 8388608
  290.0 98.8 %copy-start.114 = (f32[256]{0:T(256)S(1)}, f32[256]{0:T(256)}, u32[]{:S(2)}) copy-start(f32[256]{0:T(256)} %copy-done.113) | copy-start | bytes 3076
  395.4 8.6 %slice-start.10 = ((s8[16777216]{0:T(1024)(128)(4,1)}), s8[4194304]{0:T(1024)(128)(4,1)S(1)}, s32[]{:S(2)}) async-start(s8[16777216]{0:T(1024)(128)(4,1)} %bitcast.273), calls=%async_computation.10 | async-start | bytes 8388608
  396.0 12.1 %copy-start.27 = (bf16[256,1024]{1,0:T(8,128)(2,1)}, bf16[256,1024]{1,0:T(8,128)(2,1)S(1)}, u32[]{:S(2)}) copy-start(bf16[256,1024]{1,0:T(8,128)(2,1)S(1)} %add_convert_fusion.1.refs_17_) | copy-start | bytes 1572868
  396.5 7.9 %slice-start.13 = ((s8[16777216]{0:T(1024)(128)(4,1)}), s8[4194304]{0:T(1024)(128)(4,1)S(1)}, s32[]{:S(2)}) async-start(s8[16777216]{0:T(1024)(128)(4,1)} %bitcast.273), calls=%async_computation.13 | async-start | bytes 8388608
  410.2 141.8 %copy-start.54 = (bf16[256,1024]{1,0:T(8,128)(2,1)}, bf16[256,1024]{1,0:T(8,128)(2,1)S(1)}, u32[]{:S(2)}) copy-start(bf16[256,1024]{1,0:T(8,128)(2,1)S(1)} %fusion.115.refs_7_) | copy-start | bytes 1572868
  411.7 140.2 %copy-start.116 = (f32[256]{0:T(256)S(1)}, f32[256]{0:T(256)}, u32[]{:S(2)}) copy-start(f32[256]{0:T(256)} %copy-done.115) | copy-start | bytes 3076
  560.2 175.5 %collective-permute-start.1 = (bf16[256,1024]{1,0:T(8,128)(2,1)}, bf16[256,1024]{1,0:T(8,128)(2,1)}, u32[]{:S(2)}, u32[]{:S(2)}) collective-permute-start(bf16[256,1024]{1,0:T(8,128)(2,1)} %get-tuple-element.224), channel_id=1, source_target_pairs={{0,16},{16,0},{1,17},{17,1},{2,18},{18,2},{3,19},{19,3},{4,20},{20... | collective-permute-start | bytes 1572872 | tf_op jit(solution)/shard_map/ppermute | solution.py:478
  567.4 8.3 %copy-start.31 = (f32[1024,256]{1,0:T(8,128)S(1)}, f32[1024,256]{1,0:T(8,128)}, u32[]{:S(2)}) copy-start(f32[1024,256]{1,0:T(8,128)} %get-tuple-element.127) | copy-start | bytes 3145732
  567.4 8.3 %copy-start.45 = (f32[1024,64]{0,1:T(8,128)S(1)}, f32[1024,64]{0,1:T(8,128)}, u32[]{:S(2)}) copy-start(f32[1024,64]{0,1:T(8,128)} %copy-done.44) | copy-start | bytes 786436
  567.4 8.3 %copy-start.118 = (f32[256]{0:T(256)S(1)}, f32[256]{0:T(256)}, u32[]{:S(2)}) copy-start(f32[256]{0:T(256)} %copy-done.117) | copy-start | bytes 3076
  567.4 11.8 %copy-start.33 = (f32[1024,256]{1,0:T(8,128)S(1)}, f32[1024,256]{1,0:T(8,128)}, u32[]{:S(2)}) copy-start(f32[1024,256]{1,0:T(8,128)} %get-tuple-element.130) | copy-start | bytes 3145732
  567.4 170.5 %collective-permute-start = (bf16[256,1024]{1,0:T(8,128)(2,1)}, bf16[256,1024]{1,0:T(8,128)(2,1)}, u32[]{:S(2)}, u32[]{:S(2)}) collective-permute-start(bf16[256,1024]{1,0:T(8,128)(2,1)} %get-tuple-element.271), channel_id=1, source_target_pairs={{0,16},{16,0},{1,17},{17,1},{2,18},{18,2},{3,19},{19,3},{4,20},{20... | collective-permute-start | bytes 1572872 | tf_op jit(solution)/shard_map/ppermute | solution.py:478
  572.8 9.4 %copy-start.122 = (f32[1024]{0:T(1024)S(1)}, f32[1024]{0:T(1024)}, u32[]{:S(2)}) copy-start(f32[1024]{0:T(1024)} %get-tuple-element.208) | copy-start | bytes 12292
  572.9 9.3 %copy-start.111 = (f32[3,3072]{1,0:T(4,128)S(1)}, f32[3,3072]{1,0:T(4,128)}, u32[]{:S(2)}) copy-start(f32[3,3072]{1,0:T(4,128)} %get-tuple-element.131) | copy-start | bytes 110596
  573.6 11.2 %copy-start.112 = (f32[4,528]{1,0:T(4,128)S(1)}, f32[4,528]{1,0:T(4,128)}, u32[]{:S(2)}) copy-start(f32[4,528]{1,0:T(4,128)} %reshape.1013) | copy-start | bytes 25348
  575.6 10.0 %copy-start.136 = (f32[64]{0:T(128)S(1)}, f32[64]{0:T(128)}, u32[]{:S(2)}) copy-start(f32[64]{0:T(128)} %copy-done.135) | copy-start | bytes 772
  579.1 10.6 %copy-start.121 = (f32[1024]{0:T(1024)S(1)}, f32[1024]{0:T(1024)}, u32[]{:S(2)}) copy-start(f32[1024]{0:T(1024)} %get-tuple-element.214) | copy-start | bytes 12292
  579.1 10.6 %copy-start.110 = (f32[3,3072]{1,0:T(4,128)S(1)}, f32[3,3072]{1,0:T(4,128)}, u32[]{:S(2)}) copy-start(f32[3,3072]{1,0:T(4,128)} %get-tuple-element.128) | copy-start | bytes 110596
  581.8 7.8 %copy-start.147 = (f32[64]{0:T(128)S(1)}, f32[64]{0:T(128)}, u32[]{:S(2)}) copy-start(f32[64]{0:T(128)} %get-tuple-element.218) | copy-start | bytes 772
  581.8 7.9 %copy-start.146 = (f32[1,1024]{1,0:T(1,128)S(1)}, f32[1,1024]{1,0:T(1,128)}, u32[]{:S(2)}) copy-start(f32[1,1024]{1,0:T(1,128)} %get-tuple-element.129) | copy-start | bytes 12292
  581.8 8.6 %copy-start.145 = (f32[1024]{0:T(1024)S(1)}, f32[1024]{0:T(1024)}, u32[]{:S(2)}) copy-start(f32[1024]{0:T(1024)} %get-tuple-element.212) | copy-start | bytes 12292
  581.8 8.8 %copy-start.61 = (f32[64,1024]{1,0:T(8,128)S(1)}, f32[64,1024]{1,0:T(8,128)}, u32[]{:S(2)}) copy-start(f32[64,1024]{1,0:T(8,128)} %copy-done.60) | copy-start | bytes 786436
  (124 other events, 453.3 us)
